TPU v7x, 32 devices: a whole 2x2x4 slice. The times are simulated.
32 devices in a mesh: view: 8 (over z, core), blk: 4 (over y, x).
Axes of the slice: x: 2, y: 2, z: 4, core: 2. Of those that a mesh axis runs over, the one named last changes fastest.
Arguments:
- estimate: float32 [64, 128, 128], P('blk'), may hold values from 0.5 to 2
- images: bfloat16 [8, 64, 128, 128], P('view', 'blk'), may hold values from 0.5 to 2
- point_spread: float32 [8, 9, 7, 25], replicated, may hold values from 0.01 to 1
- covered: int32 [8, 4, 4], P(None, 'blk'), may hold values from 0 to 1, as said below
Outputs:
- estimate_next: float32 [64, 128, 128], P('blk')
Inputs may be any that keep to these rules, and one draw needn't show every extreme that they name: For each view and each block layer along the first dimension, the covered blocks are consecutive along the second dimension and at most 3; for every view some block layer has exactly 3.
All inputs are finite; a program needn't handle non-finite values.
Results may differ from a plain program's by a relative error of at most 0.0003.
Values may be sent and summed in bfloat16 or wider, within the bound.
No kernel may reach another device: no remote copies, remote signals or barrier semaphores. Data moves between devices by JAX's collectives and lax.ppermute only.
A program may use at most 128 MiB of HBM per device.

v0:
```python
import jax
import jax.numpy as jnp
from jax import lax
from jax.sharding import PartitionSpec as P

BY = 32


def with_halo(cells, sides, width):
    for axis, dim in sides:
        count = lax.axis_size(axis)
        ends = count - 1
        head = lax.slice_in_dim(cells, 0, width, axis=dim)
        tail = lax.slice_in_dim(cells, cells.shape[dim] - width, cells.shape[dim], axis=dim)
        cells = jnp.concatenate(
            [
                lax.ppermute(tail, axis, [(i, (i + 1) % count) for i in range(ends)]),
                cells,
                lax.ppermute(head, axis, [((i + 1) % count, i) for i in range(ends)]),
            ],
            axis=dim,
        )
    return cells


def swapped(block, axis, stride):
    count = lax.axis_size(axis)
    route = []
    for low in range(count):
        high = low | 1 << stride
        if high != low and high < count:
            route += [(low, high), (high, low)]
    return lax.ppermute(block, axis, route)


def band_table(kernel, depth):
    taps_x, taps_y, taps_z = kernel.shape
    span_z = depth + taps_z - 1
    shape_three = (taps_z, span_z, depth)
    offset = lax.broadcasted_iota(jnp.int32, shape_three, 1) - lax.broadcasted_iota(
        jnp.int32, shape_three, 2
    )
    onehot = (offset == lax.broadcasted_iota(jnp.int32, shape_three, 0)).astype(jnp.bfloat16)
    banded = jnp.einsum("abt,tpz->abpz", kernel, onehot, preferred_element_type=jnp.float32).astype(
        jnp.bfloat16
    )
    inner_width = taps_y * span_z
    padded_width = -(-inner_width // 128) * 128
    banded = banded.reshape(taps_x, inner_width, depth)
    return jnp.pad(banded, ((0, 0), (0, padded_width - inner_width), (0, 0)))


def convolve(padded_part, banded, rows_x, rows_y):
    taps_x = padded_part.shape[0] - rows_x + 1
    taps_y = padded_part.shape[1] - rows_y + 1
    columns = jnp.concatenate(
        [padded_part[:, step_y : step_y + rows_y, :] for step_y in range(taps_y)], axis=2
    )
    columns = jnp.pad(columns, ((0, 0), (0, 0), (0, banded.shape[1] - columns.shape[2])))
    output = None
    for shift_x in range(taps_x):
        partial_sum = jnp.dot(
            columns[shift_x : shift_x + rows_x].reshape(rows_x * rows_y, -1),
            banded[shift_x],
            preferred_element_type=jnp.float32,
        )
        output = partial_sum if output is None else output + partial_sum
    return output.reshape(rows_x, rows_y, -1)


def local(estimate, images, point_spread, covered):
    slab_x, width_y, depth = estimate.shape
    share_w = images.shape[2]
    view_count, taps_x, taps_y, taps_z = point_spread.shape
    rim_x, rim_y, rim_z = ((taps_x - 1) // 2, (taps_y - 1) // 2, (taps_z - 1) // 2)
    shares = width_y // share_w
    share_blocks = share_w // BY
    group = lax.axis_index("view")
    view_id = group // shares
    part = group % shares
    y_start = part * share_w
    source = estimate.astype(jnp.bfloat16)
    rimmed = with_halo(source, (("blk", 0),), rim_x)
    padded = jnp.pad(rimmed, ((0, 0), (rim_y, rim_y), (rim_z, rim_z)))
    spread = lax.dynamic_index_in_dim(point_spread, view_id, 0, keepdims=False)
    kernel = (spread / jnp.sum(spread)).astype(jnp.bfloat16)
    forward = band_table(kernel, depth)
    backward = band_table(kernel[::-1, ::-1, ::-1], depth)
    coverage_row = lax.dynamic_index_in_dim(covered[:, 0, :], view_id, 0, keepdims=False) > 0
    share_cover = lax.dynamic_slice_in_dim(coverage_row, part * share_blocks, share_blocks)
    cell_cover = jnp.repeat(share_cover, BY)[None, :, None]
    image = images[0]
    region = lax.dynamic_slice(
        padded, (0, y_start, 0), (slab_x + 2 * rim_x, share_w + 2 * rim_y, depth + 2 * rim_z)
    )
    blurred = convolve(region, forward, slab_x, share_w)
    quotient = jnp.where(cell_cover, image.astype(jnp.float32) / blurred, 0.0).astype(jnp.bfloat16)
    rim_zeros = jnp.zeros((slab_x, rim_y, depth), jnp.bfloat16)
    if shares > 1:
        edge_rows = jnp.where(part == 0, quotient[:, share_w - rim_y :, :], quotient[:, :rim_y, :])
        partner = swapped(edge_rows, "view", 0)
        lower_rim = jnp.where(part > 0, partner, rim_zeros)
        upper_rim = jnp.where(part < shares - 1, partner, rim_zeros)
    else:
        lower_rim = rim_zeros
        upper_rim = rim_zeros
    extended = jnp.concatenate([lower_rim, quotient, upper_rim], axis=1)
    quotient_rimmed = with_halo(extended, (("blk", 0),), rim_x)
    padded_quotient = jnp.pad(quotient_rimmed, ((0, 0), (0, 0), (rim_z, rim_z)))
    correction = convolve(padded_quotient, backward, slab_x, share_w)
    share_factor = jnp.where(cell_cover, correction, 1.0)
    factor = lax.dynamic_update_slice(
        jnp.ones((slab_x, width_y, depth), jnp.float32), share_factor, (0, y_start, 0)
    )
    pieces = lax.all_to_all(factor[None], "view", split_axis=2, concat_axis=0, tiled=True)
    own_part = jnp.prod(pieces, axis=0)
    piece_y = own_part.shape[1]
    own_slab = lax.dynamic_slice_in_dim(estimate, group * piece_y, piece_y, 1)
    return lax.all_gather(own_slab * own_part, "view", axis=1, tiled=True)


def solution(mesh):
    in_specs = (P("blk", None, None), P("view", "blk", None, None), P(), P(None, "blk", None))
    out_specs = P("blk", None, None)
    return jax.shard_map(local, mesh=mesh, in_specs=in_specs, out_specs=out_specs, check_vma=False)
```

profile of v0, /device:TPU:0, one launch (start us, length us, event | category | flops | bytes accessed | tf_op | source)
XLA Modules:
  0.0 246.5 jit_solution(9548848999403762466)
XLA Ops:
  7.9 4.8 %collective-permute-start = (bf16[4,128,128]{2,1,0:T(8,128)(2,1)S(1)}, bf16[4,128,128]{2,1,0:T(8,128)(2,1)S(1)}, u32[]{:S(2)}, u32[]{:S(2)}) collective-permute-start(bf16[4,128,128]{2,1,0:T(8,128)(2,1)S(1)} %get-tuple-element.41), channel_id=1, source_target_pairs={{0,1},{1,2},{2,3},{4,5},{5,6},{6,7},{8,9},{9,10},{10,11},{12,13},{... | collective-permute-start | bytes 393224 | tf_op jit(solution)/shard_map/ppermute | solution.py:17
  14.0 1.6 fusion.87
  15.7 1.6 fusion.9
  20.2 2.3 select_maximum_fusion.2
  22.5 4.6 %fusion.89 = (bf16[24,128,152]{2,1,0:T(8,128)(2,1)}, bf16[24,128,152]{2,1,0:T(8,128)(2,1)}, bf16[24,128,152]{2,1,0:T(8,128)(2,1)}, bf16[24,128,152]{2,1,0:T(8,12...) fusion(bf16[24,134,152]{2,1,0:T(8,128)(2,1)S(1)} %select_maximum_fusion.2), kind=kLoop, calls=%fused_computation.135 | loop fusion | bytes 13074432 | tf_op jit(solution)/shard_map/slice | solution.py:57
  27.1 15.1 %concatenate.16 = bf16[24,128,1064]{2,1,0:T(8,128)(2,1)} concatenate(bf16[24,128,152]{2,1,0:T(8,128)(2,1)} %get-tuple-element.38, bf16[24,128,152]{2,1,0:T(8,128)(2,1)} %get-tuple-element.37, bf16[24,128,152]{2,1,0:T(8,128)(2,1)} %get-tuple-element.36, bf16[24,128,152]{2,1,0:T(8,128)(2,1)} %get-tuple-element.35, bf16[24,128,152]{2,1,0:T(8,128)(2,1)} %get-tuple-element.34, ...), dimensions={2} | concatenate | bytes 13074432 | tf_op jit(solution)/shard_map/concatenate | solution.py:56
  42.2 27.8 %pad_slice_fusion.27 = (bf16[16,128,1152]{2,1,0:T(8,128)(2,1)S(1)}, bf16[16,128,1152]{2,1,0:T(8,128)(2,1)}, bf16[16,128,1152]{2,1,0:T(8,128)(2,1)}, bf16[16,128,...) fusion(bf16[24,128,1064]{2,1,0:T(8,128)(2,1)} %concatenate.16), kind=kLoop, calls=%fused_computation.73 | loop fusion | bytes 49004544 | tf_op jit(solution)/shard_map/slice | solution.py:63
  70.0 3.9 %fusion.26 = f32[2048,128]{1,0:T(8,128)S(1)} fusion(bf16[2048,1152]{1,0:T(8,128)(2,1)} %bitcast.180, bf16[9,1064,128]{2,1,0:T(8,128)(2,1)S(1)} %bitcast.118), kind=kOutput, calls=%fused_computation.83 | convolution fusion | flops 603979776 | bytes 8218624 | tf_op jit(solution)/shard_map/dot_general | solution.py:62
  73.9 1.4 convolution_add_fusion.15
  86.8 1.4 convolution_add_fusion.8
  88.2 13.6 %fusion.24 = bf16[16,128,128]{2,1,0:T(8,128)(2,1)S(1)} fusion(f32[16,128,128]{2,1,0:T(8,128)S(1)} %bitcast.183, bf16[1,16,128,128]{3,2,1,0:T(8,128)(2,1)S(1)} %copy-done, pred[128]{0:T(512)(128)(4,1)S(1)} %copy-done.1), kind=kLoop, calls=%fused_computation.44 | loop fusion | flops 1048576 | bytes 2097280 | tf_op jit(solution)/shard_map/convert_element_type | solution.py:97
  101.9 3.7 %collective-permute-start.2 = (bf16[4,134,128]{2,1,0:T(8,128)(2,1)S(1)}, bf16[4,134,128]{2,1,0:T(8,128)(2,1)S(1)}, u32[]{:S(2)}, u32[]{:S(2)}) collective-permute-start(bf16[4,134,128]{2,1,0:T(8,128)(2,1)S(1)} %get-tuple-element.39), channel_id=1, source_target_pairs={{0,1},{1,2},{2,3},{4,5},{5,6},{6,7},{8,9},{9,10},{10,11},{12,13},{... | collective-permute-start | bytes 411656 | tf_op jit(solution)/shard_map/ppermute | solution.py:17
  108.2 5.7 %collective-permute-done.3 = bf16[4,134,128]{2,1,0:T(8,128)(2,1)S(1)} collective-permute-done((bf16[4,134,128]{2,1,0:T(8,128)(2,1)S(1)}, bf16[4,134,128]{2,1,0:T(8,128)(2,1)S(1)}, u32[]{:S(2)}, u32[]{:S(2)}) %collective-permute-start.3) | collective-permute-done | bytes 137248 | tf_op jit(solution)/shard_map/ppermute | solution.py:19
  114.0 3.0 %select_maximum_fusion = bf16[24,134,152]{2,1,0:T(8,128)(2,1)S(1)} fusion(bf16[4,134,128]{2,1,0:T(8,128)(2,1)S(1)} %collective-permute-done.3, bf16[4,134,128]{2,1,0:T(8,128)(2,1)S(1)} %collective-permute-done.2, bf16[16,3,128]{2,1,0:T(4,128)(2,1)S(1)} %broadcast_in_dim.33, bf16[16,128,128]{2,1,0:T(8,128)(2,1)S(1)} %fusion.24), kind=kLoop, calls=%fused_computation.30 | loop fusion | flops 8798976 | bytes 1788672 | tf_op jit(solution)/shard_map/concatenate | solution.py:15
  117.0 4.6 %fusion.88 = (bf16[24,128,152]{2,1,0:T(8,128)(2,1)}, bf16[24,128,152]{2,1,0:T(8,128)(2,1)}, bf16[24,128,152]{2,1,0:T(8,128)(2,1)}, bf16[24,128,152]{2,1,0:T(8,12...) fusion(bf16[24,134,152]{2,1,0:T(8,128)(2,1)S(1)} %select_maximum_fusion), kind=kLoop, calls=%fused_computation.134 | loop fusion | bytes 13074432 | tf_op jit(solution)/shard_map/slice | solution.py:57
  121.6 15.1 %concatenate.19 = bf16[24,128,1064]{2,1,0:T(8,128)(2,1)} concatenate(bf16[24,128,152]{2,1,0:T(8,128)(2,1)} %get-tuple-element.31, bf16[24,128,152]{2,1,0:T(8,128)(2,1)} %get-tuple-element.30, bf16[24,128,152]{2,1,0:T(8,128)(2,1)} %get-tuple-element.29, bf16[24,128,152]{2,1,0:T(8,128)(2,1)} %get-tuple-element.28, bf16[24,128,152]{2,1,0:T(8,128)(2,1)} %get-tuple-element.27, ...), dimensions={2} | concatenate | bytes 13074432 | tf_op jit(solution)/shard_map/concatenate | solution.py:56
  136.7 27.5 %pad_slice_fusion.18 = (bf16[16,128,1152]{2,1,0:T(8,128)(2,1)S(1)}, bf16[16,128,1152]{2,1,0:T(8,128)(2,1)}, bf16[16,128,1152]{2,1,0:T(8,128)(2,1)}, bf16[16,128,...) fusion(bf16[24,128,1064]{2,1,0:T(8,128)(2,1)} %concatenate.19), kind=kLoop, calls=%fused_computation.64 | loop fusion | bytes 49004544 | tf_op jit(solution)/shard_map/slice | solution.py:63
  164.2 3.9 %fusion.45 = f32[2048,128]{1,0:T(8,128)S(1)} fusion(bf16[2048,1152]{1,0:T(8,128)(2,1)} %bitcast.181, bf16[9,1064,128]{2,1,0:T(8,128)(2,1)S(1)} %bitcast.127), kind=kOutput, calls=%fused_computation.93 | convolution fusion | flops 603979776 | bytes 8218624 | tf_op jit(solution)/shard_map/dot_general | solution.py:62
  168.2 1.4 convolution_add_fusion.7
  182.4 1.7 copy_select_fusion
  184.1 4.9 %all-to-all-start = ((f32[1,16,128,128]{3,1,0,2:T(8,128)}), f32[1,16,128,128]{3,1,0,2:T(8,128)S(1)}, u32[]{:S(2)}, u32[]{:S(2)}) async-start(f32[1,16,128,128]{3,1,0,2:T(8,128)} %copy_select_fusion), calls=%async_computation | async-start | bytes 2097152 | tf_op jit(solution)/shard_map/all_to_all | solution.py:115
  189.9 25.6 %all-to-all-done = f32[1,16,128,128]{3,1,0,2:T(8,128)S(1)} async-done(((f32[1,16,128,128]{3,1,0,2:T(8,128)}), f32[1,16,128,128]{3,1,0,2:T(8,128)S(1)}, u32[]{:S(2)}, u32[]{:S(2)}) %all-to-all-start) | async-done | bytes 1048608 | tf_op jit(solution)/shard_map/all_to_all | solution.py:115
  216.3 20.6 %all-gather.2.cloned.1.call-done = f32[16,128,128]{2,0,1:T(8,128)} async-done(((f32[16,16,128]{2,0,1:T(8,128)}), f32[16,128,128]{2,0,1:T(8,128)}) %all-gather.2.cloned.1.call-update) | async-done | bytes 1048592 | tf_op jit(solution)/shard_map/all_gather | solution.py:119
  236.9 2.5 %copy.24 = f32[16,128,128]{2,1,0:T(8,128)} copy(f32[16,128,128]{2,0,1:T(8,128)} %all-gather.2.cloned.1.call-done) | data formatting | bytes 2097152 | tf_op jit(solution)/shard_map/all_gather | solution.py:119
  (111 shorter events, 34.0 us)
Async XLA Ops:
  7.9 11.4 %collective-permute-start = (bf16[4,128,128]{2,1,0:T(8,128)(2,1)S(1)}, bf16[4,128,128]{2,1,0:T(8,128)(2,1)S(1)}, u32[]{:S(2)}, u32[]{:S(2)}) collective-permute-start(bf16[4,128,128]{2,1,0:T(8,128)(2,1)S(1)} %get-tuple-element.41), channel_id=1, source_target_pairs={{0,1},{1,2},{2,3},{4,5},{5,6},{6,7},{8,9},{9,10},{10,11},{12,13},{... | collective-permute-start | bytes 393224 | tf_op jit(solution)/shard_map/ppermute | solution.py:17
  12.7 7.5 %collective-permute-start.1 = (bf16[4,128,128]{2,1,0:T(8,128)(2,1)S(1)}, bf16[4,128,128]{2,1,0:T(8,128)(2,1)S(1)}, u32[]{:S(2)}, u32[]{:S(2)}) collective-permute-start(bf16[4,128,128]{2,1,0:T(8,128)(2,1)S(1)} %get-tuple-element.42), channel_id=1, source_target_pairs={{1,0},{2,1},{3,2},{5,4},{6,5},{7,6},{9,8},{10,9},{11,10},{13,12},{... | collective-permute-start | bytes 393224 | tf_op jit(solution)/shard_map/ppermute | solution.py:19
  69.9 3.9 %slice-start.24 = ((s8[4718592]{0:T(1024)(128)(4,1)}), s8[4194304]{0:T(1024)(128)(4,1)S(1)}, s32[]{:S(2)}) async-start(s8[4718592]{0:T(1024)(128)(4,1)} %bitcast.174), calls=%async_computation.26 | async-start | bytes 8388608
  70.0 3.9 %slice-start.25 = ((s8[4718592]{0:T(1024)(128)(4,1)}), s8[524288]{0:T(1024)(128)(4,1)S(1)}, s32[]{:S(2)}) async-start(s8[4718592]{0:T(1024)(128)(4,1)} %bitcast.174), calls=%async_computation.27 | async-start | bytes 1048576
  73.9 2.2 slice-start.20
  73.9 2.3 slice-start.21
  75.3 2.4 slice-start.16
  77.6 2.3 slice-start.12
  79.1 2.4 slice-start.8
  81.2 2.3 slice-start.4
  83.0 2.4 slice-start
  101.9 6.3 %collective-permute-start.2 = (bf16[4,134,128]{2,1,0:T(8,128)(2,1)S(1)}, bf16[4,134,128]{2,1,0:T(8,128)(2,1)S(1)}, u32[]{:S(2)}, u32[]{:S(2)}) collective-permute-start(bf16[4,134,128]{2,1,0:T(8,128)(2,1)S(1)} %get-tuple-element.39), channel_id=1, source_target_pairs={{0,1},{1,2},{2,3},{4,5},{5,6},{6,7},{8,9},{9,10},{10,11},{12,13},{... | collective-permute-start | bytes 411656 | tf_op jit(solution)/shard_map/ppermute | solution.py:17
  105.6 8.4 %collective-permute-start.3 = (bf16[4,134,128]{2,1,0:T(8,128)(2,1)S(1)}, bf16[4,134,128]{2,1,0:T(8,128)(2,1)S(1)}, u32[]{:S(2)}, u32[]{:S(2)}) collective-permute-start(bf16[4,134,128]{2,1,0:T(8,128)(2,1)S(1)} %get-tuple-element.40), channel_id=1, source_target_pairs={{1,0},{2,1},{3,2},{5,4},{6,5},{7,6},{9,8},{10,9},{11,10},{13,12},{... | collective-permute-start | bytes 411656 | tf_op jit(solution)/shard_map/ppermute | solution.py:19
  164.2 3.9 %slice-start.26 = ((s8[4718592]{0:T(1024)(128)(4,1)}), s8[4194304]{0:T(1024)(128)(4,1)S(1)}, s32[]{:S(2)}) async-start(s8[4718592]{0:T(1024)(128)(4,1)} %bitcast.177), calls=%async_computation.28 | async-start | bytes 8388608
  164.2 3.9 %slice-start.27 = ((s8[4718592]{0:T(1024)(128)(4,1)}), s8[524288]{0:T(1024)(128)(4,1)S(1)}, s32[]{:S(2)}) async-start(s8[4718592]{0:T(1024)(128)(4,1)} %bitcast.177), calls=%async_computation.29 | async-start | bytes 1048576
  168.1 2.2 slice-start.22
  168.2 2.3 slice-start.23
  169.6 2.4 slice-start.18
  171.8 2.3 slice-start.14
  173.4 2.4 slice-start.10
  175.5 2.3 slice-start.6
  177.2 2.4 slice-start.2
  184.1 31.5 %all-to-all-start = ((f32[1,16,128,128]{3,1,0,2:T(8,128)}), f32[1,16,128,128]{3,1,0,2:T(8,128)S(1)}, u32[]{:S(2)}, u32[]{:S(2)}) async-start(f32[1,16,128,128]{3,1,0,2:T(8,128)} %copy_select_fusion), calls=%async_computation | async-start | bytes 2097152 | tf_op jit(solution)/shard_map/all_to_all | solution.py:115
  188.9 48.0 %all-gather.2.cloned.1.call-start = ((), (), s32[]{:S(2)}) async-start(), calls=%async_computation.1 | async-start | bytes 1179648 | tf_op jit(solution)/shard_map/all_gather | solution.py:119
  (13 other events, 23.2 us)
Sparse Core Ops, SparseCore 0:
  216.5 20.4 all-gather.1
where the time goes:
time: 246 us
  local copies, waits for them, and re-layouts  106 us (43%)
  waiting for transfers between devices  52.9 us (22%)
  matrix products  32.8 us (13%)
  other arithmetic  25.2 us (10%)
  starting transfers between devices  16 us (7%)
  between operations  14.1 us (6%)
    slice x2, local copies, waits for them, and re-layouts, convolve(): columns[shift_x:shift_x + rows_x].reshape(rows_x * rows_y, -1)  55.3 us
    concatenate x2, local copies, waits for them, and re-layouts, convolve(): jnp.concatenate([padded_part[:, step_y:step_y + rows_y, :] for step_y in...  30.2 us
    dot_general x18, matrix products, convolve(): jnp.dot(columns[shift_x:shift_x + rows_x].reshape(rows_x * rows_y, -1), b...  30.2 us
    all_to_all x1, waiting for transfers between devices, local(): lax.all_to_all(factor[None], 'view', split_axis=2, concat_axis=0, tiled=T...  25.6 us
    all_gather x1, waiting for transfers between devices, local(): return lax.all_gather(own_slab * own_part, 'view', axis=1, tiled=True)  20.6 us
    convert_element_type x1, other arithmetic, local(): jnp.where(cell_cover, image.astype(jnp.float32) / blurred, 0.0)  13.6 us
    slice x2, local copies, waits for them, and re-layouts, convolve(): padded_part[:, step_y:step_y + rows_y, :]  9.19 us
    ppermute x2, starting transfers between devices, with_halo(): lax.ppermute(tail, axis, [(i, (i + 1) % count) for i in range(ends)])  8.55 us
  transfers between devices with their start and end apart: 6, of which 4 were waited for; matrix products, arithmetic and copies ran while one was open for 3% of the time, Pallas kernels for 0%

commit v1 on v0

v1 whole, which is shorter than its diff:
```python
import functools

import jax
import jax.numpy as jnp
from jax import lax
from jax.experimental import pallas as pl
from jax.experimental.pallas import tpu as pltpu
from jax.sharding import PartitionSpec as P

CAP = 3
LANES = 128
PAD = 8
VMEM_LIMIT = 24 * 1024 * 1024


def swap_cores(cells):
    count = lax.axis_size("view")
    return lax.ppermute(cells, "view", [(i, i ^ 1) for i in range(count)])


def swap_chips(cells, step):
    count = lax.axis_size("view")
    return lax.ppermute(cells, "view", [(i, i ^ (2 * step)) for i in range(count)])


def swap_layers(cells):
    views, layers = lax.axis_size("view"), lax.axis_size("blk")
    route = []
    for chip in range(views // 2):
        for layer in range(layers - 1):
            low = (2 * chip + 1) * layers + layer
            high = 2 * chip * layers + layer + 1
            route += [(low, high), (high, low)]
    return lax.ppermute(cells, ("view", "blk"), route)


def window_of(cov, view, blocks, window):
    first = jnp.int32(blocks - window)
    for block in range(blocks - window - 1, -1, -1):
        first = jnp.where(cov[view, 0, block] > 0, jnp.int32(block), first)
    return first


def window_mask(cov, view, first, window, block_width):
    row = lax.broadcasted_iota(jnp.int32, (window * block_width, LANES), 0)
    mask = jnp.zeros(row.shape, jnp.int32)
    for block in range(window):
        inside = (row >= block * block_width) & (row < (block + 1) * block_width)
        mask = jnp.where(inside, cov[view, 0, first + block], mask)
    return mask > 0


def tables_kernel(ids, spread, fwd, bwd, rows_f, rows_b, *, taps):
    taps_x, taps_y, taps_z = taps
    rim_z = (taps_z - 1) // 2
    depth = LANES
    row = lax.broadcasted_iota(jnp.int32, (depth, depth), 0)
    col = lax.broadcasted_iota(jnp.int32, (depth, depth), 1)
    band = jnp.abs(row - col) <= rim_z
    real = row < taps_z
    at_f = rim_z - row
    at_b = row - rim_z
    place_f = ((col == at_f) | (col == at_f + depth)) & real
    place_b = ((col == at_b) | (col == at_b + depth)) & real
    place_f = jnp.where(place_f, 1.0, 0.0).astype(jnp.bfloat16)
    place_b = jnp.where(place_b, 1.0, 0.0).astype(jnp.bfloat16)
    for j in range(fwd.shape[0]):
        taps_all = spread[ids[1] * fwd.shape[0] + j]
        kernel = (taps_all / jnp.sum(taps_all)).astype(jnp.bfloat16)
        kernel = kernel.reshape(-1, LANES)
        rows_f[...] = jnp.dot(kernel, place_f, preferred_element_type=jnp.float32)
        rows_b[...] = jnp.dot(kernel, place_b, preferred_element_type=jnp.float32)
        zero = jnp.zeros((taps_y * depth, depth), jnp.bfloat16)
        for table in (fwd, bwd):
            table[j, 0] = zero
            table[j, taps_x + 1] = zero

        def fill(a, carry):
            for b in range(taps_y):
                for table, source, at in (
                    (fwd, rows_f, a * 8 + b),
                    (bwd, rows_b, (taps_x - 1 - a) * 8 + (taps_y - 1 - b)),
                ):
                    line = jnp.broadcast_to(source[pl.ds(at, 1), :], (depth, depth))
                    line = pltpu.roll(line, 0, 1, stride=1, stride_axis=0)
                    line = jnp.where(band, line, 0.0).astype(jnp.bfloat16)
                    table[j, a + 1, b * depth : (b + 1) * depth, :] = line
            return carry

        lax.fori_loop(0, taps_x, fill, 0)


def fill_columns(pad, cols, taps_y, rows_y):
    rim_y = (taps_y - 1) // 2

    def fill(x, carry):
        for b in range(taps_y):
            low = PAD - rim_y + b
            cols[x, :, b * LANES : (b + 1) * LANES] = pad[x, low : low + rows_y, :].astype(
                jnp.bfloat16
            )
        return carry

    lax.fori_loop(0, pad.shape[0], fill, 0)


def band_dots(cols, y_start, rows_y, table, j, pairs):
    steps = (table.shape[1] - 1) // 2
    total = None
    for s in range(steps):
        left = jnp.concatenate(
            [
                jnp.concatenate(
                    [cols[2 * (i + s) + u, pl.ds(y_start, rows_y), :] for u in range(2)], axis=1
                )
                for i in pairs
            ],
            axis=0,
        )
        right = jnp.concatenate(
            [
                jnp.concatenate([table[j, 2 * s + u + 1], table[j, 2 * s + u]], axis=1)
                for u in range(2)
            ],
            axis=0,
        )
        part = jnp.dot(left, right, preferred_element_type=jnp.float32)
        total = part if total is None else total + part
    return total


def blur_kernel(
    ids, cov, est, halo, img_own, img_other, fwd, quot, remote, near, pad, cols, image, *, taps
):
    core = ids[0]
    views, half, rows_y, depth = quot.shape
    rim = halo.shape[0]
    width = est.shape[1]
    blocks = cov.shape[2]
    block_width = width // blocks
    window = rows_y // block_width
    share_w = img_own.shape[2]
    margin = jnp.zeros((pad.shape[0], PAD, depth), jnp.float32)
    pad[:, :PAD, :] = margin
    pad[:, PAD + width :, :] = margin
    for r in range(half + rim):
        pad[rim * (1 - core) + r, PAD : PAD + width, :] = est[rim * core + r]
    for r in range(rim):
        pad[(half + rim) * core + r, PAD : PAD + width, :] = halo[r].astype(jnp.float32)
    fill_columns(pad, cols, taps[1], width)
    for r in range(half):
        if views == 1:
            own_at = pl.multiple_of(core * share_w, share_w)
            other_at = pl.multiple_of((1 - core) * share_w, share_w)
            image[0, r, pl.ds(own_at, share_w), :] = img_own[0, half * core + r]
            image[0, r, pl.ds(other_at, share_w), :] = img_other[r]
        else:
            image[core, r] = img_own[0, half * core + r]
            image[1 - core, r] = img_other[r]
    for j in range(views):
        view = ids[1] * views + j
        first = window_of(cov, view, blocks, window)
        mask = window_mask(cov, view, first, window, block_width)
        y_start = pl.multiple_of(first * block_width, block_width)
        blurred = band_dots(cols, y_start, rows_y, fwd, j, range(half // 2))
        remote[j] = jnp.zeros(remote.shape[1:], remote.dtype)
        for r in range(half):
            cells = image[j, r, pl.ds(y_start, rows_y), :]
            i, w = r // 2, r % 2
            below = blurred[i * rows_y : (i + 1) * rows_y, w * depth : (w + 1) * depth]
            ratio = jnp.where(mask, cells.astype(jnp.float32) / below, 0.0)
            quot[j, r] = ratio.astype(jnp.bfloat16)
        for r in range(rim):
            remote[j, r, pl.ds(y_start, rows_y), :] = quot[j, rim * core + r]
            near[j, r] = quot[j, rim * (1 - core) + r]


def correct_kernel(ids, cov, quot, near, remote, bwd, *rest, taps):
    *pieces, pad, cols, far, product = rest
    core, chip = ids[0], ids[1]
    views, half, rows_y, depth = quot.shape
    rim = near.shape[1]
    width = remote.shape[2]
    blocks = cov.shape[2]
    block_width = width // blocks
    window = rows_y // block_width
    product[...] = jnp.ones(product.shape, jnp.float32)
    far[...] = jnp.zeros(far.shape, jnp.float32)
    pad[...] = jnp.zeros(pad.shape, jnp.float32)
    for j in range(views):
        view = ids[1] * views + j
        first = window_of(cov, view, blocks, window)
        mask = window_mask(cov, view, first, window, block_width)
        y_start = pl.multiple_of(first * block_width, block_width)
        for r in range(half):
            pad[rim + r, PAD : PAD + rows_y, :] = quot[j, r].astype(jnp.float32)
        for r in range(rim):
            pad[(half + rim) * (1 - core) + r, PAD : PAD + rows_y, :] = near[j, r].astype(
                jnp.float32
            )
            far[PAD : PAD + width, :] = remote[j, r].astype(jnp.float32)
            pad[(half + rim) * core + r] = far[pl.ds(y_start, rows_y + 2 * PAD), :]
        fill_columns(pad, cols, taps[1], rows_y)
        pad[...] = jnp.zeros(pad.shape, jnp.float32)
        correction = band_dots(cols, 0, rows_y, bwd, j, range(half // 2))
        for r in range(half):
            i, w = r // 2, r % 2
            cells = correction[i * rows_y : (i + 1) * rows_y, w * depth : (w + 1) * depth]
            factor = jnp.where(mask, cells, 1.0)
            at = (r, pl.ds(y_start, rows_y), slice(None))
            product[at] = product[at] * factor
    rows = half // len(pieces)
    for step, piece in enumerate(pieces):
        for r in range(rows):
            piece[r] = product[(chip ^ step) * rows + r]


def combine_kernel(ids, est, *rest):
    *pieces, out = rest
    core, chip = ids[0], ids[1]
    rows = out.shape[0]
    half = est.shape[0] // 2
    for r in range(rows):
        total = est[half * core + chip * rows + r]
        for piece in pieces:
            total = total * piece[r]
        out[r] = total


def gather_kernel(ids, *rest):
    *pieces, out = rest
    core, chip = ids[0], ids[1]
    count = len(pieces) // 2
    rows = pieces[0].shape[0]
    half = out.shape[0] // 2
    for step in range(count):
        for r in range(rows):
            at = (chip ^ step) * rows + r
            out[half * core + at] = pieces[step][r]
            out[half * (1 - core) + at] = pieces[count + step][r]


def call(kernel, name, outs, kinds, scratch=(), flops=0):
    spaces = {"s": pltpu.SMEM, "v": pltpu.VMEM}
    return pl.pallas_call(
        kernel,
        name=name,
        out_shape=outs,
        in_specs=[pl.BlockSpec(memory_space=spaces[kind]) for kind in kinds],
        out_specs=jax.tree.map(lambda _: pl.BlockSpec(memory_space=pltpu.VMEM), outs),
        scratch_shapes=list(scratch),
        compiler_params=pltpu.CompilerParams(vmem_limit_bytes=VMEM_LIMIT),
        cost_estimate=pl.CostEstimate(flops=flops, bytes_accessed=1 << 20, transcendentals=0),
    )


def local(estimate, images, point_spread, covered):
    slab_x, width, depth = estimate.shape
    share_w = images.shape[2]
    _, taps_x, taps_y, taps_z = point_spread.shape
    taps = (taps_x, taps_y, taps_z)
    rim = (taps_x - 1) // 2
    half = slab_x // 2
    blocks = covered.shape[2]
    window = min(CAP, blocks)
    rows_y = window * (width // blocks)
    shares = width // share_w
    views = 2 // shares
    assert shares * views == 2
    group = lax.axis_index("view")
    chips = lax.axis_size("view") // 2
    core, chip = group % 2, group // 2
    ids = jnp.stack([core, chip]).astype(jnp.int32)
    reach = half + 2 * rim
    f32, bf16 = jnp.float32, jnp.bfloat16

    edge = lax.dynamic_slice_in_dim(estimate, (slab_x - rim) * core, rim, 0).astype(bf16)
    halo = swap_layers(edge)
    given = lax.dynamic_slice_in_dim(images[0], half * (1 - core), half, 0)
    img_other = swap_cores(given)

    spread = jnp.pad(point_spread, ((0, 0), (0, 0), (0, 8 - taps_y), (0, depth - taps_z)))
    table = pltpu.VMEM((views, taps_x + 2, taps_y * depth, depth), bf16)
    fwd, bwd = call(
        functools.partial(tables_kernel, taps=taps),
        "tables",
        (table, table),
        "sv",
        [pltpu.VMEM((taps_x * 8, depth), f32)] * 2,
    )(ids, spread)

    work = 2 * half * rows_y * depth * taps_x * taps_y * depth * views
    quot, remote, near = call(
        functools.partial(blur_kernel, taps=taps),
        "blur",
        (
            jax.ShapeDtypeStruct((views, half, rows_y, depth), bf16),
            jax.ShapeDtypeStruct((views, rim, width, depth), bf16),
            jax.ShapeDtypeStruct((views, rim, rows_y, depth), bf16),
        ),
        "ssvvvvv",
        [
            pltpu.VMEM((reach, width + 2 * PAD, depth), f32),
            pltpu.VMEM((reach, width, taps_y * depth), bf16),
            pltpu.VMEM((views, half, width, depth), bf16),
        ],
        work,
    )(ids, covered, estimate, halo, images, img_other, fwd)
    remote = swap_layers(remote)
    near = swap_cores(near)

    rows = half // chips
    pieces = call(
        functools.partial(correct_kernel, taps=taps),
        "correct",
        tuple(jax.ShapeDtypeStruct((rows, width, depth), f32) for _ in range(chips)),
        "ssvvvv",
        [
            pltpu.VMEM((reach, rows_y + 2 * PAD, depth), f32),
            pltpu.VMEM((reach, rows_y, taps_y * depth), bf16),
            pltpu.VMEM((width + 2 * PAD, depth), f32),
            pltpu.VMEM((half, width, depth), f32),
        ],
        work,
    )(ids, covered, quot, near, remote, bwd)
    arrived = [pieces[0]] + [swap_chips(pieces[step], step) for step in range(1, chips)]
    mine = call(
        combine_kernel,
        "combine",
        jax.ShapeDtypeStruct((rows, width, depth), f32),
        "sv" + "v" * chips,
    )(ids, estimate, *arrived)
    column = [mine] + [swap_chips(mine, step) for step in range(1, chips)]
    across = [swap_cores(piece) for piece in column]
    return call(
        gather_kernel,
        "gather",
        jax.ShapeDtypeStruct(estimate.shape, f32),
        "s" + "v" * (2 * chips),
    )(ids, *column, *across)


def solution(mesh):
    in_specs = (P("blk", None, None), P("view", "blk", None, None), P(), P(None, "blk", None))
    out_specs = P("blk", None, None)
    return jax.shard_map(local, mesh=mesh, in_specs=in_specs, out_specs=out_specs, check_vma=False)
```

time: 246 us -> 70.7 us (0.29)
  the two profiles are of different devices: /device:TPU:0 before, /device:TPU:3 now
where the time goes in v1:
time: 70.7 us; the launch traced here: 70.4 us
  waiting for transfers between devices  27.7 us (39%)
  Pallas kernels  21 us (30%)
  starting transfers between devices  15.5 us (22%)
  local copies, waits for them, and re-layouts  5.99 us (8%)
    ppermute x6, waiting for transfers between devices, swap_chips(): lax.ppermute(cells, 'view', [(i, i ^ 2 * step) for i in range(count)])  19.6 us
    pallas_call x1, Pallas kernels, local(): call(functools.partial(correct_kernel, taps=taps), 'correct', tuple((jax....  9.05 us
    ppermute x6, starting transfers between devices, swap_chips(): lax.ppermute(cells, 'view', [(i, i ^ 2 * step) for i in range(count)])  7.31 us
    ppermute x2, starting transfers between devices, swap_layers(): return lax.ppermute(cells, ('view', 'blk'), route)  6.39 us
    ppermute x2, waiting for transfers between devices, swap_layers(): return lax.ppermute(cells, ('view', 'blk'), route)  5.35 us
    pallas_call x1, Pallas kernels, local(): call(functools.partial(blur_kernel, taps=taps), 'blur', (jax.ShapeDtypeSt...  5.13 us
    pallas_call x1, Pallas kernels, local(): call(functools.partial(tables_kernel, taps=taps), 'tables', (table, table...  4.62 us
    unnamed x8, local copies, waits for them, and re-layouts  4.03 us
  transfers between devices with their start and end apart: 14, of which 8 were waited for; matrix products, arithmetic and copies ran while one was open for 4% of the time, Pallas kernels for 7%

profile of v1, /device:TPU:3, one launch (start us, length us, event | category | flops | bytes accessed | tf_op | source)
XLA Modules:
  0.0 70.4 jit_solution(7434050481119821800)
XLA Ops:
  0.0 1.0 %dynamic-slice_bitcast_fusion = bf16[8,128,128]{2,1,0:T(8,128)(2,1)S(1)} fusion(bf16[1,16,128,128]{3,2,1,0:T(8,128)(2,1)} %img_own.1, s32[]{:T(128)S(6)} %select_n.20), kind=kLoop, calls=%fused_computation | loop fusion | bytes 524292 | tf_op jit(solution)/shard_map/dynamic_slice | solution.py:279
  1.0 0.7 %collective-permute-start.1 = (bf16[8,128,128]{2,1,0:T(8,128)(2,1)S(1)}, bf16[8,128,128]{2,1,0:T(8,128)(2,1)S(1)}, u32[]{:S(2)}, u32[]{:S(2)}) collective-permute-start(bf16[8,128,128]{2,1,0:T(8,128)(2,1)S(1)} %dynamic-slice_bitcast_fusion), channel_id=1, source_target_pairs={{0,4},{4,0},{8,12},{12,8},{16,20},{20,16},{24,28},{28,24},{1,5},{5... | collective-permute-start | bytes 786440 | tf_op jit(solution)/shard_map/ppermute | solution.py:18
  1.7 1.0 %dynamic-slice_convert_fusion = bf16[4,128,128]{2,1,0:T(8,128)(2,1)S(1)} fusion(f32[16,128,128]{2,1,0:T(8,128)} %est.3, s32[]{:T(128)S(6)} %select_n.19), kind=kLoop, calls=%fused_computation.1 | loop fusion | bytes 262148 | tf_op jit(solution)/shard_map/convert_element_type | solution.py:277
  2.7 3.0 %collective-permute-start = (bf16[4,128,128]{2,1,0:T(8,128)(2,1)S(1)}, bf16[4,128,128]{2,1,0:T(8,128)(2,1)S(1)}, u32[]{:S(2)}, u32[]{:S(2)}) collective-permute-start(bf16[4,128,128]{2,1,0:T(8,128)(2,1)S(1)} %dynamic-slice_convert_fusion), channel_id=1, source_target_pairs={{4,1},{1,4},{5,2},{2,5},{6,3},{3,6},{12,9},{9,12},{13,10},{10,13},... | collective-permute-start | bytes 393224 | tf_op jit(solution)/shard_map/ppermute | solution.py:34
  5.7 0.8 %copy.7.cov = s32[8,1,4]{2,1,0:T(1,128)S(1)} copy(s32[8,1,4]{0,2,1:T(4,128)} %param.7) | data formatting | bytes 256 | tf_op args[3]
  6.5 1.0 %copy.5 = f32[8,9,7,25]{3,2,1,0:T(8,128)S(1)} copy(f32[8,9,7,25]{3,0,2,1:T(8,128)} %param.6) | data formatting | bytes 100800 | tf_op args[2]
  7.6 4.6 %tables.1 = (bf16[2,11,896,128]{3,2,1,0:T(8,128)(2,1)S(1)}, bf16[2,11,896,128]{3,2,1,0:T(8,128)(2,1)S(1)}) custom-call(s32[2]{0:T(128)S(1)} %pad_add_fusion.ids, f32[8,9,8,128]{3,2,1,0:T(8,128)S(1)} %pad.4.spread), custom_call_target="tpu_custom_call" | custom-call | bytes 1048576 | tf_op jit(solution)/shard_map/tables/pallas_call | solution.py:284
  12.3 1.2 %copy-done = f32[16,128,128]{2,1,0:T(8,128)S(1)} copy-done((f32[16,128,128]{2,1,0:T(8,128)S(1)}, f32[16,128,128]{2,1,0:T(8,128)}, u32[]{:S(2)}) %copy-start) | copy-done | bytes 1048600
  13.5 1.0 %copy-done.2 = bf16[1,16,128,128]{3,2,1,0:T(8,128)(2,1)S(1)} copy-done((bf16[1,16,128,128]{3,2,1,0:T(8,128)(2,1)S(1)}, bf16[1,16,128,128]{3,2,1,0:T(8,128)(2,1)}, u32[]{:S(2)}) %copy-start.2) | copy-done | bytes 524312
  14.5 5.1 %blur.1 = (bf16[2,8,96,128]{3,2,1,0:T(8,128)(2,1)S(1)}, bf16[2,4,128,128]{3,2,1,0:T(8,128)(2,1)S(1)}, bf16[2,4,96,128]{3,2,1,0:T(8,128)(2,1)S(1)}) custom-call(s32[2]{0:T(128)S(1)} %pad_add_fusion.ids, s32[8,1,4]{2,1,0:T(1,128)S(1)} %copy.7.cov, f32[16,128,128]{2,1,0:T(8,128)S(1)} %copy-done, bf16[4,128,128]{2,1,0:T(8,128)(2,1)S(1)} %collective-permute-done.halo, ...), custom_call_target="tpu_custom_call" | custom-call | flops 3170893824 | bytes 1048576 | tf_op jit(solution)/shard_map/blur/pallas_call | solution.py:293
  19.7 3.4 %collective-permute-start.3 = (bf16[2,4,128,128]{3,2,1,0:T(8,128)(2,1)S(1)}, bf16[2,4,128,128]{3,2,1,0:T(8,128)(2,1)S(1)}, u32[]{:S(2)}, u32[]{:S(2)}) collective-permute-start(bf16[2,4,128,128]{3,2,1,0:T(8,128)(2,1)S(1)} %get-tuple-element.17), channel_id=1, source_target_pairs={{4,1},{1,4},{5,2},{2,5},{6,3},{3,6},{12,9},{9,12},{13,10},{10,13},... | collective-permute-start | bytes 786440 | tf_op jit(solution)/shard_map/ppermute | solution.py:34
  23.1 1.4 %collective-permute-done.2.near = bf16[2,4,96,128]{3,2,1,0:T(8,128)(2,1)S(1)} collective-permute-done((bf16[2,4,96,128]{3,2,1,0:T(8,128)(2,1)S(1)}, bf16[2,4,96,128]{3,2,1,0:T(8,128)(2,1)S(1)}, u32[]{:S(2)}, u32[]{:S(2)}) %collective-permute-start.2) | collective-permute-done | bytes 196640 | tf_op jit(solution)/shard_map/ppermute | solution.py:18
  24.6 5.3 %collective-permute-done.3.remote = bf16[2,4,128,128]{3,2,1,0:T(8,128)(2,1)S(1)} collective-permute-done((bf16[2,4,128,128]{3,2,1,0:T(8,128)(2,1)S(1)}, bf16[2,4,128,128]{3,2,1,0:T(8,128)(2,1)S(1)}, u32[]{:S(2)}, u32[]{:S(2)}) %collective-permute-start.3) | collective-permute-done | bytes 262176 | tf_op jit(solution)/shard_map/ppermute | solution.py:34
  29.9 9.1 %correct.1 = (f32[2,128,128]{2,1,0:T(8,128)S(1)}, f32[2,128,128]{2,1,0:T(8,128)S(1)}, f32[2,128,128]{2,1,0:T(8,128)S(1)}, f32[2,128,128]{2,1,0:T(8,128)S(1)}) custom-call(s32[2]{0:T(128)S(1)} %pad_add_fusion.ids, s32[8,1,4]{2,1,0:T(1,128)S(1)} %copy.7.cov, bf16[2,8,96,128]{3,2,1,0:T(8,128)(2,1)S(1)} %get-tuple-element.15.quot, ...), custom_call_target="tpu_custom_call" | custom-call | flops 3170893824 | bytes 1048576 | tf_op jit(solution)/shard_map/correct/pallas_call | solution.py:313
  39.0 1.4 %collective-permute-start.4 = (f32[2,128,128]{2,1,0:T(8,128)S(1)}, f32[2,128,128]{2,1,0:T(8,128)S(1)}, u32[]{:S(2)}, u32[]{:S(2)}) collective-permute-start(f32[2,128,128]{2,1,0:T(8,128)S(1)} %get-tuple-element.20), channel_id=1, source_target_pairs={{0,8},{4,12},{8,0},{12,4},{16,24},{20,28},{24,16},{28,20},{1,9},{5... | collective-permute-start | bytes 393224 | tf_op jit(solution)/shard_map/ppermute | solution.py:23
  40.3 2.3 %collective-permute-start.5 = (f32[2,128,128]{2,1,0:T(8,128)S(1)}, f32[2,128,128]{2,1,0:T(8,128)S(1)}, u32[]{:S(2)}, u32[]{:S(2)}) collective-permute-start(f32[2,128,128]{2,1,0:T(8,128)S(1)} %get-tuple-element.21), channel_id=1, source_target_pairs={{0,16},{4,20},{8,24},{12,28},{16,0},{20,4},{24,8},{28,12},{1,17},{... | collective-permute-start | bytes 393224 | tf_op jit(solution)/shard_map/ppermute | solution.py:23
  42.6 1.7 %collective-permute-done.4.rest_1_ = f32[2,128,128]{2,1,0:T(8,128)S(1)} collective-permute-done((f32[2,128,128]{2,1,0:T(8,128)S(1)}, f32[2,128,128]{2,1,0:T(8,128)S(1)}, u32[]{:S(2)}, u32[]{:S(2)}) %collective-permute-start.4) | collective-permute-done | bytes 131104 | tf_op jit(solution)/shard_map/ppermute | solution.py:23
  44.4 7.7 %collective-permute-done.5.rest_2_ = f32[2,128,128]{2,1,0:T(8,128)S(1)} collective-permute-done((f32[2,128,128]{2,1,0:T(8,128)S(1)}, f32[2,128,128]{2,1,0:T(8,128)S(1)}, u32[]{:S(2)}, u32[]{:S(2)}) %collective-permute-start.5) | collective-permute-done | bytes 131104 | tf_op jit(solution)/shard_map/ppermute | solution.py:23
  52.6 2.4 %collective-permute-start.9 = (f32[2,128,128]{2,1,0:T(8,128)S(1)}, f32[2,128,128]{2,1,0:T(8,128)S(1)}, u32[]{:S(2)}, u32[]{:S(2)}) collective-permute-start(f32[2,128,128]{2,1,0:T(8,128)S(1)} %combine.1.rest_0_), channel_id=1, source_target_pairs={{0,24},{4,28},{8,16},{12,20},{16,8},{20,12},{24,0},{28,4},{1,25},{... | collective-permute-start | bytes 393224 | tf_op jit(solution)/shard_map/ppermute | solution.py:23
  55.0 1.2 %collective-permute-start.8 = (f32[2,128,128]{2,1,0:T(8,128)S(1)}, f32[2,128,128]{2,1,0:T(8,128)S(1)}, u32[]{:S(2)}, u32[]{:S(2)}) collective-permute-start(f32[2,128,128]{2,1,0:T(8,128)S(1)} %combine.1.rest_0_), channel_id=1, source_target_pairs={{0,16},{4,20},{8,24},{12,28},{16,0},{20,4},{24,8},{28,12},{1,17},{... | collective-permute-start | bytes 393224 | tf_op jit(solution)/shard_map/ppermute | solution.py:23
  56.8 1.6 %collective-permute-done.9.rest_3_ = f32[2,128,128]{2,1,0:T(8,128)S(1)} collective-permute-done((f32[2,128,128]{2,1,0:T(8,128)S(1)}, f32[2,128,128]{2,1,0:T(8,128)S(1)}, u32[]{:S(2)}, u32[]{:S(2)}) %collective-permute-start.9) | collective-permute-done | bytes 131104 | tf_op jit(solution)/shard_map/ppermute | solution.py:23
  58.4 8.6 %collective-permute-done.8.rest_2_ = f32[2,128,128]{2,1,0:T(8,128)S(1)} collective-permute-done((f32[2,128,128]{2,1,0:T(8,128)S(1)}, f32[2,128,128]{2,1,0:T(8,128)S(1)}, u32[]{:S(2)}, u32[]{:S(2)}) %collective-permute-start.8) | collective-permute-done | bytes 131104 | tf_op jit(solution)/shard_map/ppermute | solution.py:23
  67.5 0.9 %collective-permute-done.12.rest_6_ = f32[2,128,128]{2,1,0:T(8,128)S(1)} collective-permute-done((f32[2,128,128]{2,1,0:T(8,128)S(1)}, f32[2,128,128]{2,1,0:T(8,128)S(1)}, u32[]{:S(2)}, u32[]{:S(2)}) %collective-permute-start.12) | collective-permute-done | bytes 131104 | tf_op jit(solution)/shard_map/ppermute | solution.py:18
  68.8 1.6 %gather.1 = f32[16,128,128]{2,1,0:T(8,128)} custom-call(s32[2]{0:T(128)S(1)} %pad_add_fusion.ids, f32[2,128,128]{2,1,0:T(8,128)S(1)} %combine.1.rest_0_, f32[2,128,128]{2,1,0:T(8,128)S(1)} %collective-permute-done.7.rest_1_, f32[2,128,128]{2,1,0:T(8,128)S(1)} %collective-permute-done.8.rest_2_, f32[2,128,128]{2,1,0:T(8,128)S(1)} %collective-permute-done.9.rest_3_, ...), custom_call_target="tpu_custom_call" | custom-call | bytes 1048576 | tf_op jit(solution)/shard_map/gather/pallas_call | solution.py:335
  (21 shorter events, 2.2 us)
Async XLA Ops:
  1.0 11.3 %collective-permute-start.1 = (bf16[8,128,128]{2,1,0:T(8,128)(2,1)S(1)}, bf16[8,128,128]{2,1,0:T(8,128)(2,1)S(1)}, u32[]{:S(2)}, u32[]{:S(2)}) collective-permute-start(bf16[8,128,128]{2,1,0:T(8,128)(2,1)S(1)} %dynamic-slice_bitcast_fusion), channel_id=1, source_target_pairs={{0,4},{4,0},{8,12},{12,8},{16,20},{20,16},{24,28},{28,24},{1,5},{5... | collective-permute-start | bytes 786440 | tf_op jit(solution)/shard_map/ppermute | solution.py:18
  2.7 9.6 %collective-permute-start = (bf16[4,128,128]{2,1,0:T(8,128)(2,1)S(1)}, bf16[4,128,128]{2,1,0:T(8,128)(2,1)S(1)}, u32[]{:S(2)}, u32[]{:S(2)}) collective-permute-start(bf16[4,128,128]{2,1,0:T(8,128)(2,1)S(1)} %dynamic-slice_convert_fusion), channel_id=1, source_target_pairs={{4,1},{1,4},{5,2},{2,5},{6,3},{3,6},{12,9},{9,12},{13,10},{10,13},... | collective-permute-start | bytes 393224 | tf_op jit(solution)/shard_map/ppermute | solution.py:34
  12.3 1.2 %copy-start = (f32[16,128,128]{2,1,0:T(8,128)S(1)}, f32[16,128,128]{2,1,0:T(8,128)}, u32[]{:S(2)}) copy-start(f32[16,128,128]{2,1,0:T(8,128)} %est.3) | copy-start | bytes 3145732
  13.5 1.0 %copy-start.2 = (bf16[1,16,128,128]{3,2,1,0:T(8,128)(2,1)S(1)}, bf16[1,16,128,128]{3,2,1,0:T(8,128)(2,1)}, u32[]{:S(2)}) copy-start(bf16[1,16,128,128]{3,2,1,0:T(8,128)(2,1)} %img_own.1) | copy-start | bytes 1572868
  19.7 10.2 %collective-permute-start.3 = (bf16[2,4,128,128]{3,2,1,0:T(8,128)(2,1)S(1)}, bf16[2,4,128,128]{3,2,1,0:T(8,128)(2,1)S(1)}, u32[]{:S(2)}, u32[]{:S(2)}) collective-permute-start(bf16[2,4,128,128]{3,2,1,0:T(8,128)(2,1)S(1)} %get-tuple-element.17), channel_id=1, source_target_pairs={{4,1},{1,4},{5,2},{2,5},{6,3},{3,6},{12,9},{9,12},{13,10},{10,13},... | collective-permute-start | bytes 786440 | tf_op jit(solution)/shard_map/ppermute | solution.py:34
  23.0 1.5 %collective-permute-start.2 = (bf16[2,4,96,128]{3,2,1,0:T(8,128)(2,1)S(1)}, bf16[2,4,96,128]{3,2,1,0:T(8,128)(2,1)S(1)}, u32[]{:S(2)}, u32[]{:S(2)}) collective-permute-start(bf16[2,4,96,128]{3,2,1,0:T(8,128)(2,1)S(1)} %get-tuple-element.16), channel_id=1, source_target_pairs={{0,4},{4,0},{8,12},{12,8},{16,20},{20,16},{24,28},{28,24},{1,5},{5... | collective-permute-start | bytes 589832 | tf_op jit(solution)/shard_map/ppermute | solution.py:18
  29.9 22.1 %copy-start.1 = (f32[16,128,128]{2,1,0:T(8,128)S(1)}, f32[16,128,128]{2,1,0:T(8,128)}, u32[]{:S(2)}) copy-start(f32[16,128,128]{2,1,0:T(8,128)} %est.3) | copy-start | bytes 3145732
  39.0 5.4 %collective-permute-start.4 = (f32[2,128,128]{2,1,0:T(8,128)S(1)}, f32[2,128,128]{2,1,0:T(8,128)S(1)}, u32[]{:S(2)}, u32[]{:S(2)}) collective-permute-start(f32[2,128,128]{2,1,0:T(8,128)S(1)} %get-tuple-element.20), channel_id=1, source_target_pairs={{0,8},{4,12},{8,0},{12,4},{16,24},{20,28},{24,16},{28,20},{1,9},{5... | collective-permute-start | bytes 393224 | tf_op jit(solution)/shard_map/ppermute | solution.py:23
  40.3 11.7 %collective-permute-start.5 = (f32[2,128,128]{2,1,0:T(8,128)S(1)}, f32[2,128,128]{2,1,0:T(8,128)S(1)}, u32[]{:S(2)}, u32[]{:S(2)}) collective-permute-start(f32[2,128,128]{2,1,0:T(8,128)S(1)} %get-tuple-element.21), channel_id=1, source_target_pairs={{0,16},{4,20},{8,24},{12,28},{16,0},{20,4},{24,8},{28,12},{1,17},{... | collective-permute-start | bytes 393224 | tf_op jit(solution)/shard_map/ppermute | solution.py:23
  42.6 9.4 %collective-permute-start.6 = (f32[2,128,128]{2,1,0:T(8,128)S(1)}, f32[2,128,128]{2,1,0:T(8,128)S(1)}, u32[]{:S(2)}, u32[]{:S(2)}) collective-permute-start(f32[2,128,128]{2,1,0:T(8,128)S(1)} %get-tuple-element.22), channel_id=1, source_target_pairs={{0,24},{4,28},{8,16},{12,20},{16,8},{20,12},{24,0},{28,4},{1,25},{... | collective-permute-start | bytes 393224 | tf_op jit(solution)/shard_map/ppermute | solution.py:23
  52.6 5.8 %collective-permute-start.9 = (f32[2,128,128]{2,1,0:T(8,128)S(1)}, f32[2,128,128]{2,1,0:T(8,128)S(1)}, u32[]{:S(2)}, u32[]{:S(2)}) collective-permute-start(f32[2,128,128]{2,1,0:T(8,128)S(1)} %combine.1.rest_0_), channel_id=1, source_target_pairs={{0,24},{4,28},{8,16},{12,20},{16,8},{20,12},{24,0},{28,4},{1,25},{... | collective-permute-start | bytes 393224 | tf_op jit(solution)/shard_map/ppermute | solution.py:23
  55.0 12.0 %collective-permute-start.8 = (f32[2,128,128]{2,1,0:T(8,128)S(1)}, f32[2,128,128]{2,1,0:T(8,128)S(1)}, u32[]{:S(2)}, u32[]{:S(2)}) collective-permute-start(f32[2,128,128]{2,1,0:T(8,128)S(1)} %combine.1.rest_0_), channel_id=1, source_target_pairs={{0,16},{4,20},{8,24},{12,28},{16,0},{20,4},{24,8},{28,12},{1,17},{... | collective-permute-start | bytes 393224 | tf_op jit(solution)/shard_map/ppermute | solution.py:23
  56.3 11.2 %collective-permute-start.7 = (f32[2,128,128]{2,1,0:T(8,128)S(1)}, f32[2,128,128]{2,1,0:T(8,128)S(1)}, u32[]{:S(2)}, u32[]{:S(2)}) collective-permute-start(f32[2,128,128]{2,1,0:T(8,128)S(1)} %combine.1.rest_0_), channel_id=1, source_target_pairs={{0,8},{4,12},{8,0},{12,4},{16,24},{20,28},{24,16},{28,20},{1,9},{5... | collective-permute-start | bytes 393224 | tf_op jit(solution)/shard_map/ppermute | solution.py:23
  56.3 11.2 %collective-permute-start.10 = (f32[2,128,128]{2,1,0:T(8,128)S(1)}, f32[2,128,128]{2,1,0:T(8,128)S(1)}, u32[]{:S(2)}, u32[]{:S(2)}) collective-permute-start(f32[2,128,128]{2,1,0:T(8,128)S(1)} %combine.1.rest_0_), channel_id=1, source_target_pairs={{0,4},{4,0},{8,12},{12,8},{16,20},{20,16},{24,28},{28,24},{1,5},{5... | collective-permute-start | bytes 393224 | tf_op jit(solution)/shard_map/ppermute | solution.py:18
  58.4 9.1 %collective-permute-start.13 = (f32[2,128,128]{2,1,0:T(8,128)S(1)}, f32[2,128,128]{2,1,0:T(8,128)S(1)}, u32[]{:S(2)}, u32[]{:S(2)}) collective-permute-start(f32[2,128,128]{2,1,0:T(8,128)S(1)} %collective-permute-done.9.rest_3_), channel_id=1, source_target_pairs={{0,4},{4,0},{8,12},{12,8},{16,20},{20,16},{24,28},{28,24},{1,5},{5... | collective-permute-start | bytes 393224 | tf_op jit(solution)/shard_map/ppermute | solution.py:18
  67.0 1.4 %collective-permute-start.12 = (f32[2,128,128]{2,1,0:T(8,128)S(1)}, f32[2,128,128]{2,1,0:T(8,128)S(1)}, u32[]{:S(2)}, u32[]{:S(2)}) collective-permute-start(f32[2,128,128]{2,1,0:T(8,128)S(1)} %collective-permute-done.8.rest_2_), channel_id=1, source_target_pairs={{0,4},{4,0},{8,12},{12,8},{16,20},{20,16},{24,28},{28,24},{1,5},{5... | collective-permute-start | bytes 393224 | tf_op jit(solution)/shard_map/ppermute | solution.py:18
  67.4 1.3 %collective-permute-start.11 = (f32[2,128,128]{2,1,0:T(8,128)S(1)}, f32[2,128,128]{2,1,0:T(8,128)S(1)}, u32[]{:S(2)}, u32[]{:S(2)}) collective-permute-start(f32[2,128,128]{2,1,0:T(8,128)S(1)} %collective-permute-done.7.rest_1_), channel_id=1, source_target_pairs={{0,4},{4,0},{8,12},{12,8},{16,20},{20,16},{24,28},{28,24},{1,5},{5... | collective-permute-start | bytes 393224 | tf_op jit(solution)/shard_map/ppermute | solution.py:18

commit v2 on v1

--- a/solution.py
+++ b/solution.py
@@ -10,6 +10,10 @@
 CAP = 3
 LANES = 128
 PAD = 8
+HEADER = 16
+MARK = 256.0
+LEVEL = 32767.0
+SPAN = 16.6
 VMEM_LIMIT = 24 * 1024 * 1024
 
 
@@ -32,6 +36,32 @@
             high = 2 * chip * layers + layer + 1
             route += [(low, high), (high, low)]
     return lax.ppermute(cells, ("view", "blk"), route)
+
+
+def code_header(low, high):
+    low_mark = jnp.floor(low * MARK)
+    span_mark = jnp.floor(high * MARK) + 1.0 - low_mark
+    row = lax.broadcasted_iota(jnp.int32, (HEADER, LANES), 0)
+    header = jnp.where(row == 0, low_mark, span_mark).astype(jnp.int32).astype(jnp.int16)
+    return header, low_mark / MARK, (2 * LEVEL * MARK) / span_mark
+
+
+def encode(logs, low, scale):
+    steps = (logs - low) * scale - (LEVEL - 0.5)
+    steps = jnp.clip(jnp.floor(steps), -LEVEL, LEVEL)
+    return steps.astype(jnp.int32).astype(jnp.int16)
+
+
+def code_marks(piece):
+    header = piece[:HEADER, :].astype(jnp.int32).astype(jnp.float32)
+    step = header[1:2, :] * (1.0 / (2 * LEVEL * MARK))
+    return header[0:1, :] * (1.0 / MARK) + step * LEVEL, step
+
+
+def decode(piece, marks, at, rows):
+    middle, step = marks
+    cells = piece[at : at + rows, :].astype(jnp.int32).astype(jnp.float32)
+    return cells * step + middle
 
 
 def window_of(cov, view, blocks, window):
@@ -176,7 +206,7 @@
 
 
 def correct_kernel(ids, cov, quot, near, remote, bwd, *rest, taps):
-    *pieces, pad, cols, far, product = rest
+    *pieces, pad, cols, far, product, logs = rest
     core, chip = ids[0], ids[1]
     views, half, rows_y, depth = quot.shape
     rim = near.shape[1]
@@ -210,34 +240,58 @@
             at = (r, pl.ds(y_start, rows_y), slice(None))
             product[at] = product[at] * factor
     rows = half // len(pieces)
-    for step, piece in enumerate(pieces):
+    least = jnp.full((width, depth), jnp.inf, jnp.float32)
+    most = -least
+    for r in range(half):
+        cells = jnp.log(product[r])
+        logs[r] = cells
+        least = jnp.minimum(least, cells)
+        most = jnp.maximum(most, cells)
+    header, low, scale = code_header(jnp.min(least), jnp.max(most))
+    for r in range(rows):
+        pieces[0][r] = product[chip * rows + r]
+    for step in range(1, len(pieces)):
+        pieces[step][:HEADER, :] = header
         for r in range(rows):
-            piece[r] = product[(chip ^ step) * rows + r]
-
-
-def combine_kernel(ids, est, *rest):
+            at = HEADER + r * width
+            pieces[step][at : at + width, :] = encode(logs[(chip ^ step) * rows + r], low, scale)
+
+
+def combine_kernel(ids, est, own, *rest):
     *pieces, out = rest
     core, chip = ids[0], ids[1]
-    rows = out.shape[0]
+    rows, width, _ = own.shape
     half = est.shape[0] // 2
+    marks = [code_marks(piece) for piece in pieces]
+    all_logs = []
     for r in range(rows):
-        total = est[half * core + chip * rows + r]
-        for piece in pieces:
-            total = total * piece[r]
-        out[r] = total
+        logs = jnp.log(est[half * core + chip * rows + r] * own[r])
+        for piece, mark in zip(pieces, marks):
+            logs = logs + decode(piece, mark, HEADER + r * width, width)
+        all_logs.append(logs)
+    low = functools.reduce(jnp.minimum, all_logs)
+    high = functools.reduce(jnp.maximum, all_logs)
+    high = jnp.max(high)
+    header, low, scale = code_header(jnp.maximum(jnp.min(low), high - SPAN), high)
+    out[:HEADER, :] = header
+    for r, logs in enumerate(all_logs):
+        at = HEADER + r * width
+        out[at : at + width, :] = encode(logs, low, scale)
 
 
 def gather_kernel(ids, *rest):
     *pieces, out = rest
     core, chip = ids[0], ids[1]
     count = len(pieces) // 2
-    rows = pieces[0].shape[0]
+    width = out.shape[1]
     half = out.shape[0] // 2
-    for step in range(count):
+    rows = half // count
+    for place, piece in enumerate(pieces):
+        side = core if place < count else 1 - core
+        marks = code_marks(piece)
         for r in range(rows):
-            at = (chip ^ step) * rows + r
-            out[half * core + at] = pieces[step][r]
-            out[half * (1 - core) + at] = pieces[count + step][r]
+            at = half * side + (chip ^ (place % count)) * rows + r
+            out[at] = jnp.exp(decode(piece, marks, HEADER + r * width, width))
 
 
 def call(kernel, name, outs, kinds, scratch=(), flops=0):
@@ -310,15 +364,17 @@
     near = swap_cores(near)
 
     rows = half // chips
+    coded = jax.ShapeDtypeStruct((HEADER + rows * width, depth), jnp.int16)
     pieces = call(
         functools.partial(correct_kernel, taps=taps),
         "correct",
-        tuple(jax.ShapeDtypeStruct((rows, width, depth), f32) for _ in range(chips)),
+        (jax.ShapeDtypeStruct((rows, width, depth), f32),) + (coded,) * (chips - 1),
         "ssvvvv",
         [
             pltpu.VMEM((reach, rows_y + 2 * PAD, depth), f32),
             pltpu.VMEM((reach, rows_y, taps_y * depth), bf16),
             pltpu.VMEM((width + 2 * PAD, depth), f32),
+            pltpu.VMEM((half, width, depth), f32),
             pltpu.VMEM((half, width, depth), f32),
         ],
         work,
@@ -327,7 +383,7 @@
     mine = call(
         combine_kernel,
         "combine",
-        jax.ShapeDtypeStruct((rows, width, depth), f32),
+        coded,
         "sv" + "v" * chips,
     )(ids, estimate, *arrived)
     column = [mine] + [swap_chips(mine, step) for step in range(1, chips)]

time: 70.7 us -> 62.5 us (0.88)
  the two profiles are of different devices: /device:TPU:3 before, /device:TPU:5 now
where the time goes in v2:
time: 62.5 us; the launch traced here: 62.2 us
  starting transfers between devices  23 us (37%)
  Pallas kernels  21.9 us (35%)
  waiting for transfers between devices  11.2 us (18%)
  local copies, waits for them, and re-layouts  5.99 us (10%)
    ppermute x6, starting transfers between devices, swap_cores(): return lax.ppermute(cells, 'view', [(i, i ^ 1) for i in range(count)])  10.2 us
    pallas_call x1, Pallas kernels, local(): call(functools.partial(correct_kernel, taps=taps), 'correct', (jax.ShapeD...  9.54 us
    ppermute x6, starting transfers between devices, swap_chips(): lax.ppermute(cells, 'view', [(i, i ^ 2 * step) for i in range(count)])  7.22 us
    ppermute x2, starting transfers between devices, swap_layers(): return lax.ppermute(cells, ('view', 'blk'), route)  5.49 us
    ppermute x6, waiting for transfers between devices, swap_chips(): lax.ppermute(cells, 'view', [(i, i ^ 2 * step) for i in range(count)])  5.46 us
    pallas_call x1, Pallas kernels, local(): call(functools.partial(blur_kernel, taps=taps), 'blur', (jax.ShapeDtypeSt...  5.12 us
    pallas_call x1, Pallas kernels, local(): call(functools.partial(tables_kernel, taps=taps), 'tables', (table, table...  4.62 us
    unnamed x8, local copies, waits for them, and re-layouts  4.03 us
  transfers between devices with their start and end apart: 14, of which 6 were waited for; matrix products, arithmetic and copies ran while one was open for 5% of the time, Pallas kernels for 7%

profile of v2, /device:TPU:5, one launch (start us, length us, event | category | flops | bytes accessed | tf_op | source)
XLA Modules:
  0.0 62.2 jit_solution(15681792075761166704)
XLA Ops:
  0.0 1.0 %dynamic-slice_bitcast_fusion = bf16[8,128,128]{2,1,0:T(8,128)(2,1)S(1)} fusion(bf16[1,16,128,128]{3,2,1,0:T(8,128)(2,1)} %img_own.1, s32[]{:T(128)S(6)} %select_n.20), kind=kLoop, calls=%fused_computation | loop fusion | bytes 524292 | tf_op jit(solution)/shard_map/dynamic_slice | solution.py:333
  1.7 1.0 %dynamic-slice_convert_fusion = bf16[4,128,128]{2,1,0:T(8,128)(2,1)S(1)} fusion(f32[16,128,128]{2,1,0:T(8,128)} %est.3, s32[]{:T(128)S(6)} %select_n.19), kind=kLoop, calls=%fused_computation.1 | loop fusion | bytes 262148 | tf_op jit(solution)/shard_map/convert_element_type | solution.py:331
  2.7 3.0 %collective-permute-start = (bf16[4,128,128]{2,1,0:T(8,128)(2,1)S(1)}, bf16[4,128,128]{2,1,0:T(8,128)(2,1)S(1)}, u32[]{:S(2)}, u32[]{:S(2)}) collective-permute-start(bf16[4,128,128]{2,1,0:T(8,128)(2,1)S(1)} %dynamic-slice_convert_fusion), channel_id=1, source_target_pairs={{4,1},{1,4},{5,2},{2,5},{6,3},{3,6},{12,9},{9,12},{13,10},{10,13},... | collective-permute-start | bytes 393224 | tf_op jit(solution)/shard_map/ppermute | solution.py:38
  6.5 1.0 %copy.5 = f32[8,9,7,25]{3,2,1,0:T(8,128)S(1)} copy(f32[8,9,7,25]{3,0,2,1:T(8,128)} %param.6) | data formatting | bytes 100800 | tf_op args[2]
  7.6 4.6 %tables.1 = (bf16[2,11,896,128]{3,2,1,0:T(8,128)(2,1)S(1)}, bf16[2,11,896,128]{3,2,1,0:T(8,128)(2,1)S(1)}) custom-call(s32[2]{0:T(128)S(1)} %pad_add_fusion.ids, f32[8,9,8,128]{3,2,1,0:T(8,128)S(1)} %pad.4.spread), custom_call_target="tpu_custom_call" | custom-call | bytes 1048576 | tf_op jit(solution)/shard_map/tables/pallas_call | solution.py:338
  12.3 1.2 %copy-done = f32[16,128,128]{2,1,0:T(8,128)S(1)} copy-done((f32[16,128,128]{2,1,0:T(8,128)S(1)}, f32[16,128,128]{2,1,0:T(8,128)}, u32[]{:S(2)}) %copy-start) | copy-done | bytes 1048600
  13.5 1.0 %copy-done.2 = bf16[1,16,128,128]{3,2,1,0:T(8,128)(2,1)S(1)} copy-done((bf16[1,16,128,128]{3,2,1,0:T(8,128)(2,1)S(1)}, bf16[1,16,128,128]{3,2,1,0:T(8,128)(2,1)}, u32[]{:S(2)}) %copy-start.2) | copy-done | bytes 524312
  14.6 5.1 %blur.1 = (bf16[2,8,96,128]{3,2,1,0:T(8,128)(2,1)S(1)}, bf16[2,4,128,128]{3,2,1,0:T(8,128)(2,1)S(1)}, bf16[2,4,96,128]{3,2,1,0:T(8,128)(2,1)S(1)}) custom-call(s32[2]{0:T(128)S(1)} %pad_add_fusion.ids, s32[8,1,4]{2,1,0:T(1,128)S(1)} %copy.7.cov, f32[16,128,128]{2,1,0:T(8,128)S(1)} %copy-done, bf16[4,128,128]{2,1,0:T(8,128)(2,1)S(1)} %collective-permute-done.halo, ...), custom_call_target="tpu_custom_call" | custom-call | flops 3170893824 | bytes 1048576 | tf_op jit(solution)/shard_map/blur/pallas_call | solution.py:347
  19.7 2.5 %collective-permute-start.3 = (bf16[2,4,128,128]{3,2,1,0:T(8,128)(2,1)S(1)}, bf16[2,4,128,128]{3,2,1,0:T(8,128)(2,1)S(1)}, u32[]{:S(2)}, u32[]{:S(2)}) collective-permute-start(bf16[2,4,128,128]{3,2,1,0:T(8,128)(2,1)S(1)} %get-tuple-element.17), channel_id=1, source_target_pairs={{4,1},{1,4},{5,2},{2,5},{6,3},{3,6},{12,9},{9,12},{13,10},{10,13},... | collective-permute-start | bytes 786440 | tf_op jit(solution)/shard_map/ppermute | solution.py:38
  22.1 1.1 %collective-permute-start.2 = (bf16[2,4,96,128]{3,2,1,0:T(8,128)(2,1)S(1)}, bf16[2,4,96,128]{3,2,1,0:T(8,128)(2,1)S(1)}, u32[]{:S(2)}, u32[]{:S(2)}) collective-permute-start(bf16[2,4,96,128]{3,2,1,0:T(8,128)(2,1)S(1)} %get-tuple-element.16), channel_id=1, source_target_pairs={{0,4},{4,0},{8,12},{12,8},{16,20},{20,16},{24,28},{28,24},{1,5},{5... | collective-permute-start | bytes 589832 | tf_op jit(solution)/shard_map/ppermute | solution.py:22
  23.2 1.1 %collective-permute-done.2.near = bf16[2,4,96,128]{3,2,1,0:T(8,128)(2,1)S(1)} collective-permute-done((bf16[2,4,96,128]{3,2,1,0:T(8,128)(2,1)S(1)}, bf16[2,4,96,128]{3,2,1,0:T(8,128)(2,1)S(1)}, u32[]{:S(2)}, u32[]{:S(2)}) %collective-permute-start.2) | collective-permute-done | bytes 196640 | tf_op jit(solution)/shard_map/ppermute | solution.py:22
  24.3 3.4 %collective-permute-done.3.remote = bf16[2,4,128,128]{3,2,1,0:T(8,128)(2,1)S(1)} collective-permute-done((bf16[2,4,128,128]{3,2,1,0:T(8,128)(2,1)S(1)}, bf16[2,4,128,128]{3,2,1,0:T(8,128)(2,1)S(1)}, u32[]{:S(2)}, u32[]{:S(2)}) %collective-permute-start.3) | collective-permute-done | bytes 262176 | tf_op jit(solution)/shard_map/ppermute | solution.py:38
  27.7 9.5 %correct.1 = (f32[2,128,128]{2,1,0:T(8,128)S(1)}, s16[272,128]{1,0:T(8,128)(2,1)S(1)}, s16[272,128]{1,0:T(8,128)(2,1)S(1)}, s16[272,128]{1,0:T(8,128)(2,1)S(1)}) custom-call(s32[2]{0:T(128)S(1)} %pad_add_fusion.ids, s32[8,1,4]{2,1,0:T(1,128)S(1)} %copy.7.cov, bf16[2,8,96,128]{3,2,1,0:T(8,128)(2,1)S(1)} %get-tuple-element.15.quot, ...), custom_call_target="tpu_custom_call" | custom-call | flops 3170893824 | bytes 1048576 | tf_op jit(solution)/shard_map/correct/pallas_call | solution.py:368
  37.2 1.4 %collective-permute-start.4 = (s16[272,128]{1,0:T(8,128)(2,1)S(1)}, s16[272,128]{1,0:T(8,128)(2,1)S(1)}, u32[]{:S(2)}, u32[]{:S(2)}) collective-permute-start(s16[272,128]{1,0:T(8,128)(2,1)S(1)} %get-tuple-element.20), channel_id=1, source_target_pairs={{0,8},{4,12},{8,0},{12,4},{16,24},{20,28},{24,16},{28,20},{1,9},{5... | collective-permute-start | bytes 208904 | tf_op jit(solution)/shard_map/ppermute | solution.py:27
  38.6 2.2 %collective-permute-start.5 = (s16[272,128]{1,0:T(8,128)(2,1)S(1)}, s16[272,128]{1,0:T(8,128)(2,1)S(1)}, u32[]{:S(2)}, u32[]{:S(2)}) collective-permute-start(s16[272,128]{1,0:T(8,128)(2,1)S(1)} %get-tuple-element.21), channel_id=1, source_target_pairs={{0,16},{4,20},{8,24},{12,28},{16,0},{20,4},{24,8},{28,12},{1,17},{... | collective-permute-start | bytes 208904 | tf_op jit(solution)/shard_map/ppermute | solution.py:27
  40.8 2.7 %collective-permute-done.5.rest_1_ = s16[272,128]{1,0:T(8,128)(2,1)S(1)} collective-permute-done((s16[272,128]{1,0:T(8,128)(2,1)S(1)}, s16[272,128]{1,0:T(8,128)(2,1)S(1)}, u32[]{:S(2)}, u32[]{:S(2)}) %collective-permute-start.5) | collective-permute-done | bytes 69664 | tf_op jit(solution)/shard_map/ppermute | solution.py:27
  43.5 2.8 %collective-permute-done.6.rest_2_ = s16[272,128]{1,0:T(8,128)(2,1)S(1)} collective-permute-done((s16[272,128]{1,0:T(8,128)(2,1)S(1)}, s16[272,128]{1,0:T(8,128)(2,1)S(1)}, u32[]{:S(2)}, u32[]{:S(2)}) %collective-permute-start.6) | collective-permute-done | bytes 69664 | tf_op jit(solution)/shard_map/ppermute | solution.py:27
  46.3 0.8 %combine.1.rest_0_ = s16[272,128]{1,0:T(8,128)(2,1)S(1)} custom-call(s32[2]{0:T(128)S(1)} %pad_add_fusion.ids, f32[16,128,128]{2,1,0:T(8,128)S(1)} %copy-done.1, f32[2,128,128]{2,1,0:T(8,128)S(1)} %get-tuple-element.19.own, s16[272,128]{1,0:T(8,128)(2,1)S(1)} %collective-permute-done.4.rest_0_, s16[272,128]{1,0:T(8,128)(2,1)S(1)} %collective-permute-done.5.rest_1_, ...), custom_call_target="tpu_custom_call" | custom-call | bytes 1048576 | tf_op jit(solution)/shard_map/combine/pallas_call | solution.py:383
  47.7 3.1 %collective-permute-start.7 = (s16[272,128]{1,0:T(8,128)(2,1)S(1)}, s16[272,128]{1,0:T(8,128)(2,1)S(1)}, u32[]{:S(2)}, u32[]{:S(2)}) collective-permute-start(s16[272,128]{1,0:T(8,128)(2,1)S(1)} %combine.1.rest_0_), channel_id=1, source_target_pairs={{0,8},{4,12},{8,0},{12,4},{16,24},{20,28},{24,16},{28,20},{1,9},{5... | collective-permute-start | bytes 208904 | tf_op jit(solution)/shard_map/ppermute | solution.py:27
  50.7 5.3 %collective-permute-start.10 = (s16[272,128]{1,0:T(8,128)(2,1)S(1)}, s16[272,128]{1,0:T(8,128)(2,1)S(1)}, u32[]{:S(2)}, u32[]{:S(2)}) collective-permute-start(s16[272,128]{1,0:T(8,128)(2,1)S(1)} %combine.1.rest_0_), channel_id=1, source_target_pairs={{0,4},{4,0},{8,12},{12,8},{16,20},{20,16},{24,28},{28,24},{1,5},{5... | collective-permute-start | bytes 208904 | tf_op jit(solution)/shard_map/ppermute | solution.py:22
  56.0 1.8 %collective-permute-start.13 = (s16[272,128]{1,0:T(8,128)(2,1)S(1)}, s16[272,128]{1,0:T(8,128)(2,1)S(1)}, u32[]{:S(2)}, u32[]{:S(2)}) collective-permute-start(s16[272,128]{1,0:T(8,128)(2,1)S(1)} %collective-permute-done.9.rest_3_), channel_id=1, source_target_pairs={{0,4},{4,0},{8,12},{12,8},{16,20},{20,16},{24,28},{28,24},{1,5},{5... | collective-permute-start | bytes 208904 | tf_op jit(solution)/shard_map/ppermute | solution.py:22
  57.9 1.3 %collective-permute-start.12 = (s16[272,128]{1,0:T(8,128)(2,1)S(1)}, s16[272,128]{1,0:T(8,128)(2,1)S(1)}, u32[]{:S(2)}, u32[]{:S(2)}) collective-permute-start(s16[272,128]{1,0:T(8,128)(2,1)S(1)} %collective-permute-done.8.rest_2_), channel_id=1, source_target_pairs={{0,4},{4,0},{8,12},{12,8},{16,20},{20,16},{24,28},{28,24},{1,5},{5... | collective-permute-start | bytes 208904 | tf_op jit(solution)/shard_map/ppermute | solution.py:22
  59.2 0.9 %collective-permute-done.12.rest_6_ = s16[272,128]{1,0:T(8,128)(2,1)S(1)} collective-permute-done((s16[272,128]{1,0:T(8,128)(2,1)S(1)}, s16[272,128]{1,0:T(8,128)(2,1)S(1)}, u32[]{:S(2)}, u32[]{:S(2)}) %collective-permute-start.12) | collective-permute-done | bytes 69664 | tf_op jit(solution)/shard_map/ppermute | solution.py:22
  60.5 1.7 %gather.1 = f32[16,128,128]{2,1,0:T(8,128)} custom-call(s32[2]{0:T(128)S(1)} %pad_add_fusion.ids, s16[272,128]{1,0:T(8,128)(2,1)S(1)} %combine.1.rest_0_, s16[272,128]{1,0:T(8,128)(2,1)S(1)} %collective-permute-done.7.rest_1_, s16[272,128]{1,0:T(8,128)(2,1)S(1)} %collective-permute-done.8.rest_2_, s16[272,128]{1,0:T(8,128)(2,1)S(1)} %collective-permute-done.9.rest_3_, ...), custom_call_target="tpu_custom_call" | custom-call | bytes 1048576 | tf_op jit(solution)/shard_map/gather/pallas_call | solution.py:391
  (21 shorter events, 2.6 us)
Async XLA Ops:
  1.0 11.3 %collective-permute-start.1 = (bf16[8,128,128]{2,1,0:T(8,128)(2,1)S(1)}, bf16[8,128,128]{2,1,0:T(8,128)(2,1)S(1)}, u32[]{:S(2)}, u32[]{:S(2)}) collective-permute-start(bf16[8,128,128]{2,1,0:T(8,128)(2,1)S(1)} %dynamic-slice_bitcast_fusion), channel_id=1, source_target_pairs={{0,4},{4,0},{8,12},{12,8},{16,20},{20,16},{24,28},{28,24},{1,5},{5... | collective-permute-start | bytes 786440 | tf_op jit(solution)/shard_map/ppermute | solution.py:22
  2.7 9.6 %collective-permute-start = (bf16[4,128,128]{2,1,0:T(8,128)(2,1)S(1)}, bf16[4,128,128]{2,1,0:T(8,128)(2,1)S(1)}, u32[]{:S(2)}, u32[]{:S(2)}) collective-permute-start(bf16[4,128,128]{2,1,0:T(8,128)(2,1)S(1)} %dynamic-slice_convert_fusion), channel_id=1, source_target_pairs={{4,1},{1,4},{5,2},{2,5},{6,3},{3,6},{12,9},{9,12},{13,10},{10,13},... | collective-permute-start | bytes 393224 | tf_op jit(solution)/shard_map/ppermute | solution.py:38
  12.3 1.2 %copy-start = (f32[16,128,128]{2,1,0:T(8,128)S(1)}, f32[16,128,128]{2,1,0:T(8,128)}, u32[]{:S(2)}) copy-start(f32[16,128,128]{2,1,0:T(8,128)} %est.3) | copy-start | bytes 3145732
  13.5 1.0 %copy-start.2 = (bf16[1,16,128,128]{3,2,1,0:T(8,128)(2,1)S(1)}, bf16[1,16,128,128]{3,2,1,0:T(8,128)(2,1)}, u32[]{:S(2)}) copy-start(bf16[1,16,128,128]{3,2,1,0:T(8,128)(2,1)} %img_own.1) | copy-start | bytes 1572868
  19.7 8.0 %collective-permute-start.3 = (bf16[2,4,128,128]{3,2,1,0:T(8,128)(2,1)S(1)}, bf16[2,4,128,128]{3,2,1,0:T(8,128)(2,1)S(1)}, u32[]{:S(2)}, u32[]{:S(2)}) collective-permute-start(bf16[2,4,128,128]{3,2,1,0:T(8,128)(2,1)S(1)} %get-tuple-element.17), channel_id=1, source_target_pairs={{4,1},{1,4},{5,2},{2,5},{6,3},{3,6},{12,9},{9,12},{13,10},{10,13},... | collective-permute-start | bytes 786440 | tf_op jit(solution)/shard_map/ppermute | solution.py:38
  22.1 2.1 %collective-permute-start.2 = (bf16[2,4,96,128]{3,2,1,0:T(8,128)(2,1)S(1)}, bf16[2,4,96,128]{3,2,1,0:T(8,128)(2,1)S(1)}, u32[]{:S(2)}, u32[]{:S(2)}) collective-permute-start(bf16[2,4,96,128]{3,2,1,0:T(8,128)(2,1)S(1)} %get-tuple-element.16), channel_id=1, source_target_pairs={{0,4},{4,0},{8,12},{12,8},{16,20},{20,16},{24,28},{28,24},{1,5},{5... | collective-permute-start | bytes 589832 | tf_op jit(solution)/shard_map/ppermute | solution.py:22
  27.7 18.6 %copy-start.1 = (f32[16,128,128]{2,1,0:T(8,128)S(1)}, f32[16,128,128]{2,1,0:T(8,128)}, u32[]{:S(2)}) copy-start(f32[16,128,128]{2,1,0:T(8,128)} %est.3) | copy-start | bytes 3145732
  37.2 3.6 %collective-permute-start.4 = (s16[272,128]{1,0:T(8,128)(2,1)S(1)}, s16[272,128]{1,0:T(8,128)(2,1)S(1)}, u32[]{:S(2)}, u32[]{:S(2)}) collective-permute-start(s16[272,128]{1,0:T(8,128)(2,1)S(1)} %get-tuple-element.20), channel_id=1, source_target_pairs={{0,8},{4,12},{8,0},{12,4},{16,24},{20,28},{24,16},{28,20},{1,9},{5... | collective-permute-start | bytes 208904 | tf_op jit(solution)/shard_map/ppermute | solution.py:27
  38.6 4.9 %collective-permute-start.5 = (s16[272,128]{1,0:T(8,128)(2,1)S(1)}, s16[272,128]{1,0:T(8,128)(2,1)S(1)}, u32[]{:S(2)}, u32[]{:S(2)}) collective-permute-start(s16[272,128]{1,0:T(8,128)(2,1)S(1)} %get-tuple-element.21), channel_id=1, source_target_pairs={{0,16},{4,20},{8,24},{12,28},{16,0},{20,4},{24,8},{28,12},{1,17},{... | collective-permute-start | bytes 208904 | tf_op jit(solution)/shard_map/ppermute | solution.py:27
  40.8 5.5 %collective-permute-start.6 = (s16[272,128]{1,0:T(8,128)(2,1)S(1)}, s16[272,128]{1,0:T(8,128)(2,1)S(1)}, u32[]{:S(2)}, u32[]{:S(2)}) collective-permute-start(s16[272,128]{1,0:T(8,128)(2,1)S(1)} %get-tuple-element.22), channel_id=1, source_target_pairs={{0,24},{4,28},{8,16},{12,20},{16,8},{20,12},{24,0},{28,4},{1,25},{... | collective-permute-start | bytes 208904 | tf_op jit(solution)/shard_map/ppermute | solution.py:27
  47.1 8.9 %collective-permute-start.9 = (s16[272,128]{1,0:T(8,128)(2,1)S(1)}, s16[272,128]{1,0:T(8,128)(2,1)S(1)}, u32[]{:S(2)}, u32[]{:S(2)}) collective-permute-start(s16[272,128]{1,0:T(8,128)(2,1)S(1)} %combine.1.rest_0_), channel_id=1, source_target_pairs={{0,24},{4,28},{8,16},{12,20},{16,8},{20,12},{24,0},{28,4},{1,25},{... | collective-permute-start | bytes 208904 | tf_op jit(solution)/shard_map/ppermute | solution.py:27
  47.7 10.2 %collective-permute-start.8 = (s16[272,128]{1,0:T(8,128)(2,1)S(1)}, s16[272,128]{1,0:T(8,128)(2,1)S(1)}, u32[]{:S(2)}, u32[]{:S(2)}) collective-permute-start(s16[272,128]{1,0:T(8,128)(2,1)S(1)} %combine.1.rest_0_), channel_id=1, source_target_pairs={{0,16},{4,20},{8,24},{12,28},{16,0},{20,4},{24,8},{28,12},{1,17},{... | collective-permute-start | bytes 208904 | tf_op jit(solution)/shard_map/ppermute | solution.py:27
  47.7 11.5 %collective-permute-start.7 = (s16[272,128]{1,0:T(8,128)(2,1)S(1)}, s16[272,128]{1,0:T(8,128)(2,1)S(1)}, u32[]{:S(2)}, u32[]{:S(2)}) collective-permute-start(s16[272,128]{1,0:T(8,128)(2,1)S(1)} %combine.1.rest_0_), channel_id=1, source_target_pairs={{0,8},{4,12},{8,0},{12,4},{16,24},{20,28},{24,16},{28,20},{1,9},{5... | collective-permute-start | bytes 208904 | tf_op jit(solution)/shard_map/ppermute | solution.py:27
  50.7 8.5 %collective-permute-start.10 = (s16[272,128]{1,0:T(8,128)(2,1)S(1)}, s16[272,128]{1,0:T(8,128)(2,1)S(1)}, u32[]{:S(2)}, u32[]{:S(2)}) collective-permute-start(s16[272,128]{1,0:T(8,128)(2,1)S(1)} %combine.1.rest_0_), channel_id=1, source_target_pairs={{0,4},{4,0},{8,12},{12,8},{16,20},{20,16},{24,28},{28,24},{1,5},{5... | collective-permute-start | bytes 208904 | tf_op jit(solution)/shard_map/ppermute | solution.py:22
  56.0 3.2 %collective-permute-start.13 = (s16[272,128]{1,0:T(8,128)(2,1)S(1)}, s16[272,128]{1,0:T(8,128)(2,1)S(1)}, u32[]{:S(2)}, u32[]{:S(2)}) collective-permute-start(s16[272,128]{1,0:T(8,128)(2,1)S(1)} %collective-permute-done.9.rest_3_), channel_id=1, source_target_pairs={{0,4},{4,0},{8,12},{12,8},{16,20},{20,16},{24,28},{28,24},{1,5},{5... | collective-permute-start | bytes 208904 | tf_op jit(solution)/shard_map/ppermute | solution.py:22
  57.9 2.2 %collective-permute-start.12 = (s16[272,128]{1,0:T(8,128)(2,1)S(1)}, s16[272,128]{1,0:T(8,128)(2,1)S(1)}, u32[]{:S(2)}, u32[]{:S(2)}) collective-permute-start(s16[272,128]{1,0:T(8,128)(2,1)S(1)} %collective-permute-done.8.rest_2_), channel_id=1, source_target_pairs={{0,4},{4,0},{8,12},{12,8},{16,20},{20,16},{24,28},{28,24},{1,5},{5... | collective-permute-start | bytes 208904 | tf_op jit(solution)/shard_map/ppermute | solution.py:22
  59.2 1.3 %collective-permute-start.11 = (s16[272,128]{1,0:T(8,128)(2,1)S(1)}, s16[272,128]{1,0:T(8,128)(2,1)S(1)}, u32[]{:S(2)}, u32[]{:S(2)}) collective-permute-start(s16[272,128]{1,0:T(8,128)(2,1)S(1)} %collective-permute-done.7.rest_1_), channel_id=1, source_target_pairs={{0,4},{4,0},{8,12},{12,8},{16,20},{20,16},{24,28},{28,24},{1,5},{5... | collective-permute-start | bytes 208904 | tf_op jit(solution)/shard_map/ppermute | solution.py:22

commit v3 on v2

v3 whole, which is shorter than its diff:
```python
import functools

import jax
import jax.numpy as jnp
from jax import lax
from jax.experimental import pallas as pl
from jax.experimental.pallas import tpu as pltpu
from jax.sharding import PartitionSpec as P

CAP = 3
LANES = 128
PAD = 8
HEADER = 16
MARK = 256.0
LEVEL = 32767.0
SPAN = 16.6
VMEM_LIMIT = 24 * 1024 * 1024


def swap_cores(cells):
    count = lax.axis_size("view")
    return lax.ppermute(cells, "view", [(i, i ^ 1) for i in range(count)])


def swap_chips(cells, step):
    count = lax.axis_size("view")
    return lax.ppermute(cells, "view", [(i, i ^ (2 * step)) for i in range(count)])


def swap_layers(cells):
    views, layers = lax.axis_size("view"), lax.axis_size("blk")
    route = []
    for chip in range(views // 2):
        for layer in range(layers - 1):
            low = (2 * chip + 1) * layers + layer
            high = 2 * chip * layers + layer + 1
            route += [(low, high), (high, low)]
    return lax.ppermute(cells, ("view", "blk"), route)


def code_header(low, high):
    low_mark = jnp.floor(low * MARK)
    span_mark = jnp.floor(high * MARK) + 1.0 - low_mark
    row = lax.broadcasted_iota(jnp.int32, (HEADER, LANES), 0)
    header = jnp.where(row == 0, low_mark, span_mark).astype(jnp.int32).astype(jnp.int16)
    return header, low_mark / MARK, (2 * LEVEL * MARK) / span_mark


def encode(logs, low, scale):
    steps = (logs - low) * scale - (LEVEL - 0.5)
    steps = jnp.clip(jnp.floor(steps), -LEVEL, LEVEL)
    return steps.astype(jnp.int32).astype(jnp.int16)


def code_marks(piece):
    header = piece[:HEADER, :].astype(jnp.int32).astype(jnp.float32)
    step = header[1:2, :] * (1.0 / (2 * LEVEL * MARK))
    return header[0:1, :] * (1.0 / MARK) + step * LEVEL, step


def decode(piece, marks, at, rows):
    middle, step = marks
    cells = piece[at : at + rows, :].astype(jnp.int32).astype(jnp.float32)
    return cells * step + middle


def window_of(cov, view, blocks, window):
    first = jnp.int32(blocks - window)
    for block in range(blocks - window - 1, -1, -1):
        first = jnp.where(cov[view, 0, block] > 0, jnp.int32(block), first)
    return first


def window_mask(cov, view, first, window, block_width):
    row = lax.broadcasted_iota(jnp.int32, (window * block_width, LANES), 0)
    mask = jnp.zeros(row.shape, jnp.int32)
    for block in range(window):
        inside = (row >= block * block_width) & (row < (block + 1) * block_width)
        mask = jnp.where(inside, cov[view, 0, first + block], mask)
    return mask > 0


def canonical(core, row, last):
    return jnp.where(core == 0, row, last - row)


def payload_kernel(ids, est, images, edge, given, rows, sems):
    core = ids[0]
    rim = edge.shape[0]
    half = given.shape[0]
    copy_rows = pltpu.make_async_copy(
        est.at[pl.ds((est.shape[0] - rim) * core, rim)], rows, sems.at[0]
    )
    copy_given = pltpu.make_async_copy(
        images.at[0, pl.ds(half * (1 - core), half)], given, sems.at[1]
    )
    copy_rows.start()
    copy_given.start()
    copy_rows.wait()
    edge[...] = rows[...].astype(edge.dtype)
    copy_given.wait()


def tables_kernel(ids, spread, est, table, cols, rows, pad, sems, *, taps):
    taps_x, taps_y, taps_z = taps
    core, chip = ids[0], ids[1]
    rim_z = (taps_z - 1) // 2
    depth = LANES
    count, width = cols.shape[0], cols.shape[1]
    margin = jnp.zeros((count, PAD, depth), jnp.float32)
    pad[:, :PAD, :] = margin
    pad[:, PAD + width :, :] = margin
    copies = [
        pltpu.make_async_copy(
            est.at[canonical(core, i, est.shape[0] - 1)], pad.at[i, pl.ds(PAD, width)], sems.at[i]
        )
        for i in range(count)
    ]
    for copy in copies:
        copy.start()
    row = lax.broadcasted_iota(jnp.int32, (depth, depth), 0)
    col = lax.broadcasted_iota(jnp.int32, (depth, depth), 1)
    band = jnp.abs(row - col) <= rim_z
    at = row - rim_z
    place = ((col == at) | (col == at + depth)) & (row < taps_z)
    place = jnp.where(place, 1.0, 0.0).astype(jnp.bfloat16)
    for j in range(table.shape[0]):
        taps_all = spread[chip * table.shape[0] + j]
        kernel = (taps_all / jnp.sum(taps_all)).astype(jnp.bfloat16)
        kernel = kernel.reshape(-1, LANES)
        rows[...] = jnp.dot(kernel, place, preferred_element_type=jnp.float32)
        zero = jnp.zeros((taps_y * depth, depth), jnp.bfloat16)
        table[j, 0] = zero
        table[j, taps_x + 1] = zero

        def fill(a, carry):
            at_x = canonical(1 - core, a, taps_x - 1) * 8
            for b in range(taps_y):
                line = rows[pl.ds(at_x + (taps_y - 1 - b), 1), :]
                line = jnp.broadcast_to(line, (depth, depth))
                line = pltpu.roll(line, 0, 1, stride=1, stride_axis=0)
                line = jnp.where(band, line, 0.0).astype(jnp.bfloat16)
                table[j, a + 1, b * depth : (b + 1) * depth, :] = line
            return carry

        lax.fori_loop(0, taps_x, fill, 0)
    for copy in copies:
        copy.wait()
    fill_columns(pad, cols, taps_y, width)


def fill_columns(pad, cols, taps_y, rows_y):
    rim_y = (taps_y - 1) // 2
    for x in range(cols.shape[0]):
        for b in range(taps_y):
            low = PAD - rim_y + b
            cols[x, :, b * LANES : (b + 1) * LANES] = pad[x, low : low + rows_y, :].astype(
                jnp.bfloat16
            )


def left_side(slab, pairs, s):
    return jnp.concatenate(
        [jnp.concatenate([slab(2 * (i + s) + u) for u in range(2)], axis=1) for i in pairs], axis=0
    )


def right_side(table, j, s):
    return jnp.concatenate(
        [
            jnp.concatenate([table[j, 2 * s + u + 1], table[j, 2 * s + u]], axis=1)
            for u in range(2)
        ],
        axis=0,
    )


def right_side_turned(table, j, s):
    taps_x = table.shape[1] - 2
    taps_y = table.shape[2] // LANES
    lines = []
    for w in range(2):
        line = []
        for u in range(2):
            at = taps_x - 1 - (2 * s + u - w) + 1
            for b in range(taps_y):
                low = (taps_y - 1 - b) * LANES
                line.append(table[j, at, low : low + LANES, :])
        lines.append(jnp.concatenate(line, axis=1))
    return jnp.concatenate(lines, axis=0)


def blur_kernel(
    ids, cov, halo, img_own, img_other, cols, table, quot, remote, near, pad, edge, image, sems, *, taps
):
    core, chip = ids[0], ids[1]
    views, half, rows_y, depth = quot.shape
    rim, width, _ = halo.shape
    blocks = cov.shape[2]
    block_width = width // blocks
    window = rows_y // block_width
    share_w = img_own.shape[2]
    if views == 1:
        own_at = pl.multiple_of(core * share_w, share_w)
        other_at = pl.multiple_of((1 - core) * share_w, share_w)
        own_to = image.at[0, :, pl.ds(own_at, share_w)]
        other_to = image.at[0, :, pl.ds(other_at, share_w)]
    else:
        own_to = image.at[core]
        other_to = image.at[1 - core]
    copies = [
        pltpu.make_async_copy(img_own.at[0, pl.ds(half * core, half)], own_to, sems.at[0]),
        pltpu.make_async_copy(img_other, other_to, sems.at[1]),
    ]
    for copy in copies:
        copy.start()
    margin = jnp.zeros((rim, PAD, depth), jnp.float32)
    pad[:, :PAD, :] = margin
    pad[:, PAD + width :, :] = margin
    for x in range(rim):
        pad[x, PAD : PAD + width, :] = halo[canonical(core, x, rim - 1)].astype(jnp.float32)
    fill_columns(pad, edge, taps[1], width)
    for copy in copies:
        copy.wait()
    for j in range(views):
        view = chip * views + j
        first = window_of(cov, view, blocks, window)
        mask = window_mask(cov, view, first, window, block_width)
        y_start = pl.multiple_of(first * block_width, block_width)

        def slab(x):
            part = edge.at[x] if x < rim else cols.at[x - rim]
            return part[pl.ds(y_start, rows_y), :]

        blurred = None
        for s in range((table.shape[1] - 1) // 2):
            part = lax.dot_general(
                left_side(slab, range(half // 2), s),
                right_side_turned(table, j, s),
                (((1,), (1,)), ((), ())),
                preferred_element_type=jnp.float32,
            )
            blurred = part if blurred is None else blurred + part
        remote[j] = jnp.zeros(remote.shape[1:], remote.dtype)
        for r in range(half):
            cells = image[j, canonical(core, r, half - 1), pl.ds(y_start, rows_y), :]
            i, w = r // 2, r % 2
            below = blurred[i * rows_y : (i + 1) * rows_y, w * depth : (w + 1) * depth]
            ratio = jnp.where(mask, cells.astype(jnp.float32) / below, 0.0).astype(jnp.bfloat16)
            quot[j, r] = ratio
            if r < rim:
                remote[j, r, pl.ds(y_start, rows_y), :] = ratio
            else:
                near[j, r - rim] = ratio


def inner_kernel(quot, near, table, sums, pad, cols, *, taps):
    views, half, rows_y, depth = quot.shape
    rim = near.shape[1]
    pairs = half // 2
    steps = (table.shape[1] - 1) // 2
    margin = jnp.zeros((half + rim, PAD, depth), jnp.float32)
    for j in range(views):
        pad[j, :, :PAD, :] = margin
        pad[j, :, PAD + rows_y :, :] = margin
        for r in range(half):
            pad[j, r, PAD : PAD + rows_y, :] = quot[j, r].astype(jnp.float32)
        for r in range(rim):
            pad[j, half + rim - 1 - r, PAD : PAD + rows_y, :] = near[j, r].astype(jnp.float32)
        fill_columns(pad.at[j], cols.at[j], taps[1], rows_y)
        total = None
        for s in range(steps - 1, -1, -1):
            skip = max(0, rim // 2 - s)
            part = jnp.dot(
                left_side(lambda x: cols[j, x - rim], range(skip, pairs), s),
                right_side(table, j, s),
                preferred_element_type=jnp.float32,
            )
            if total is None:
                total = part
            elif not skip:
                total = total + part
            else:
                cut = skip * rows_y
                total = jnp.concatenate([total[:cut], total[cut:] + part], axis=0)
        sums[j] = total


def correct_kernel(ids, cov, remote, sums, table, *rest, taps):
    *pieces, pad, cols, far, product, logs = rest
    chip = ids[1]
    views, rim, width, depth = remote.shape
    half = product.shape[0]
    rows_y = cols.shape[2]
    blocks = cov.shape[2]
    block_width = width // blocks
    window = rows_y // block_width
    product[...] = jnp.ones(product.shape, jnp.float32)
    margin = jnp.zeros((rim, PAD, depth), jnp.float32)
    for j in range(views):
        view = chip * views + j
        first = window_of(cov, view, blocks, window)
        mask = window_mask(cov, view, first, window, block_width)
        y_start = pl.multiple_of(first * block_width, block_width)
        far[j, :, :PAD, :] = margin
        far[j, :, PAD + width :, :] = margin
        for r in range(rim):
            far[j, rim - 1 - r, PAD : PAD + width, :] = remote[j, r].astype(jnp.float32)
        for r in range(rim):
            pad[j, r] = far[j, r, pl.ds(y_start, rows_y + 2 * PAD), :]
        fill_columns(pad.at[j], cols.at[j], taps[1], rows_y)
        edges = [None] * (half // 2)
        for s in range(rim // 2):
            pairs = range(rim // 2 - s)
            part = jnp.dot(
                left_side(lambda x: cols[j, x], pairs, s),
                right_side(table, j, s),
                preferred_element_type=jnp.float32,
            )
            for i in pairs:
                cells = part[i * rows_y : (i + 1) * rows_y]
                edges[i] = cells if edges[i] is None else edges[i] + cells
        for r in range(half):
            i, w = r // 2, r % 2
            cells = sums[j, i * rows_y : (i + 1) * rows_y, w * depth : (w + 1) * depth]
            if edges[i] is not None:
                cells = cells + edges[i][:, w * depth : (w + 1) * depth]
            factor = jnp.where(mask, cells, 1.0)
            at = (r, pl.ds(y_start, rows_y), slice(None))
            product[at] = product[at] * factor
    rows = half // len(pieces)
    least = jnp.full((width, depth), jnp.inf, jnp.float32)
    most = -least
    for r in range(half):
        cells = jnp.log(product[r])
        logs[r] = cells
        least = jnp.minimum(least, cells)
        most = jnp.maximum(most, cells)
    header, low, scale = code_header(jnp.min(least), jnp.max(most))
    for r in range(rows):
        pieces[0][r] = product[chip * rows + r]
    for step in range(1, len(pieces)):
        pieces[step][:HEADER, :] = header
        for r in range(rows):
            at = HEADER + r * width
            pieces[step][at : at + width, :] = encode(logs[(chip ^ step) * rows + r], low, scale)


def combine_kernel(ids, est, own, *rest):
    *pieces, out, held, sems = rest
    core, chip = ids[0], ids[1]
    rows, width, _ = own.shape
    copies = [
        pltpu.make_async_copy(
            est.at[canonical(core, chip * rows + r, est.shape[0] - 1)], held.at[r], sems.at[r]
        )
        for r in range(rows)
    ]
    for copy in copies:
        copy.start()
    marks = [code_marks(piece) for piece in pieces]
    for copy in copies:
        copy.wait()
    all_logs = []
    for r in range(rows):
        logs = jnp.log(held[r] * own[r])
        for piece, mark in zip(pieces, marks):
            logs = logs + decode(piece, mark, HEADER + r * width, width)
        all_logs.append(logs)
    low = functools.reduce(jnp.minimum, all_logs)
    high = functools.reduce(jnp.maximum, all_logs)
    high = jnp.max(high)
    header, low, scale = code_header(jnp.maximum(jnp.min(low), high - SPAN), high)
    out[:HEADER, :] = header
    for r, logs in enumerate(all_logs):
        at = HEADER + r * width
        out[at : at + width, :] = encode(logs, low, scale)


def gather_kernel(ids, *rest):
    *pieces, out = rest
    core, chip = ids[0], ids[1]
    count = len(pieces) // 2
    slab_x, width, _ = out.shape
    rows = slab_x // 2 // count
    for place, piece in enumerate(pieces):
        side = core if place < count else 1 - core
        marks = code_marks(piece)
        for r in range(rows):
            at = canonical(side, (chip ^ (place % count)) * rows + r, slab_x - 1)
            out[at] = jnp.exp(decode(piece, marks, HEADER + r * width, width))


def call(kernel, name, outs, kinds, scratch=(), flops=0, out_kinds=None):
    spaces = {"s": pltpu.SMEM, "v": pltpu.VMEM, "a": pl.ANY}
    many = isinstance(outs, tuple)
    out_kinds = out_kinds or "v" * (len(outs) if many else 1)
    out_specs = tuple(pl.BlockSpec(memory_space=spaces[kind]) for kind in out_kinds)
    return pl.pallas_call(
        kernel,
        name=name,
        out_shape=outs,
        in_specs=[pl.BlockSpec(memory_space=spaces[kind]) for kind in kinds],
        out_specs=out_specs if many else out_specs[0],
        scratch_shapes=list(scratch),
        compiler_params=pltpu.CompilerParams(vmem_limit_bytes=VMEM_LIMIT),
        cost_estimate=pl.CostEstimate(flops=flops, bytes_accessed=1 << 20, transcendentals=0),
    )


def local(estimate, images, point_spread, covered):
    slab_x, width, depth = estimate.shape
    share_w = images.shape[2]
    _, taps_x, taps_y, taps_z = point_spread.shape
    taps = (taps_x, taps_y, taps_z)
    rim = (taps_x - 1) // 2
    half = slab_x // 2
    blocks = covered.shape[2]
    window = min(CAP, blocks)
    rows_y = window * (width // blocks)
    shares = width // share_w
    views = 2 // shares
    assert shares * views == 2 and half == 2 * rim and depth == LANES
    group = lax.axis_index("view")
    chips = lax.axis_size("view") // 2
    core, chip = group % 2, group // 2
    ids = jnp.stack([core, chip]).astype(jnp.int32)
    inner = half + rim
    f32, bf16 = jnp.float32, jnp.bfloat16
    shape = jax.ShapeDtypeStruct
    deep = taps_y * depth
    wide = width + 2 * PAD
    tall = rows_y + 2 * PAD
    sems = pltpu.SemaphoreType.DMA
    work = 2 * half * rows_y * depth * taps_x * taps_y * depth * views

    edge, given = call(
        payload_kernel,
        "payload",
        (shape((rim, width, depth), bf16), shape((half, share_w, depth), bf16)),
        "saa",
        [pltpu.VMEM((rim, width, depth), f32), sems((2,))],
        out_kinds="va",
    )(ids, estimate, images)
    halo = swap_layers(edge)
    img_other = swap_cores(given)

    spread = jnp.pad(point_spread, ((0, 0), (0, 0), (0, 8 - taps_y), (0, depth - taps_z)))
    table, cols = call(
        functools.partial(tables_kernel, taps=taps),
        "tables",
        (
            pltpu.VMEM((views, taps_x + 2, deep, depth), bf16),
            pltpu.VMEM((inner, width, deep), bf16),
        ),
        "sva",
        [
            pltpu.VMEM((taps_x * 8, depth), f32),
            pltpu.VMEM((inner, wide, depth), f32),
            sems((inner,)),
        ],
        work // 2,
    )(ids, spread, estimate)

    quot, remote, near = call(
        functools.partial(blur_kernel, taps=taps),
        "blur",
        (
            pltpu.VMEM((views, half, rows_y, depth), bf16),
            shape((views, rim, width, depth), bf16),
            shape((views, rim, rows_y, depth), bf16),
        ),
        "ssvaavv",
        [
            pltpu.VMEM((rim, wide, depth), f32),
            pltpu.VMEM((rim, width, deep), bf16),
            pltpu.VMEM((views, half, width, depth), bf16),
            sems((2,)),
        ],
        work,
    )(ids, covered, halo, images, img_other, cols, table)
    near = swap_cores(near)
    remote = swap_layers(remote)

    sums = call(
        functools.partial(inner_kernel, taps=taps),
        "inner",
        pltpu.VMEM((views, half // 2 * rows_y, 2 * depth), f32),
        "vvv",
        [
            pltpu.VMEM((views, inner, tall, depth), f32),
            pltpu.VMEM((views, inner, rows_y, deep), bf16),
        ],
        work,
    )(quot, near, table)

    rows = half // chips
    coded = shape((HEADER + rows * width, depth), jnp.int16)
    pieces = call(
        functools.partial(correct_kernel, taps=taps),
        "correct",
        (shape((rows, width, depth), f32),) + (coded,) * (chips - 1),
        "ssvvv",
        [
            pltpu.VMEM((views, rim, tall, depth), f32),
            pltpu.VMEM((views, rim, rows_y, deep), bf16),
            pltpu.VMEM((views, rim, wide, depth), f32),
            pltpu.VMEM((half, width, depth), f32),
            pltpu.VMEM((half, width, depth), f32),
        ],
        work // 4,
    )(ids, covered, remote, sums, table)
    arrived = [pieces[0]] + [swap_chips(pieces[step], step) for step in range(1, chips)]
    mine = call(
        combine_kernel,
        "combine",
        coded,
        "sa" + "v" * chips,
        [pltpu.VMEM((rows, width, depth), f32), sems((rows,))],
    )(ids, estimate, *arrived)
    column = [mine] + [swap_chips(mine, step) for step in range(1, chips)]
    across = [swap_cores(piece) for piece in column]
    return call(
        gather_kernel,
        "gather",
        shape(estimate.shape, f32),
        "s" + "v" * (2 * chips),
    )(ids, *column, *across)


def solution(mesh):
    in_specs = (P("blk", None, None), P("view", "blk", None, None), P(), P(None, "blk", None))
    out_specs = P("blk", None, None)
    return jax.shard_map(local, mesh=mesh, in_specs=in_specs, out_specs=out_specs, check_vma=False)
```

time: 62.5 us -> 55.2 us (0.88)
  Pallas kernels: 21.9 us -> 18.9 us
  waiting for transfers between devices: 11.2 us -> 9.24 us
  starting transfers between devices: 23 us -> 21.3 us
  local copies, waits for them, and re-layouts: 5.99 us -> 5.29 us
    pallas_call x5 -> x7, Pallas kernels: 21.9 us -> 18.9 us  [the longest x1 5.12 us: local(): call(functools.partial(tables_kernel, taps=taps), 'tables', (pltpu.VMEM((...]
    ppermute x6, starting transfers between devices: 10.2 us -> 8.85 us  [swap_cores(): return lax.ppermute(cells, 'view', [(i, i ^ 1) for i in range(count)])]
    unnamed x8 -> x12, local copies, waits for them, and re-layouts: 4.03 us -> 5.26 us
    ppermute x2, waiting for transfers between devices: 3.39 us -> 2.18 us  [swap_layers(): return lax.ppermute(cells, ('view', 'blk'), route)]
    ppermute x6, waiting for transfers between devices: 2.32 us -> 1.25 us  [swap_cores(): return lax.ppermute(cells, 'view', [(i, i ^ 1) for i in range(count)])]
    convert_element_type x1 -> x0, local copies, waits for them, and re-layouts: 0.97 us -> none  [local(): lax.dynamic_slice_in_dim(estimate, (slab_x - rim) * core, rim, 0)]
    dynamic_slice x1 -> x0, local copies, waits for them, and re-layouts: 0.97 us -> none  [local(): given = lax.dynamic_slice_in_dim(images[0], half * (1 - core), half, 0)]
  transfers between devices with their start and end apart: 14 -> 14, of which waited for: 6 -> 5; matrix products, arithmetic and copies ran while one was open for 5% -> 3% of each run, Pallas kernels for 7% -> 16%
where the time goes in v3:
time: 55.2 us; the launch traced here: 54.9 us
  starting transfers between devices  21.3 us (39%)
  Pallas kernels  18.9 us (34%)
  waiting for transfers between devices  9.24 us (17%)
  local copies, waits for them, and re-layouts  5.29 us (10%)
    ppermute x6, starting transfers between devices, swap_cores(): return lax.ppermute(cells, 'view', [(i, i ^ 1) for i in range(count)])  8.85 us
    ppermute x6, starting transfers between devices, swap_chips(): lax.ppermute(cells, 'view', [(i, i ^ 2 * step) for i in range(count)])  7.28 us
    ppermute x6, waiting for transfers between devices, swap_chips(): lax.ppermute(cells, 'view', [(i, i ^ 2 * step) for i in range(count)])  5.81 us
    unnamed x12, local copies, waits for them, and re-layouts  5.26 us
    ppermute x2, starting transfers between devices, swap_layers(): return lax.ppermute(cells, ('view', 'blk'), route)  5.14 us
    pallas_call x1, Pallas kernels, local(): call(functools.partial(tables_kernel, taps=taps), 'tables', (pltpu.VMEM((...  5.12 us
    pallas_call x1, Pallas kernels, local(): call(functools.partial(blur_kernel, taps=taps), 'blur', (pltpu.VMEM((view...  4.57 us
    pallas_call x1, Pallas kernels, local(): call(functools.partial(inner_kernel, taps=taps), 'inner', pltpu.VMEM((vie...  3.64 us
  transfers between devices with their start and end apart: 14, of which 5 were waited for; matrix products, arithmetic and copies ran while one was open for 3% of the time, Pallas kernels for 16%

profile of v3, /device:TPU:5, one launch (start us, length us, event | category | flops | bytes accessed | tf_op | source)
XLA Modules:
  0.0 54.9 jit_solution(3194102490366823485)
XLA Ops:
  0.1 1.2 %copy-done = f32[16,128,128]{2,1,0:T(8,128)S(1)} copy-done((f32[16,128,128]{2,1,0:T(8,128)S(1)}, f32[16,128,128]{2,1,0:T(8,128)}, u32[]{:S(2)}) %copy-start) | copy-done | bytes 1048600
  1.3 1.0 %copy-done.3 = bf16[1,16,128,128]{3,2,1,0:T(8,128)(2,1)S(1)} copy-done((bf16[1,16,128,128]{3,2,1,0:T(8,128)(2,1)S(1)}, bf16[1,16,128,128]{3,2,1,0:T(8,128)(2,1)}, u32[]{:S(2)}) %copy-start.3) | copy-done | bytes 524312
  3.0 0.7 %collective-permute-start.1 = (bf16[8,128,128]{2,1,0:T(8,128)(2,1)S(1)}, bf16[8,128,128]{2,1,0:T(8,128)(2,1)S(1)}, u32[]{:S(2)}, u32[]{:S(2)}) collective-permute-start(bf16[8,128,128]{2,1,0:T(8,128)(2,1)S(1)} %get-tuple-element.17), channel_id=1, source_target_pairs={{0,4},{4,0},{8,12},{12,8},{16,20},{20,16},{24,28},{28,24},{1,5},{5... | collective-permute-start | bytes 786440 | tf_op jit(solution)/shard_map/ppermute | solution.py:22
  3.7 3.0 %collective-permute-start = (bf16[4,128,128]{2,1,0:T(8,128)(2,1)S(1)}, bf16[4,128,128]{2,1,0:T(8,128)(2,1)S(1)}, u32[]{:S(2)}, u32[]{:S(2)}) collective-permute-start(bf16[4,128,128]{2,1,0:T(8,128)(2,1)S(1)} %get-tuple-element.16), channel_id=1, source_target_pairs={{4,1},{1,4},{5,2},{2,5},{6,3},{3,6},{12,9},{9,12},{13,10},{10,13},... | collective-permute-start | bytes 393224 | tf_op jit(solution)/shard_map/ppermute | solution.py:38
  6.7 0.8 %copy.7.cov = s32[8,1,4]{2,1,0:T(1,128)S(1)} copy(s32[8,1,4]{0,2,1:T(4,128)} %param.7) | data formatting | bytes 256 | tf_op args[3]
  7.5 1.0 %copy.5 = f32[8,9,7,25]{3,2,1,0:T(8,128)S(1)} copy(f32[8,9,7,25]{3,0,2,1:T(8,128)} %param.6) | data formatting | bytes 100800 | tf_op args[2]
  8.6 1.2 %copy-done.1 = f32[16,128,128]{2,1,0:T(8,128)S(1)} copy-done((f32[16,128,128]{2,1,0:T(8,128)S(1)}, f32[16,128,128]{2,1,0:T(8,128)}, u32[]{:S(2)}) %copy-start.1) | copy-done | bytes 1048600
  9.8 5.1 %tables.1 = (bf16[2,11,896,128]{3,2,1,0:T(8,128)(2,1)S(1)}, bf16[12,128,896]{2,1,0:T(8,128)(2,1)S(1)}) custom-call(s32[2]{0:T(128)S(1)} %pad_add_fusion.ids, f32[8,9,8,128]{3,2,1,0:T(8,128)S(1)} %pad.4.spread, f32[16,128,128]{2,1,0:T(8,128)S(1)} %copy-done.1), custom_call_target="tpu_custom_call" | custom-call | flops 1585446912 | bytes 1048576 | tf_op jit(solution)/shard_map/tables/pallas_call | solution.py:449
  14.9 4.6 %blur.1 = (bf16[2,8,96,128]{3,2,1,0:T(8,128)(2,1)S(1)}, bf16[2,4,128,128]{3,2,1,0:T(8,128)(2,1)S(1)}, bf16[2,4,96,128]{3,2,1,0:T(8,128)(2,1)S(1)}) custom-call(s32[2]{0:T(128)S(1)} %pad_add_fusion.ids, s32[8,1,4]{2,1,0:T(1,128)S(1)} %copy.7.cov, bf16[4,128,128]{2,1,0:T(8,128)(2,1)S(1)} %collective-permute-done.halo, bf16[1,16,128,128]{3,2,1,0:T(8,128)(2,1)S(1)} %copy-done.4, ...), custom_call_target="tpu_custom_call" | custom-call | flops 3170893824 | bytes 1048576 | tf_op jit(solution)/shard_map/blur/pallas_call | solution.py:465
  20.0 2.1 %collective-permute-start.2 = (bf16[2,4,128,128]{3,2,1,0:T(8,128)(2,1)S(1)}, bf16[2,4,128,128]{3,2,1,0:T(8,128)(2,1)S(1)}, u32[]{:S(2)}, u32[]{:S(2)}) collective-permute-start(bf16[2,4,128,128]{3,2,1,0:T(8,128)(2,1)S(1)} %get-tuple-element.20), channel_id=1, source_target_pairs={{4,1},{1,4},{5,2},{2,5},{6,3},{3,6},{12,9},{9,12},{13,10},{10,13},... | collective-permute-start | bytes 786440 | tf_op jit(solution)/shard_map/ppermute | solution.py:38
  22.1 3.6 %inner.1.sums = f32[2,384,256]{2,1,0:T(8,128)S(1)} custom-call(bf16[2,8,96,128]{3,2,1,0:T(8,128)(2,1)S(1)} %get-tuple-element.21.quot, bf16[2,4,96,128]{3,2,1,0:T(8,128)(2,1)S(1)} %collective-permute-done.3.near, bf16[2,11,896,128]{3,2,1,0:T(8,128)(2,1)S(1)} %get-tuple-element.19.table), custom_call_target="tpu_custom_call" | custom-call | flops 3170893824 | bytes 1048576 | tf_op jit(solution)/shard_map/inner/pallas_call | solution.py:485
  25.8 2.2 %collective-permute-done.2.remote = bf16[2,4,128,128]{3,2,1,0:T(8,128)(2,1)S(1)} collective-permute-done((bf16[2,4,128,128]{3,2,1,0:T(8,128)(2,1)S(1)}, bf16[2,4,128,128]{3,2,1,0:T(8,128)(2,1)S(1)}, u32[]{:S(2)}, u32[]{:S(2)}) %collective-permute-start.2) | collective-permute-done | bytes 262176 | tf_op jit(solution)/shard_map/ppermute | solution.py:38
  28.0 2.1 %correct.1 = (f32[2,128,128]{2,1,0:T(8,128)S(1)}, s16[272,128]{1,0:T(8,128)(2,1)S(1)}, s16[272,128]{1,0:T(8,128)(2,1)S(1)}, s16[272,128]{1,0:T(8,128)(2,1)S(1)}) custom-call(s32[2]{0:T(128)S(1)} %pad_add_fusion.ids, s32[8,1,4]{2,1,0:T(1,128)S(1)} %copy.7.cov, bf16[2,4,128,128]{3,2,1,0:T(8,128)(2,1)S(1)} %collective-permute-done.2.remote, ...), custom_call_target="tpu_custom_call" | custom-call | flops 792723456 | bytes 1048576 | tf_op jit(solution)/shard_map/correct/pallas_call | solution.py:499
  30.1 1.4 %collective-permute-start.4 = (s16[272,128]{1,0:T(8,128)(2,1)S(1)}, s16[272,128]{1,0:T(8,128)(2,1)S(1)}, u32[]{:S(2)}, u32[]{:S(2)}) collective-permute-start(s16[272,128]{1,0:T(8,128)(2,1)S(1)} %get-tuple-element.24), channel_id=1, source_target_pairs={{0,8},{4,12},{8,0},{12,4},{16,24},{20,28},{24,16},{28,20},{1,9},{5... | collective-permute-start | bytes 208904 | tf_op jit(solution)/shard_map/ppermute | solution.py:27
  31.5 2.3 %collective-permute-start.5 = (s16[272,128]{1,0:T(8,128)(2,1)S(1)}, s16[272,128]{1,0:T(8,128)(2,1)S(1)}, u32[]{:S(2)}, u32[]{:S(2)}) collective-permute-start(s16[272,128]{1,0:T(8,128)(2,1)S(1)} %get-tuple-element.25), channel_id=1, source_target_pairs={{0,16},{4,20},{8,24},{12,28},{16,0},{20,4},{24,8},{28,12},{1,17},{... | collective-permute-start | bytes 208904 | tf_op jit(solution)/shard_map/ppermute | solution.py:27
  33.8 2.6 %collective-permute-done.5.rest_1_ = s16[272,128]{1,0:T(8,128)(2,1)S(1)} collective-permute-done((s16[272,128]{1,0:T(8,128)(2,1)S(1)}, s16[272,128]{1,0:T(8,128)(2,1)S(1)}, u32[]{:S(2)}, u32[]{:S(2)}) %collective-permute-start.5) | collective-permute-done | bytes 69664 | tf_op jit(solution)/shard_map/ppermute | solution.py:27
  36.4 3.2 %collective-permute-done.6.rest_2_ = s16[272,128]{1,0:T(8,128)(2,1)S(1)} collective-permute-done((s16[272,128]{1,0:T(8,128)(2,1)S(1)}, s16[272,128]{1,0:T(8,128)(2,1)S(1)}, u32[]{:S(2)}, u32[]{:S(2)}) %collective-permute-start.6) | collective-permute-done | bytes 69664 | tf_op jit(solution)/shard_map/ppermute | solution.py:27
  39.6 1.0 %combine.1.rest_0_ = s16[272,128]{1,0:T(8,128)(2,1)S(1)} custom-call(s32[2]{0:T(128)S(1)} %pad_add_fusion.ids, f32[16,128,128]{2,1,0:T(8,128)S(1)} %copy-done.2, f32[2,128,128]{2,1,0:T(8,128)S(1)} %get-tuple-element.23.own, s16[272,128]{1,0:T(8,128)(2,1)S(1)} %collective-permute-done.4.rest_0_, s16[272,128]{1,0:T(8,128)(2,1)S(1)} %collective-permute-done.5.rest_1_, ...), custom_call_target="tpu_custom_call" | custom-call | bytes 1048576 | tf_op jit(solution)/shard_map/combine/pallas_call | solution.py:514
  41.2 3.0 %collective-permute-start.7 = (s16[272,128]{1,0:T(8,128)(2,1)S(1)}, s16[272,128]{1,0:T(8,128)(2,1)S(1)}, u32[]{:S(2)}, u32[]{:S(2)}) collective-permute-start(s16[272,128]{1,0:T(8,128)(2,1)S(1)} %combine.1.rest_0_), channel_id=1, source_target_pairs={{0,8},{4,12},{8,0},{12,4},{16,24},{20,28},{24,16},{28,20},{1,9},{5... | collective-permute-start | bytes 208904 | tf_op jit(solution)/shard_map/ppermute | solution.py:27
  44.3 4.6 %collective-permute-start.10 = (s16[272,128]{1,0:T(8,128)(2,1)S(1)}, s16[272,128]{1,0:T(8,128)(2,1)S(1)}, u32[]{:S(2)}, u32[]{:S(2)}) collective-permute-start(s16[272,128]{1,0:T(8,128)(2,1)S(1)} %combine.1.rest_0_), channel_id=1, source_target_pairs={{0,4},{4,0},{8,12},{12,8},{16,20},{20,16},{24,28},{28,24},{1,5},{5... | collective-permute-start | bytes 208904 | tf_op jit(solution)/shard_map/ppermute | solution.py:22
  48.8 1.8 %collective-permute-start.13 = (s16[272,128]{1,0:T(8,128)(2,1)S(1)}, s16[272,128]{1,0:T(8,128)(2,1)S(1)}, u32[]{:S(2)}, u32[]{:S(2)}) collective-permute-start(s16[272,128]{1,0:T(8,128)(2,1)S(1)} %collective-permute-done.9.rest_3_), channel_id=1, source_target_pairs={{0,4},{4,0},{8,12},{12,8},{16,20},{20,16},{24,28},{28,24},{1,5},{5... | collective-permute-start | bytes 208904 | tf_op jit(solution)/shard_map/ppermute | solution.py:22
  50.7 1.2 %collective-permute-start.12 = (s16[272,128]{1,0:T(8,128)(2,1)S(1)}, s16[272,128]{1,0:T(8,128)(2,1)S(1)}, u32[]{:S(2)}, u32[]{:S(2)}) collective-permute-start(s16[272,128]{1,0:T(8,128)(2,1)S(1)} %collective-permute-done.8.rest_2_), channel_id=1, source_target_pairs={{0,4},{4,0},{8,12},{12,8},{16,20},{20,16},{24,28},{28,24},{1,5},{5... | collective-permute-start | bytes 208904 | tf_op jit(solution)/shard_map/ppermute | solution.py:22
  51.9 0.9 %collective-permute-done.12.rest_6_ = s16[272,128]{1,0:T(8,128)(2,1)S(1)} collective-permute-done((s16[272,128]{1,0:T(8,128)(2,1)S(1)}, s16[272,128]{1,0:T(8,128)(2,1)S(1)}, u32[]{:S(2)}, u32[]{:S(2)}) %collective-permute-start.12) | collective-permute-done | bytes 69664 | tf_op jit(solution)/shard_map/ppermute | solution.py:22
  53.1 1.7 %gather.1 = f32[16,128,128]{2,1,0:T(8,128)} custom-call(s32[2]{0:T(128)S(1)} %pad_add_fusion.ids, s16[272,128]{1,0:T(8,128)(2,1)S(1)} %combine.1.rest_0_, s16[272,128]{1,0:T(8,128)(2,1)S(1)} %collective-permute-done.7.rest_1_, s16[272,128]{1,0:T(8,128)(2,1)S(1)} %collective-permute-done.8.rest_2_, s16[272,128]{1,0:T(8,128)(2,1)S(1)} %collective-permute-done.9.rest_3_, ...), custom_call_target="tpu_custom_call" | custom-call | bytes 1048576 | tf_op jit(solution)/shard_map/gather/pallas_call | solution.py:523
  (25 shorter events, 2.2 us)
Async XLA Ops:
  0.1 1.2 %copy-start = (f32[16,128,128]{2,1,0:T(8,128)S(1)}, f32[16,128,128]{2,1,0:T(8,128)}, u32[]{:S(2)}) copy-start(f32[16,128,128]{2,1,0:T(8,128)} %est.5) | copy-start | bytes 3145732
  1.3 1.0 %copy-start.3 = (bf16[1,16,128,128]{3,2,1,0:T(8,128)(2,1)S(1)}, bf16[1,16,128,128]{3,2,1,0:T(8,128)(2,1)}, u32[]{:S(2)}) copy-start(bf16[1,16,128,128]{3,2,1,0:T(8,128)(2,1)} %img_own.1) | copy-start | bytes 1572868
  2.3 12.6 %copy-start.4 = (bf16[1,16,128,128]{3,2,1,0:T(8,128)(2,1)S(1)}, bf16[1,16,128,128]{3,2,1,0:T(8,128)(2,1)}, u32[]{:S(2)}) copy-start(bf16[1,16,128,128]{3,2,1,0:T(8,128)(2,1)} %img_own.1) | copy-start | bytes 1572868
  3.0 11.9 %collective-permute-start.1 = (bf16[8,128,128]{2,1,0:T(8,128)(2,1)S(1)}, bf16[8,128,128]{2,1,0:T(8,128)(2,1)S(1)}, u32[]{:S(2)}, u32[]{:S(2)}) collective-permute-start(bf16[8,128,128]{2,1,0:T(8,128)(2,1)S(1)} %get-tuple-element.17), channel_id=1, source_target_pairs={{0,4},{4,0},{8,12},{12,8},{16,20},{20,16},{24,28},{28,24},{1,5},{5... | collective-permute-start | bytes 786440 | tf_op jit(solution)/shard_map/ppermute | solution.py:22
  3.7 11.2 %collective-permute-start = (bf16[4,128,128]{2,1,0:T(8,128)(2,1)S(1)}, bf16[4,128,128]{2,1,0:T(8,128)(2,1)S(1)}, u32[]{:S(2)}, u32[]{:S(2)}) collective-permute-start(bf16[4,128,128]{2,1,0:T(8,128)(2,1)S(1)} %get-tuple-element.16), channel_id=1, source_target_pairs={{4,1},{1,4},{5,2},{2,5},{6,3},{3,6},{12,9},{9,12},{13,10},{10,13},... | collective-permute-start | bytes 393224 | tf_op jit(solution)/shard_map/ppermute | solution.py:38
  8.5 1.2 %copy-start.1 = (f32[16,128,128]{2,1,0:T(8,128)S(1)}, f32[16,128,128]{2,1,0:T(8,128)}, u32[]{:S(2)}) copy-start(f32[16,128,128]{2,1,0:T(8,128)} %est.5) | copy-start | bytes 3145732
  19.5 2.6 %collective-permute-start.3 = (bf16[2,4,96,128]{3,2,1,0:T(8,128)(2,1)S(1)}, bf16[2,4,96,128]{3,2,1,0:T(8,128)(2,1)S(1)}, u32[]{:S(2)}, u32[]{:S(2)}) collective-permute-start(bf16[2,4,96,128]{3,2,1,0:T(8,128)(2,1)S(1)} %get-tuple-element.22), channel_id=1, source_target_pairs={{0,4},{4,0},{8,12},{12,8},{16,20},{20,16},{24,28},{28,24},{1,5},{5... | collective-permute-start | bytes 589832 | tf_op jit(solution)/shard_map/ppermute | solution.py:22
  20.0 8.0 %collective-permute-start.2 = (bf16[2,4,128,128]{3,2,1,0:T(8,128)(2,1)S(1)}, bf16[2,4,128,128]{3,2,1,0:T(8,128)(2,1)S(1)}, u32[]{:S(2)}, u32[]{:S(2)}) collective-permute-start(bf16[2,4,128,128]{3,2,1,0:T(8,128)(2,1)S(1)} %get-tuple-element.20), channel_id=1, source_target_pairs={{4,1},{1,4},{5,2},{2,5},{6,3},{3,6},{12,9},{9,12},{13,10},{10,13},... | collective-permute-start | bytes 786440 | tf_op jit(solution)/shard_map/ppermute | solution.py:38
  25.8 13.8 %copy-start.2 = (f32[16,128,128]{2,1,0:T(8,128)S(1)}, f32[16,128,128]{2,1,0:T(8,128)}, u32[]{:S(2)}) copy-start(f32[16,128,128]{2,1,0:T(8,128)} %est.5) | copy-start | bytes 3145732
  30.1 3.7 %collective-permute-start.4 = (s16[272,128]{1,0:T(8,128)(2,1)S(1)}, s16[272,128]{1,0:T(8,128)(2,1)S(1)}, u32[]{:S(2)}, u32[]{:S(2)}) collective-permute-start(s16[272,128]{1,0:T(8,128)(2,1)S(1)} %get-tuple-element.24), channel_id=1, source_target_pairs={{0,8},{4,12},{8,0},{12,4},{16,24},{20,28},{24,16},{28,20},{1,9},{5... | collective-permute-start | bytes 208904 | tf_op jit(solution)/shard_map/ppermute | solution.py:27
  31.5 4.9 %collective-permute-start.5 = (s16[272,128]{1,0:T(8,128)(2,1)S(1)}, s16[272,128]{1,0:T(8,128)(2,1)S(1)}, u32[]{:S(2)}, u32[]{:S(2)}) collective-permute-start(s16[272,128]{1,0:T(8,128)(2,1)S(1)} %get-tuple-element.25), channel_id=1, source_target_pairs={{0,16},{4,20},{8,24},{12,28},{16,0},{20,4},{24,8},{28,12},{1,17},{... | collective-permute-start | bytes 208904 | tf_op jit(solution)/shard_map/ppermute | solution.py:27
  33.8 5.8 %collective-permute-start.6 = (s16[272,128]{1,0:T(8,128)(2,1)S(1)}, s16[272,128]{1,0:T(8,128)(2,1)S(1)}, u32[]{:S(2)}, u32[]{:S(2)}) collective-permute-start(s16[272,128]{1,0:T(8,128)(2,1)S(1)} %get-tuple-element.26), channel_id=1, source_target_pairs={{0,24},{4,28},{8,16},{12,20},{16,8},{20,12},{24,0},{28,4},{1,25},{... | collective-permute-start | bytes 208904 | tf_op jit(solution)/shard_map/ppermute | solution.py:27
  40.6 8.2 %collective-permute-start.9 = (s16[272,128]{1,0:T(8,128)(2,1)S(1)}, s16[272,128]{1,0:T(8,128)(2,1)S(1)}, u32[]{:S(2)}, u32[]{:S(2)}) collective-permute-start(s16[272,128]{1,0:T(8,128)(2,1)S(1)} %combine.1.rest_0_), channel_id=1, source_target_pairs={{0,24},{4,28},{8,16},{12,20},{16,8},{20,12},{24,0},{28,4},{1,25},{... | collective-permute-start | bytes 208904 | tf_op jit(solution)/shard_map/ppermute | solution.py:27
  41.2 9.5 %collective-permute-start.8 = (s16[272,128]{1,0:T(8,128)(2,1)S(1)}, s16[272,128]{1,0:T(8,128)(2,1)S(1)}, u32[]{:S(2)}, u32[]{:S(2)}) collective-permute-start(s16[272,128]{1,0:T(8,128)(2,1)S(1)} %combine.1.rest_0_), channel_id=1, source_target_pairs={{0,16},{4,20},{8,24},{12,28},{16,0},{20,4},{24,8},{28,12},{1,17},{... | collective-permute-start | bytes 208904 | tf_op jit(solution)/shard_map/ppermute | solution.py:27
  41.2 10.7 %collective-permute-start.7 = (s16[272,128]{1,0:T(8,128)(2,1)S(1)}, s16[272,128]{1,0:T(8,128)(2,1)S(1)}, u32[]{:S(2)}, u32[]{:S(2)}) collective-permute-start(s16[272,128]{1,0:T(8,128)(2,1)S(1)} %combine.1.rest_0_), channel_id=1, source_target_pairs={{0,8},{4,12},{8,0},{12,4},{16,24},{20,28},{24,16},{28,20},{1,9},{5... | collective-permute-start | bytes 208904 | tf_op jit(solution)/shard_map/ppermute | solution.py:27
  44.3 7.6 %collective-permute-start.10 = (s16[272,128]{1,0:T(8,128)(2,1)S(1)}, s16[272,128]{1,0:T(8,128)(2,1)S(1)}, u32[]{:S(2)}, u32[]{:S(2)}) collective-permute-start(s16[272,128]{1,0:T(8,128)(2,1)S(1)} %combine.1.rest_0_), channel_id=1, source_target_pairs={{0,4},{4,0},{8,12},{12,8},{16,20},{20,16},{24,28},{28,24},{1,5},{5... | collective-permute-start | bytes 208904 | tf_op jit(solution)/shard_map/ppermute | solution.py:22
  48.8 3.1 %collective-permute-start.13 = (s16[272,128]{1,0:T(8,128)(2,1)S(1)}, s16[272,128]{1,0:T(8,128)(2,1)S(1)}, u32[]{:S(2)}, u32[]{:S(2)}) collective-permute-start(s16[272,128]{1,0:T(8,128)(2,1)S(1)} %collective-permute-done.9.rest_3_), channel_id=1, source_target_pairs={{0,4},{4,0},{8,12},{12,8},{16,20},{20,16},{24,28},{28,24},{1,5},{5... | collective-permute-start | bytes 208904 | tf_op jit(solution)/shard_map/ppermute | solution.py:22
  50.7 2.1 %collective-permute-start.12 = (s16[272,128]{1,0:T(8,128)(2,1)S(1)}, s16[272,128]{1,0:T(8,128)(2,1)S(1)}, u32[]{:S(2)}, u32[]{:S(2)}) collective-permute-start(s16[272,128]{1,0:T(8,128)(2,1)S(1)} %collective-permute-done.8.rest_2_), channel_id=1, source_target_pairs={{0,4},{4,0},{8,12},{12,8},{16,20},{20,16},{24,28},{28,24},{1,5},{5... | collective-permute-start | bytes 208904 | tf_op jit(solution)/shard_map/ppermute | solution.py:22
  51.9 1.3 %collective-permute-start.11 = (s16[272,128]{1,0:T(8,128)(2,1)S(1)}, s16[272,128]{1,0:T(8,128)(2,1)S(1)}, u32[]{:S(2)}, u32[]{:S(2)}) collective-permute-start(s16[272,128]{1,0:T(8,128)(2,1)S(1)} %collective-permute-done.7.rest_1_), channel_id=1, source_target_pairs={{0,4},{4,0},{8,12},{12,8},{16,20},{20,16},{24,28},{28,24},{1,5},{5... | collective-permute-start | bytes 208904 | tf_op jit(solution)/shard_map/ppermute | solution.py:22

commit v4 on v3

--- a/solution.py
+++ b/solution.py
@@ -10,6 +10,7 @@
 CAP = 3
 LANES = 128
 PAD = 8
+MARKS = 2
 HEADER = 16
 MARK = 256.0
 LEVEL = 32767.0
@@ -64,19 +65,24 @@
     return cells * step + middle
 
 
-def window_of(cov, view, blocks, window):
+def is_covered(info, j, block):
+    return ((info[MARKS + j] >> block) & 1) > 0
+
+
+def window_of(info, j, blocks, window):
     first = jnp.int32(blocks - window)
     for block in range(blocks - window - 1, -1, -1):
-        first = jnp.where(cov[view, 0, block] > 0, jnp.int32(block), first)
+        first = jnp.where(is_covered(info, j, block), jnp.int32(block), first)
     return first
 
 
-def window_mask(cov, view, first, window, block_width):
+def window_mask(info, j, first, window, block_width):
     row = lax.broadcasted_iota(jnp.int32, (window * block_width, LANES), 0)
     mask = jnp.zeros(row.shape, jnp.int32)
     for block in range(window):
         inside = (row >= block * block_width) & (row < (block + 1) * block_width)
-        mask = jnp.where(inside, cov[view, 0, first + block], mask)
+        here = jnp.where(is_covered(info, j, first + block), 1, 0)
+        mask = jnp.where(inside, here, mask)
     return mask > 0
 
 
@@ -84,28 +90,31 @@
     return jnp.where(core == 0, row, last - row)
 
 
-def payload_kernel(ids, est, images, edge, given, rows, sems):
+def payload_kernel(ids, cov, spread, est, edge, cov_here, spread_here, rows, sems):
     core = ids[0]
     rim = edge.shape[0]
-    half = given.shape[0]
-    copy_rows = pltpu.make_async_copy(
-        est.at[pl.ds((est.shape[0] - rim) * core, rim)], rows, sems.at[0]
-    )
-    copy_given = pltpu.make_async_copy(
-        images.at[0, pl.ds(half * (1 - core), half)], given, sems.at[1]
-    )
-    copy_rows.start()
-    copy_given.start()
-    copy_rows.wait()
+    far_rows = est.at[pl.ds((est.shape[0] - rim) * core, rim)]
+    copies = [
+        pltpu.make_async_copy(far_rows, rows, sems.at[0]),
+        pltpu.make_async_copy(spread, spread_here, sems.at[1]),
+        pltpu.make_async_copy(cov, cov_here, sems.at[2]),
+    ]
+    for copy in copies:
+        copy.start()
+    copies[0].wait()
     edge[...] = rows[...].astype(edge.dtype)
-    copy_given.wait()
-
-
-def tables_kernel(ids, spread, est, table, cols, rows, pad, sems, *, taps):
+    for copy in copies[1:]:
+        copy.wait()
+
+
+def tables_kernel(
+    ids, cov, spread, est, images, table, cols, info, img_own, est_own, rows, pad, sems, *, taps
+):
     taps_x, taps_y, taps_z = taps
     core, chip = ids[0], ids[1]
     rim_z = (taps_z - 1) // 2
     depth = LANES
+    views = table.shape[0]
     count, width = cols.shape[0], cols.shape[1]
     margin = jnp.zeros((count, PAD, depth), jnp.float32)
     pad[:, :PAD, :] = margin
@@ -116,6 +125,10 @@
         )
         for i in range(count)
     ]
+    half = img_own.shape[0]
+    copies.append(
+        pltpu.make_async_copy(images.at[0, pl.ds(half * core, half)], img_own, sems.at[count])
+    )
     for copy in copies:
         copy.start()
     row = lax.broadcasted_iota(jnp.int32, (depth, depth), 0)
@@ -124,29 +137,43 @@
     at = row - rim_z
     place = ((col == at) | (col == at + depth)) & (row < taps_z)
     place = jnp.where(place, 1.0, 0.0).astype(jnp.bfloat16)
-    for j in range(table.shape[0]):
-        taps_all = spread[chip * table.shape[0] + j]
-        kernel = (taps_all / jnp.sum(taps_all)).astype(jnp.bfloat16)
-        kernel = kernel.reshape(-1, LANES)
-        rows[...] = jnp.dot(kernel, place, preferred_element_type=jnp.float32)
-        zero = jnp.zeros((taps_y * depth, depth), jnp.bfloat16)
+    zero = jnp.zeros((taps_y * depth, depth), jnp.bfloat16)
+    rows[...] = jnp.zeros(rows.shape, jnp.float32)
+    total_views = spread.shape[0] // (taps_x * taps_y)
+    info[0] = core
+    info[1] = chip
+    block = lax.broadcasted_iota(jnp.int32, cov.shape, 0)
+    lane = lax.broadcasted_iota(jnp.int32, cov.shape, 1)
+    bits = jnp.where(cov[...] != 0, jnp.left_shift(1, block), 0)
+    for j in range(views):
+        view = chip * views + j
+        code = jnp.sum(jnp.where(lane == view, bits, 0).astype(jnp.float32))
+        info[MARKS + j] = code.astype(jnp.int32)
         table[j, 0] = zero
         table[j, taps_x + 1] = zero
-
-        def fill(a, carry):
-            at_x = canonical(1 - core, a, taps_x - 1) * 8
+        taps_all = spread[pl.ds(view, taps_x * taps_y, stride=total_views), :]
+        rows[j, : taps_x * taps_y, :taps_z] = taps_all
+        weights = rows[j]
+        kernel = (weights / jnp.sum(weights)).astype(jnp.bfloat16)
+        rows[j] = jnp.dot(kernel, place, preferred_element_type=jnp.float32)
+
+    def fill(a, carry):
+        at_x = canonical(1 - core, a, taps_x - 1)
+        for j in range(views):
             for b in range(taps_y):
-                line = rows[pl.ds(at_x + (taps_y - 1 - b), 1), :]
+                line = rows[j, pl.ds(at_x * taps_y + taps_y - 1 - b, 1), :]
                 line = jnp.broadcast_to(line, (depth, depth))
                 line = pltpu.roll(line, 0, 1, stride=1, stride_axis=0)
                 line = jnp.where(band, line, 0.0).astype(jnp.bfloat16)
                 table[j, a + 1, b * depth : (b + 1) * depth, :] = line
-            return carry
-
-        lax.fori_loop(0, taps_x, fill, 0)
+        return carry
+
+    lax.fori_loop(0, taps_x, fill, 0, unroll=3)
     for copy in copies:
         copy.wait()
     fill_columns(pad, cols, taps_y, width)
+    for r in range(est_own.shape[0]):
+        est_own[r] = pad[chip * est_own.shape[0] + r, PAD : PAD + width, :]
 
 
 def fill_columns(pad, cols, taps_y, rows_y):
@@ -191,15 +218,14 @@
 
 
 def blur_kernel(
-    ids, cov, halo, img_own, img_other, cols, table, quot, remote, near, pad, edge, image, sems, *, taps
+    info, halo, img_own, img_other, cols, table, quot, remote, near, pad, edge, image, sems, *, taps, blocks
 ):
-    core, chip = ids[0], ids[1]
+    core, chip = info[0], info[1]
     views, half, rows_y, depth = quot.shape
     rim, width, _ = halo.shape
-    blocks = cov.shape[2]
     block_width = width // blocks
     window = rows_y // block_width
-    share_w = img_own.shape[2]
+    share_w = img_own.shape[1]
     if views == 1:
         own_at = pl.multiple_of(core * share_w, share_w)
         other_at = pl.multiple_of((1 - core) * share_w, share_w)
@@ -209,8 +235,8 @@
         own_to = image.at[core]
         other_to = image.at[1 - core]
     copies = [
-        pltpu.make_async_copy(img_own.at[0, pl.ds(half * core, half)], own_to, sems.at[0]),
-        pltpu.make_async_copy(img_other, other_to, sems.at[1]),
+        pltpu.make_async_copy(img_own, own_to, sems.at[0]),
+        pltpu.make_async_copy(img_other.at[pl.ds(half * core, half)], other_to, sems.at[1]),
     ]
     for copy in copies:
         copy.start()
@@ -223,9 +249,8 @@
     for copy in copies:
         copy.wait()
     for j in range(views):
-        view = chip * views + j
-        first = window_of(cov, view, blocks, window)
-        mask = window_mask(cov, view, first, window, block_width)
+        first = window_of(info, j, blocks, window)
+        mask = window_mask(info, j, first, window, block_width)
         y_start = pl.multiple_of(first * block_width, block_width)
 
         def slab(x):
@@ -241,7 +266,7 @@
                 preferred_element_type=jnp.float32,
             )
             blurred = part if blurred is None else blurred + part
-        remote[j] = jnp.zeros(remote.shape[1:], remote.dtype)
+        remote[j, :HEADER, :] = jnp.full((HEADER, depth), first, jnp.int32).astype(jnp.bfloat16)
         for r in range(half):
             cells = image[j, canonical(core, r, half - 1), pl.ds(y_start, rows_y), :]
             i, w = r // 2, r % 2
@@ -249,7 +274,8 @@
             ratio = jnp.where(mask, cells.astype(jnp.float32) / below, 0.0).astype(jnp.bfloat16)
             quot[j, r] = ratio
             if r < rim:
-                remote[j, r, pl.ds(y_start, rows_y), :] = ratio
+                low = HEADER + r * rows_y
+                remote[j, low : low + rows_y, :] = ratio
             else:
                 near[j, r - rim] = ratio
 
@@ -286,26 +312,27 @@
         sums[j] = total
 
 
-def correct_kernel(ids, cov, remote, sums, table, *rest, taps):
+def correct_kernel(info, remote, sums, table, est_own, *rest, taps, blocks):
     *pieces, pad, cols, far, product, logs = rest
-    chip = ids[1]
-    views, rim, width, depth = remote.shape
-    half = product.shape[0]
-    rows_y = cols.shape[2]
-    blocks = cov.shape[2]
+    chip = info[1]
+    views, rim, rows_y, _ = cols.shape
+    half, width, depth = product.shape
     block_width = width // blocks
     window = rows_y // block_width
+    rows = half // len(pieces)
     product[...] = jnp.ones(product.shape, jnp.float32)
-    margin = jnp.zeros((rim, PAD, depth), jnp.float32)
+    far[...] = jnp.zeros(far.shape, jnp.float32)
     for j in range(views):
-        view = chip * views + j
-        first = window_of(cov, view, blocks, window)
-        mask = window_mask(cov, view, first, window, block_width)
+        first = window_of(info, j, blocks, window)
+        mask = window_mask(info, j, first, window, block_width)
         y_start = pl.multiple_of(first * block_width, block_width)
-        far[j, :, :PAD, :] = margin
-        far[j, :, PAD + width :, :] = margin
+        there = jnp.max(remote[j, :HEADER, :].astype(jnp.float32)).astype(jnp.int32)
+        there = jnp.clip(there, 0, blocks - window)
+        y_there = pl.multiple_of(there * block_width, block_width)
         for r in range(rim):
-            far[j, rim - 1 - r, PAD : PAD + width, :] = remote[j, r].astype(jnp.float32)
+            low = HEADER + r * rows_y
+            cells = remote[j, low : low + rows_y, :].astype(jnp.float32)
+            far[j, rim - 1 - r, pl.ds(PAD + y_there, rows_y), :] = cells
         for r in range(rim):
             pad[j, r] = far[j, r, pl.ds(y_start, rows_y + 2 * PAD), :]
         fill_columns(pad.at[j], cols.at[j], taps[1], rows_y)
@@ -328,7 +355,6 @@
             factor = jnp.where(mask, cells, 1.0)
             at = (r, pl.ds(y_start, rows_y), slice(None))
             product[at] = product[at] * factor
-    rows = half // len(pieces)
     least = jnp.full((width, depth), jnp.inf, jnp.float32)
     most = -least
     for r in range(half):
@@ -338,7 +364,7 @@
         most = jnp.maximum(most, cells)
     header, low, scale = code_header(jnp.min(least), jnp.max(most))
     for r in range(rows):
-        pieces[0][r] = product[chip * rows + r]
+        pieces[0][r] = est_own[r] * product[chip * rows + r]
     for step in range(1, len(pieces)):
         pieces[step][:HEADER, :] = header
         for r in range(rows):
@@ -346,24 +372,13 @@
             pieces[step][at : at + width, :] = encode(logs[(chip ^ step) * rows + r], low, scale)
 
 
-def combine_kernel(ids, est, own, *rest):
-    *pieces, out, held, sems = rest
-    core, chip = ids[0], ids[1]
+def combine_kernel(own, *rest):
+    *pieces, out = rest
     rows, width, _ = own.shape
-    copies = [
-        pltpu.make_async_copy(
-            est.at[canonical(core, chip * rows + r, est.shape[0] - 1)], held.at[r], sems.at[r]
-        )
-        for r in range(rows)
-    ]
-    for copy in copies:
-        copy.start()
     marks = [code_marks(piece) for piece in pieces]
-    for copy in copies:
-        copy.wait()
     all_logs = []
     for r in range(rows):
-        logs = jnp.log(held[r] * own[r])
+        logs = jnp.log(own[r])
         for piece, mark in zip(pieces, marks):
             logs = logs + decode(piece, mark, HEADER + r * width, width)
         all_logs.append(logs)
@@ -378,21 +393,28 @@
 
 
 def gather_kernel(ids, *rest):
-    *pieces, out = rest
+    *pieces, out, cells, sems = rest
     core, chip = ids[0], ids[1]
     count = len(pieces) // 2
     slab_x, width, _ = out.shape
     rows = slab_x // 2 // count
+    stores = []
     for place, piece in enumerate(pieces):
         side = core if place < count else 1 - core
         marks = code_marks(piece)
         for r in range(rows):
             at = canonical(side, (chip ^ (place % count)) * rows + r, slab_x - 1)
-            out[at] = jnp.exp(decode(piece, marks, HEADER + r * width, width))
+            slot = place * rows + r
+            cells[slot] = jnp.exp(decode(piece, marks, HEADER + r * width, width))
+            store = pltpu.make_async_copy(cells.at[slot], out.at[at], sems.at[slot])
+            store.start()
+            stores.append(store)
+    for store in stores:
+        store.wait()
 
 
 def call(kernel, name, outs, kinds, scratch=(), flops=0, out_kinds=None):
-    spaces = {"s": pltpu.SMEM, "v": pltpu.VMEM, "a": pl.ANY}
+    spaces = {"s": pltpu.SMEM, "v": pltpu.VMEM, "h": pltpu.HBM}
     many = isinstance(outs, tuple)
     out_kinds = out_kinds or "v" * (len(outs) if many else 1)
     out_specs = tuple(pl.BlockSpec(memory_space=spaces[kind]) for kind in out_kinds)
@@ -426,6 +448,7 @@
     core, chip = group % 2, group // 2
     ids = jnp.stack([core, chip]).astype(jnp.int32)
     inner = half + rim
+    rows = half // chips
     f32, bf16 = jnp.float32, jnp.bfloat16
     shape = jax.ShapeDtypeStruct
     deep = taps_y * depth
@@ -434,43 +457,55 @@
     sems = pltpu.SemaphoreType.DMA
     work = 2 * half * rows_y * depth * taps_x * taps_y * depth * views
 
-    edge, given = call(
+    img_other = swap_cores(images[0])
+    estimate = pltpu.with_memory_space_constraint(estimate, pltpu.HBM)
+    images = pltpu.with_memory_space_constraint(images, pltpu.HBM)
+    spread = jnp.transpose(point_spread, (1, 2, 0, 3)).reshape(-1, taps_z)
+    spread = pltpu.with_memory_space_constraint(spread, pltpu.HBM)
+    cov = pltpu.with_memory_space_constraint(jnp.transpose(covered[:, 0, :]), pltpu.HBM)
+
+    edge, cov, spread = call(
         payload_kernel,
         "payload",
-        (shape((rim, width, depth), bf16), shape((half, share_w, depth), bf16)),
-        "saa",
-        [pltpu.VMEM((rim, width, depth), f32), sems((2,))],
-        out_kinds="va",
-    )(ids, estimate, images)
+        (
+            shape((rim, width, depth), bf16),
+            pltpu.VMEM(cov.shape, jnp.int32),
+            pltpu.VMEM(spread.shape, f32),
+        ),
+        "shhh",
+        [pltpu.VMEM((rim, width, depth), f32), sems((3,))],
+    )(ids, cov, spread, estimate)
     halo = swap_layers(edge)
-    img_other = swap_cores(given)
-
-    spread = jnp.pad(point_spread, ((0, 0), (0, 0), (0, 8 - taps_y), (0, depth - taps_z)))
-    table, cols = call(
+
+    table, cols, info, img_own, est_own = call(
         functools.partial(tables_kernel, taps=taps),
         "tables",
         (
             pltpu.VMEM((views, taps_x + 2, deep, depth), bf16),
             pltpu.VMEM((inner, width, deep), bf16),
+            shape((MARKS + views,), jnp.int32),
+            pltpu.VMEM((half, share_w, depth), bf16),
+            pltpu.VMEM((rows, width, depth), f32),
         ),
-        "sva",
+        "svvhh",
         [
-            pltpu.VMEM((taps_x * 8, depth), f32),
+            pltpu.VMEM((views, -(-taps_x * taps_y // 8) * 8, depth), f32),
             pltpu.VMEM((inner, wide, depth), f32),
-            sems((inner,)),
+            sems((inner + 1,)),
         ],
         work // 2,
-    )(ids, spread, estimate)
+        "vvsvv",
+    )(ids, cov, spread, estimate, images)
 
     quot, remote, near = call(
-        functools.partial(blur_kernel, taps=taps),
+        functools.partial(blur_kernel, taps=taps, blocks=blocks),
         "blur",
         (
             pltpu.VMEM((views, half, rows_y, depth), bf16),
-            shape((views, rim, width, depth), bf16),
+            shape((views, HEADER + rim * rows_y, depth), bf16),
             shape((views, rim, rows_y, depth), bf16),
         ),
-        "ssvaavv",
+        "svvvvv",
         [
             pltpu.VMEM((rim, wide, depth), f32),
             pltpu.VMEM((rim, width, deep), bf16),
@@ -478,7 +513,7 @@
             sems((2,)),
         ],
         work,
-    )(ids, covered, halo, images, img_other, cols, table)
+    )(info, halo, img_own, img_other, cols, table)
     near = swap_cores(near)
     remote = swap_layers(remote)
 
@@ -494,13 +529,12 @@
         work,
     )(quot, near, table)
 
-    rows = half // chips
     coded = shape((HEADER + rows * width, depth), jnp.int16)
     pieces = call(
-        functools.partial(correct_kernel, taps=taps),
+        functools.partial(correct_kernel, taps=taps, blocks=blocks),
         "correct",
-        (shape((rows, width, depth), f32),) + (coded,) * (chips - 1),
-        "ssvvv",
+        (pltpu.VMEM((rows, width, depth), f32),) + (coded,) * (chips - 1),
+        "svvvv",
         [
             pltpu.VMEM((views, rim, tall, depth), f32),
             pltpu.VMEM((views, rim, rows_y, deep), bf16),
@@ -509,15 +543,14 @@
             pltpu.VMEM((half, width, depth), f32),
         ],
         work // 4,
-    )(ids, covered, remote, sums, table)
+    )(info, remote, sums, table, est_own)
     arrived = [pieces[0]] + [swap_chips(pieces[step], step) for step in range(1, chips)]
     mine = call(
         combine_kernel,
         "combine",
         coded,
-        "sa" + "v" * chips,
-        [pltpu.VMEM((rows, width, depth), f32), sems((rows,))],
-    )(ids, estimate, *arrived)
+        "v" * chips,
+    )(*arrived)
     column = [mine] + [swap_chips(mine, step) for step in range(1, chips)]
     across = [swap_cores(piece) for piece in column]
     return call(
@@ -525,6 +558,8 @@
         "gather",
         shape(estimate.shape, f32),
         "s" + "v" * (2 * chips),
+        [pltpu.VMEM(estimate.shape, f32), sems((slab_x,))],
+        out_kinds="h",
     )(ids, *column, *across)
 
 

time: 55.2 us -> 48.5 us (0.88)
  the two profiles are of different devices: /device:TPU:5 before, /device:TPU:3 now
where the time goes in v4:
time: 48.5 us; the launch traced here: 48.4 us
  starting transfers between devices  18 us (37%)
  Pallas kernels  16.6 us (34%)
  waiting for transfers between devices  13.7 us (28%)
    ppermute x6, waiting for transfers between devices, swap_chips(): lax.ppermute(cells, 'view', [(i, i ^ 2 * step) for i in range(count)])  7.99 us
    ppermute x6, starting transfers between devices, swap_chips(): lax.ppermute(cells, 'view', [(i, i ^ 2 * step) for i in range(count)])  7.39 us
    ppermute x2, starting transfers between devices, swap_layers(): return lax.ppermute(cells, ('view', 'blk'), route)  5.75 us
    ppermute x6, starting transfers between devices, swap_cores(): return lax.ppermute(cells, 'view', [(i, i ^ 1) for i in range(count)])  4.83 us
    pallas_call x1, Pallas kernels, local(): call(functools.partial(blur_kernel, taps=taps, blocks=blocks), 'blur', (p...  4.5 us
    ppermute x2, waiting for transfers between devices, swap_layers(): return lax.ppermute(cells, ('view', 'blk'), route)  4.41 us
    pallas_call x1, Pallas kernels, local(): call(functools.partial(inner_kernel, taps=taps), 'inner', pltpu.VMEM((vie...  3.6 us
    pallas_call x1, Pallas kernels, local(): call(functools.partial(tables_kernel, taps=taps), 'tables', (pltpu.VMEM((...  2.86 us
  transfers between devices with their start and end apart: 14, of which 8 were waited for; matrix products, arithmetic and copies ran while one was open for 0% of the time, Pallas kernels for 17%

profile of v4, /device:TPU:3, one launch (start us, length us, event | category | flops | bytes accessed | tf_op | source)
XLA Modules:
  0.0 48.4 jit_solution(119182953424749856)
XLA Ops:
  0.0 0.7 %collective-permute-start.1 = (bf16[16,128,128]{2,1,0:T(8,128)(2,1)}, bf16[16,128,128]{2,1,0:T(8,128)(2,1)S(1)}, u32[]{:S(2)}, u32[]{:S(2)}) collective-permute-start(bf16[16,128,128]{2,1,0:T(8,128)(2,1)} %bitcast.11), channel_id=1, source_target_pairs={{0,4},{4,0},{8,12},{12,8},{16,20},{20,16},{24,28},{28,24},{1,5},{5... | collective-permute-start | bytes 1572872 | tf_op jit(solution)/shard_map/ppermute | solution.py:23
  0.8 1.6 %payload.1 = (bf16[4,128,128]{2,1,0:T(8,128)(2,1)S(1)}, s32[4,8]{1,0:T(4,128)S(1)}, f32[504,25]{1,0:T(8,128)S(1)}) custom-call(s32[2]{0:T(128)S(1)} %pad_add_fusion.ids, s32[4,8]{1,0:T(4,128)} %bitcast.10, f32[504,25]{1,0:T(8,128)} %bitcast.9, f32[16,128,128]{2,1,0:T(8,128)} %est.3), custom_call_target="tpu_custom_call" | custom-call | bytes 1048576 | tf_op jit(solution)/shard_map/payload/pallas_call | solution.py:467
  2.4 3.0 %collective-permute-start = (bf16[4,128,128]{2,1,0:T(8,128)(2,1)S(1)}, bf16[4,128,128]{2,1,0:T(8,128)(2,1)S(1)}, u32[]{:S(2)}, u32[]{:S(2)}) collective-permute-start(bf16[4,128,128]{2,1,0:T(8,128)(2,1)S(1)} %get-tuple-element.23), channel_id=1, source_target_pairs={{4,1},{1,4},{5,2},{2,5},{6,3},{3,6},{12,9},{9,12},{13,10},{10,13},... | collective-permute-start | bytes 393224 | tf_op jit(solution)/shard_map/ppermute | solution.py:39
  5.4 2.9 %tables.1 = (bf16[2,11,896,128]{3,2,1,0:T(8,128)(2,1)S(1)}, bf16[12,128,896]{2,1,0:T(8,128)(2,1)S(1)}, s32[4]{0:T(128)S(1)}, bf16[8,128,128]{2,1,0:T(8,128)(2,1)S(1)}, f32[2,128,128]{2,1,0:T(8,128)S(1)}) custom-call(s32[2]{0:T(128)S(1)} %pad_add_fusion.ids, s32[4,8]{1,0:T(4,128)S(1)} %get-tuple-element.20.cov, f32[504,25]{1,0:T(8,128)S(1)} %get-tuple-element.21.spread, ...), custom_call_target="tpu_custom_call" | custom-call | flops 1585446912 | bytes 1048576 | tf_op jit(solution)/shard_map/tables/pallas_call | solution.py:480
  8.2 2.1 %collective-permute-done.halo = bf16[4,128,128]{2,1,0:T(8,128)(2,1)S(1)} collective-permute-done((bf16[4,128,128]{2,1,0:T(8,128)(2,1)S(1)}, bf16[4,128,128]{2,1,0:T(8,128)(2,1)S(1)}, u32[]{:S(2)}, u32[]{:S(2)}) %collective-permute-start) | collective-permute-done | bytes 131104 | tf_op jit(solution)/shard_map/ppermute | solution.py:39
  10.3 4.5 %blur.1 = (bf16[2,8,96,128]{3,2,1,0:T(8,128)(2,1)S(1)}, bf16[2,400,128]{2,1,0:T(8,128)(2,1)S(1)}, bf16[2,4,96,128]{3,2,1,0:T(8,128)(2,1)S(1)}) custom-call(s32[4]{0:T(128)S(1)} %get-tuple-element.22.info, bf16[4,128,128]{2,1,0:T(8,128)(2,1)S(1)} %collective-permute-done.halo, bf16[8,128,128]{2,1,0:T(8,128)(2,1)S(1)} %get-tuple-element.24.img_own, ...), custom_call_target="tpu_custom_call" | custom-call | flops 3170893824 | bytes 1048576 | tf_op jit(solution)/shard_map/blur/pallas_call | solution.py:500
  14.9 2.7 %collective-permute-start.2 = (bf16[2,400,128]{2,1,0:T(8,128)(2,1)S(1)}, bf16[2,400,128]{2,1,0:T(8,128)(2,1)S(1)}, u32[]{:S(2)}, u32[]{:S(2)}) collective-permute-start(bf16[2,400,128]{2,1,0:T(8,128)(2,1)S(1)} %get-tuple-element.27), channel_id=1, source_target_pairs={{4,1},{1,4},{5,2},{2,5},{6,3},{3,6},{12,9},{9,12},{13,10},{10,13},... | collective-permute-start | bytes 614408 | tf_op jit(solution)/shard_map/ppermute | solution.py:39
  17.7 3.6 %inner.1.sums = f32[2,384,256]{2,1,0:T(8,128)S(1)} custom-call(bf16[2,8,96,128]{3,2,1,0:T(8,128)(2,1)S(1)} %get-tuple-element.28.quot, bf16[2,4,96,128]{3,2,1,0:T(8,128)(2,1)S(1)} %collective-permute-done.3.near, bf16[2,11,896,128]{3,2,1,0:T(8,128)(2,1)S(1)} %get-tuple-element.26.table), custom_call_target="tpu_custom_call" | custom-call | flops 3170893824 | bytes 1048576 | tf_op jit(solution)/shard_map/inner/pallas_call | solution.py:520
  21.3 2.3 %collective-permute-done.2.remote = bf16[2,400,128]{2,1,0:T(8,128)(2,1)S(1)} collective-permute-done((bf16[2,400,128]{2,1,0:T(8,128)(2,1)S(1)}, bf16[2,400,128]{2,1,0:T(8,128)(2,1)S(1)}, u32[]{:S(2)}, u32[]{:S(2)}) %collective-permute-start.2) | collective-permute-done | bytes 204832 | tf_op jit(solution)/shard_map/ppermute | solution.py:39
  23.6 2.1 %correct.1 = (f32[2,128,128]{2,1,0:T(8,128)S(1)}, s16[272,128]{1,0:T(8,128)(2,1)S(1)}, s16[272,128]{1,0:T(8,128)(2,1)S(1)}, s16[272,128]{1,0:T(8,128)(2,1)S(1)}) custom-call(s32[4]{0:T(128)S(1)} %get-tuple-element.22.info, bf16[2,400,128]{2,1,0:T(8,128)(2,1)S(1)} %collective-permute-done.2.remote, f32[2,384,256]{2,1,0:T(8,128)S(1)} %inner.1.sums, ...), custom_call_target="tpu_custom_call" | custom-call | flops 792723456 | bytes 1048576 | tf_op jit(solution)/shard_map/correct/pallas_call | solution.py:533
  25.7 1.4 %collective-permute-start.4 = (s16[272,128]{1,0:T(8,128)(2,1)S(1)}, s16[272,128]{1,0:T(8,128)(2,1)S(1)}, u32[]{:S(2)}, u32[]{:S(2)}) collective-permute-start(s16[272,128]{1,0:T(8,128)(2,1)S(1)} %get-tuple-element.32), channel_id=1, source_target_pairs={{0,8},{4,12},{8,0},{12,4},{16,24},{20,28},{24,16},{28,20},{1,9},{5... | collective-permute-start | bytes 208904 | tf_op jit(solution)/shard_map/ppermute | solution.py:28
  27.2 2.3 %collective-permute-start.5 = (s16[272,128]{1,0:T(8,128)(2,1)S(1)}, s16[272,128]{1,0:T(8,128)(2,1)S(1)}, u32[]{:S(2)}, u32[]{:S(2)}) collective-permute-start(s16[272,128]{1,0:T(8,128)(2,1)S(1)} %get-tuple-element.33), channel_id=1, source_target_pairs={{0,16},{4,20},{8,24},{12,28},{16,0},{20,4},{24,8},{28,12},{1,17},{... | collective-permute-start | bytes 208904 | tf_op jit(solution)/shard_map/ppermute | solution.py:28
  29.5 3.8 %collective-permute-done.5.rest_1_ = s16[272,128]{1,0:T(8,128)(2,1)S(1)} collective-permute-done((s16[272,128]{1,0:T(8,128)(2,1)S(1)}, s16[272,128]{1,0:T(8,128)(2,1)S(1)}, u32[]{:S(2)}, u32[]{:S(2)}) %collective-permute-start.5) | collective-permute-done | bytes 69664 | tf_op jit(solution)/shard_map/ppermute | solution.py:28
  33.3 1.8 %collective-permute-done.6.rest_2_ = s16[272,128]{1,0:T(8,128)(2,1)S(1)} collective-permute-done((s16[272,128]{1,0:T(8,128)(2,1)S(1)}, s16[272,128]{1,0:T(8,128)(2,1)S(1)}, u32[]{:S(2)}, u32[]{:S(2)}) %collective-permute-start.6) | collective-permute-done | bytes 69664 | tf_op jit(solution)/shard_map/ppermute | solution.py:28
  35.4 2.1 %collective-permute-start.9 = (s16[272,128]{1,0:T(8,128)(2,1)S(1)}, s16[272,128]{1,0:T(8,128)(2,1)S(1)}, u32[]{:S(2)}, u32[]{:S(2)}) collective-permute-start(s16[272,128]{1,0:T(8,128)(2,1)S(1)} %combine.1.rest_0_), channel_id=1, source_target_pairs={{0,24},{4,28},{8,16},{12,20},{16,8},{20,12},{24,0},{28,4},{1,25},{... | collective-permute-start | bytes 208904 | tf_op jit(solution)/shard_map/ppermute | solution.py:28
  37.5 0.3 collective-permute-start.8
  37.8 1.2 %collective-permute-start.7 = (s16[272,128]{1,0:T(8,128)(2,1)S(1)}, s16[272,128]{1,0:T(8,128)(2,1)S(1)}, u32[]{:S(2)}, u32[]{:S(2)}) collective-permute-start(s16[272,128]{1,0:T(8,128)(2,1)S(1)} %combine.1.rest_0_), channel_id=1, source_target_pairs={{0,8},{4,12},{8,0},{12,4},{16,24},{20,28},{24,16},{28,20},{1,9},{5... | collective-permute-start | bytes 208904 | tf_op jit(solution)/shard_map/ppermute | solution.py:28
  39.0 1.3 %collective-permute-start.10 = (s16[272,128]{1,0:T(8,128)(2,1)S(1)}, s16[272,128]{1,0:T(8,128)(2,1)S(1)}, u32[]{:S(2)}, u32[]{:S(2)}) collective-permute-start(s16[272,128]{1,0:T(8,128)(2,1)S(1)} %combine.1.rest_0_), channel_id=1, source_target_pairs={{0,4},{4,0},{8,12},{12,8},{16,20},{20,16},{24,28},{28,24},{1,5},{5... | collective-permute-start | bytes 208904 | tf_op jit(solution)/shard_map/ppermute | solution.py:23
  40.5 1.9 %collective-permute-start.13 = (s16[272,128]{1,0:T(8,128)(2,1)S(1)}, s16[272,128]{1,0:T(8,128)(2,1)S(1)}, u32[]{:S(2)}, u32[]{:S(2)}) collective-permute-start(s16[272,128]{1,0:T(8,128)(2,1)S(1)} %collective-permute-done.9.rest_3_), channel_id=1, source_target_pairs={{0,4},{4,0},{8,12},{12,8},{16,20},{20,16},{24,28},{28,24},{1,5},{5... | collective-permute-start | bytes 208904 | tf_op jit(solution)/shard_map/ppermute | solution.py:23
  42.5 2.2 %collective-permute-done.8.rest_2_ = s16[272,128]{1,0:T(8,128)(2,1)S(1)} collective-permute-done((s16[272,128]{1,0:T(8,128)(2,1)S(1)}, s16[272,128]{1,0:T(8,128)(2,1)S(1)}, u32[]{:S(2)}, u32[]{:S(2)}) %collective-permute-start.8) | collective-permute-done | bytes 69664 | tf_op jit(solution)/shard_map/ppermute | solution.py:28
  44.6 0.9 %collective-permute-start.12 = (s16[272,128]{1,0:T(8,128)(2,1)S(1)}, s16[272,128]{1,0:T(8,128)(2,1)S(1)}, u32[]{:S(2)}, u32[]{:S(2)}) collective-permute-start(s16[272,128]{1,0:T(8,128)(2,1)S(1)} %collective-permute-done.8.rest_2_), channel_id=1, source_target_pairs={{0,4},{4,0},{8,12},{12,8},{16,20},{20,16},{24,28},{28,24},{1,5},{5... | collective-permute-start | bytes 208904 | tf_op jit(solution)/shard_map/ppermute | solution.py:23
  45.5 0.9 %collective-permute-done.12.rest_6_ = s16[272,128]{1,0:T(8,128)(2,1)S(1)} collective-permute-done((s16[272,128]{1,0:T(8,128)(2,1)S(1)}, s16[272,128]{1,0:T(8,128)(2,1)S(1)}, u32[]{:S(2)}, u32[]{:S(2)}) %collective-permute-start.12) | collective-permute-done | bytes 69664 | tf_op jit(solution)/shard_map/ppermute | solution.py:23
  46.4 0.4 collective-permute-done.11.rest_5_
  46.7 1.7 %gather.1 = f32[16,128,128]{2,1,0:T(8,128)} custom-call(s32[2]{0:T(128)S(1)} %pad_add_fusion.ids, s16[272,128]{1,0:T(8,128)(2,1)S(1)} %combine.1.rest_0_, s16[272,128]{1,0:T(8,128)(2,1)S(1)} %collective-permute-done.7.rest_1_, s16[272,128]{1,0:T(8,128)(2,1)S(1)} %collective-permute-done.8.rest_2_, s16[272,128]{1,0:T(8,128)(2,1)S(1)} %collective-permute-done.9.rest_3_, ...), custom_call_target="tpu_custom_call" | custom-call | bytes 1048576 | tf_op jit(solution)/shard_map/gather/pallas_call | solution.py:556
  (12 shorter events, 0.7 us)
Async XLA Ops:
  0.0 10.3 %collective-permute-start.1 = (bf16[16,128,128]{2,1,0:T(8,128)(2,1)}, bf16[16,128,128]{2,1,0:T(8,128)(2,1)S(1)}, u32[]{:S(2)}, u32[]{:S(2)}) collective-permute-start(bf16[16,128,128]{2,1,0:T(8,128)(2,1)} %bitcast.11), channel_id=1, source_target_pairs={{0,4},{4,0},{8,12},{12,8},{16,20},{20,16},{24,28},{28,24},{1,5},{5... | collective-permute-start | bytes 1572872 | tf_op jit(solution)/shard_map/ppermute | solution.py:23
  2.4 8.0 %collective-permute-start = (bf16[4,128,128]{2,1,0:T(8,128)(2,1)S(1)}, bf16[4,128,128]{2,1,0:T(8,128)(2,1)S(1)}, u32[]{:S(2)}, u32[]{:S(2)}) collective-permute-start(bf16[4,128,128]{2,1,0:T(8,128)(2,1)S(1)} %get-tuple-element.23), channel_id=1, source_target_pairs={{4,1},{1,4},{5,2},{2,5},{6,3},{3,6},{12,9},{9,12},{13,10},{10,13},... | collective-permute-start | bytes 393224 | tf_op jit(solution)/shard_map/ppermute | solution.py:39
  14.8 2.8 %collective-permute-start.3 = (bf16[2,4,96,128]{3,2,1,0:T(8,128)(2,1)S(1)}, bf16[2,4,96,128]{3,2,1,0:T(8,128)(2,1)S(1)}, u32[]{:S(2)}, u32[]{:S(2)}) collective-permute-start(bf16[2,4,96,128]{3,2,1,0:T(8,128)(2,1)S(1)} %get-tuple-element.29), channel_id=1, source_target_pairs={{0,4},{4,0},{8,12},{12,8},{16,20},{20,16},{24,28},{28,24},{1,5},{5... | collective-permute-start | bytes 589832 | tf_op jit(solution)/shard_map/ppermute | solution.py:23
  14.9 8.7 %collective-permute-start.2 = (bf16[2,400,128]{2,1,0:T(8,128)(2,1)S(1)}, bf16[2,400,128]{2,1,0:T(8,128)(2,1)S(1)}, u32[]{:S(2)}, u32[]{:S(2)}) collective-permute-start(bf16[2,400,128]{2,1,0:T(8,128)(2,1)S(1)} %get-tuple-element.27), channel_id=1, source_target_pairs={{4,1},{1,4},{5,2},{2,5},{6,3},{3,6},{12,9},{9,12},{13,10},{10,13},... | collective-permute-start | bytes 614408 | tf_op jit(solution)/shard_map/ppermute | solution.py:39
  25.7 3.8 %collective-permute-start.4 = (s16[272,128]{1,0:T(8,128)(2,1)S(1)}, s16[272,128]{1,0:T(8,128)(2,1)S(1)}, u32[]{:S(2)}, u32[]{:S(2)}) collective-permute-start(s16[272,128]{1,0:T(8,128)(2,1)S(1)} %get-tuple-element.32), channel_id=1, source_target_pairs={{0,8},{4,12},{8,0},{12,4},{16,24},{20,28},{24,16},{28,20},{1,9},{5... | collective-permute-start | bytes 208904 | tf_op jit(solution)/shard_map/ppermute | solution.py:28
  27.2 6.1 %collective-permute-start.5 = (s16[272,128]{1,0:T(8,128)(2,1)S(1)}, s16[272,128]{1,0:T(8,128)(2,1)S(1)}, u32[]{:S(2)}, u32[]{:S(2)}) collective-permute-start(s16[272,128]{1,0:T(8,128)(2,1)S(1)} %get-tuple-element.33), channel_id=1, source_target_pairs={{0,16},{4,20},{8,24},{12,28},{16,0},{20,4},{24,8},{28,12},{1,17},{... | collective-permute-start | bytes 208904 | tf_op jit(solution)/shard_map/ppermute | solution.py:28
  29.5 5.6 %collective-permute-start.6 = (s16[272,128]{1,0:T(8,128)(2,1)S(1)}, s16[272,128]{1,0:T(8,128)(2,1)S(1)}, u32[]{:S(2)}, u32[]{:S(2)}) collective-permute-start(s16[272,128]{1,0:T(8,128)(2,1)S(1)} %get-tuple-element.34), channel_id=1, source_target_pairs={{0,24},{4,28},{8,16},{12,20},{16,8},{20,12},{24,0},{28,4},{1,25},{... | collective-permute-start | bytes 208904 | tf_op jit(solution)/shard_map/ppermute | solution.py:28
  35.4 5.2 %collective-permute-start.9 = (s16[272,128]{1,0:T(8,128)(2,1)S(1)}, s16[272,128]{1,0:T(8,128)(2,1)S(1)}, u32[]{:S(2)}, u32[]{:S(2)}) collective-permute-start(s16[272,128]{1,0:T(8,128)(2,1)S(1)} %combine.1.rest_0_), channel_id=1, source_target_pairs={{0,24},{4,28},{8,16},{12,20},{16,8},{20,12},{24,0},{28,4},{1,25},{... | collective-permute-start | bytes 208904 | tf_op jit(solution)/shard_map/ppermute | solution.py:28
  37.5 7.1 %collective-permute-start.8 = (s16[272,128]{1,0:T(8,128)(2,1)S(1)}, s16[272,128]{1,0:T(8,128)(2,1)S(1)}, u32[]{:S(2)}, u32[]{:S(2)}) collective-permute-start(s16[272,128]{1,0:T(8,128)(2,1)S(1)} %combine.1.rest_0_), channel_id=1, source_target_pairs={{0,16},{4,20},{8,24},{12,28},{16,0},{20,4},{24,8},{28,12},{1,17},{... | collective-permute-start | bytes 208904 | tf_op jit(solution)/shard_map/ppermute | solution.py:28
  37.8 7.7 %collective-permute-start.7 = (s16[272,128]{1,0:T(8,128)(2,1)S(1)}, s16[272,128]{1,0:T(8,128)(2,1)S(1)}, u32[]{:S(2)}, u32[]{:S(2)}) collective-permute-start(s16[272,128]{1,0:T(8,128)(2,1)S(1)} %combine.1.rest_0_), channel_id=1, source_target_pairs={{0,8},{4,12},{8,0},{12,4},{16,24},{20,28},{24,16},{28,20},{1,9},{5... | collective-permute-start | bytes 208904 | tf_op jit(solution)/shard_map/ppermute | solution.py:28
  39.0 6.5 %collective-permute-start.10 = (s16[272,128]{1,0:T(8,128)(2,1)S(1)}, s16[272,128]{1,0:T(8,128)(2,1)S(1)}, u32[]{:S(2)}, u32[]{:S(2)}) collective-permute-start(s16[272,128]{1,0:T(8,128)(2,1)S(1)} %combine.1.rest_0_), channel_id=1, source_target_pairs={{0,4},{4,0},{8,12},{12,8},{16,20},{20,16},{24,28},{28,24},{1,5},{5... | collective-permute-start | bytes 208904 | tf_op jit(solution)/shard_map/ppermute | solution.py:23
  40.5 5.0 %collective-permute-start.13 = (s16[272,128]{1,0:T(8,128)(2,1)S(1)}, s16[272,128]{1,0:T(8,128)(2,1)S(1)}, u32[]{:S(2)}, u32[]{:S(2)}) collective-permute-start(s16[272,128]{1,0:T(8,128)(2,1)S(1)} %collective-permute-done.9.rest_3_), channel_id=1, source_target_pairs={{0,4},{4,0},{8,12},{12,8},{16,20},{20,16},{24,28},{28,24},{1,5},{5... | collective-permute-start | bytes 208904 | tf_op jit(solution)/shard_map/ppermute | solution.py:23
  44.6 1.8 %collective-permute-start.12 = (s16[272,128]{1,0:T(8,128)(2,1)S(1)}, s16[272,128]{1,0:T(8,128)(2,1)S(1)}, u32[]{:S(2)}, u32[]{:S(2)}) collective-permute-start(s16[272,128]{1,0:T(8,128)(2,1)S(1)} %collective-permute-done.8.rest_2_), channel_id=1, source_target_pairs={{0,4},{4,0},{8,12},{12,8},{16,20},{20,16},{24,28},{28,24},{1,5},{5... | collective-permute-start | bytes 208904 | tf_op jit(solution)/shard_map/ppermute | solution.py:23
  45.5 1.3 %collective-permute-start.11 = (s16[272,128]{1,0:T(8,128)(2,1)S(1)}, s16[272,128]{1,0:T(8,128)(2,1)S(1)}, u32[]{:S(2)}, u32[]{:S(2)}) collective-permute-start(s16[272,128]{1,0:T(8,128)(2,1)S(1)} %collective-permute-done.7.rest_1_), channel_id=1, source_target_pairs={{0,4},{4,0},{8,12},{12,8},{16,20},{20,16},{24,28},{28,24},{1,5},{5... | collective-permute-start | bytes 208904 | tf_op jit(solution)/shard_map/ppermute | solution.py:23

commit v5 on v4

--- a/solution.py
+++ b/solution.py
@@ -63,6 +63,10 @@
     middle, step = marks
     cells = piece[at : at + rows, :].astype(jnp.int32).astype(jnp.float32)
     return cells * step + middle
+
+
+def view_slot(core, j, views):
+    return core ^ j if views > 1 else 0
 
 
 def is_covered(info, j, block):
@@ -125,10 +129,7 @@
         )
         for i in range(count)
     ]
-    half = img_own.shape[0]
-    copies.append(
-        pltpu.make_async_copy(images.at[0, pl.ds(half * core, half)], img_own, sems.at[count])
-    )
+    copies.append(pltpu.make_async_copy(images.at[0], img_own, sems.at[count]))
     for copy in copies:
         copy.start()
     row = lax.broadcasted_iota(jnp.int32, (depth, depth), 0)
@@ -146,7 +147,7 @@
     lane = lax.broadcasted_iota(jnp.int32, cov.shape, 1)
     bits = jnp.where(cov[...] != 0, jnp.left_shift(1, block), 0)
     for j in range(views):
-        view = chip * views + j
+        view = chip * views + view_slot(core, j, views)
         code = jnp.sum(jnp.where(lane == view, bits, 0).astype(jnp.float32))
         info[MARKS + j] = code.astype(jnp.int32)
         table[j, 0] = zero
@@ -217,8 +218,48 @@
     return jnp.concatenate(lines, axis=0)
 
 
+def dot_turned(slab, pairs, table, j, s):
+    return lax.dot_general(
+        left_side(slab, pairs, s),
+        right_side_turned(table, j, s),
+        (((1,), (1,)), ((), ())),
+        preferred_element_type=jnp.float32,
+    )
+
+
+def add_rows(total, part, cut):
+    if total is None:
+        return part
+    if not cut:
+        return total + part
+    return jnp.concatenate([total[:cut], total[cut:] + part], axis=0)
+
+
+def early_steps(j, rim, steps):
+    return range(rim // 2 + j, steps)
+
+
+def early_kernel(info, cols, table, sums, *, blocks):
+    views, steps = table.shape[0], (table.shape[1] - 1) // 2
+    pairs = cols.shape[0] // 3
+    rim = cols.shape[0] // 3
+    width = cols.shape[1]
+    rows_y = sums.shape[1] // pairs
+    block_width = width // blocks
+    for j in range(views):
+        first = window_of(info, j, blocks, rows_y // block_width)
+        y_start = pl.multiple_of(first * block_width, block_width)
+        total = None
+        for s in early_steps(j, rim, steps):
+            part = dot_turned(
+                lambda x: cols[x - rim, pl.ds(y_start, rows_y), :], range(pairs), table, j, s
+            )
+            total = part if total is None else total + part
+        sums[j] = total
+
+
 def blur_kernel(
-    info, halo, img_own, img_other, cols, table, quot, remote, near, pad, edge, image, sems, *, taps, blocks
+    info, halo, img_own, img_other, cols, table, early, quot, remote, near, pad, edge, image, *, taps, blocks
 ):
     core, chip = info[0], info[1]
     views, half, rows_y, depth = quot.shape
@@ -229,25 +270,15 @@
     if views == 1:
         own_at = pl.multiple_of(core * share_w, share_w)
         other_at = pl.multiple_of((1 - core) * share_w, share_w)
-        own_to = image.at[0, :, pl.ds(own_at, share_w)]
-        other_to = image.at[0, :, pl.ds(other_at, share_w)]
-    else:
-        own_to = image.at[core]
-        other_to = image.at[1 - core]
-    copies = [
-        pltpu.make_async_copy(img_own, own_to, sems.at[0]),
-        pltpu.make_async_copy(img_other.at[pl.ds(half * core, half)], other_to, sems.at[1]),
-    ]
-    for copy in copies:
-        copy.start()
+        for r in range(half):
+            image[r, pl.ds(own_at, share_w), :] = img_own[half * core + r]
+            image[r, pl.ds(other_at, share_w), :] = img_other[half * core + r]
     margin = jnp.zeros((rim, PAD, depth), jnp.float32)
     pad[:, :PAD, :] = margin
     pad[:, PAD + width :, :] = margin
     for x in range(rim):
         pad[x, PAD : PAD + width, :] = halo[canonical(core, x, rim - 1)].astype(jnp.float32)
     fill_columns(pad, edge, taps[1], width)
-    for copy in copies:
-        copy.wait()
     for j in range(views):
         first = window_of(info, j, blocks, window)
         mask = window_mask(info, j, first, window, block_width)
@@ -257,30 +288,30 @@
             part = edge.at[x] if x < rim else cols.at[x - rim]
             return part[pl.ds(y_start, rows_y), :]
 
-        blurred = None
-        for s in range((table.shape[1] - 1) // 2):
-            part = lax.dot_general(
-                left_side(slab, range(half // 2), s),
-                right_side_turned(table, j, s),
-                (((1,), (1,)), ((), ())),
-                preferred_element_type=jnp.float32,
-            )
-            blurred = part if blurred is None else blurred + part
-        remote[j, :HEADER, :] = jnp.full((HEADER, depth), first, jnp.int32).astype(jnp.bfloat16)
+        total = early[j]
+        for s in range(early_steps(j, rim, 0).start):
+            total = total + dot_turned(slab, range(half // 2), table, j, s)
+        blurred = [total[i * rows_y : (i + 1) * rows_y] for i in range(half // 2)]
+        slot = view_slot(core, j, views)
+        remote[slot, :HEADER, :] = jnp.full((HEADER, depth), first, jnp.int32).astype(jnp.bfloat16)
         for r in range(half):
-            cells = image[j, canonical(core, r, half - 1), pl.ds(y_start, rows_y), :]
+            row = canonical(core, r, half - 1)
+            if views == 1:
+                cells = image[row, pl.ds(y_start, rows_y), :]
+            else:
+                cells = (img_other if j else img_own)[half * core + row, pl.ds(y_start, rows_y), :]
             i, w = r // 2, r % 2
-            below = blurred[i * rows_y : (i + 1) * rows_y, w * depth : (w + 1) * depth]
+            below = blurred[i][:, w * depth : (w + 1) * depth]
             ratio = jnp.where(mask, cells.astype(jnp.float32) / below, 0.0).astype(jnp.bfloat16)
             quot[j, r] = ratio
             if r < rim:
                 low = HEADER + r * rows_y
-                remote[j, low : low + rows_y, :] = ratio
+                remote[slot, low : low + rows_y, :] = ratio
             else:
-                near[j, r - rim] = ratio
-
-
-def inner_kernel(quot, near, table, sums, pad, cols, *, taps):
+                near[slot, r - rim] = ratio
+
+
+def inner_kernel(info, quot, near, table, sums, pad, cols, *, taps):
     views, half, rows_y, depth = quot.shape
     rim = near.shape[1]
     pairs = half // 2
@@ -292,7 +323,9 @@
         for r in range(half):
             pad[j, r, PAD : PAD + rows_y, :] = quot[j, r].astype(jnp.float32)
         for r in range(rim):
-            pad[j, half + rim - 1 - r, PAD : PAD + rows_y, :] = near[j, r].astype(jnp.float32)
+            pad[j, half + rim - 1 - r, PAD : PAD + rows_y, :] = near[view_slot(info[0], j, views), r].astype(
+                jnp.float32
+            )
         fill_columns(pad.at[j], cols.at[j], taps[1], rows_y)
         total = None
         for s in range(steps - 1, -1, -1):
@@ -302,13 +335,7 @@
                 right_side(table, j, s),
                 preferred_element_type=jnp.float32,
             )
-            if total is None:
-                total = part
-            elif not skip:
-                total = total + part
-            else:
-                cut = skip * rows_y
-                total = jnp.concatenate([total[:cut], total[cut:] + part], axis=0)
+            total = add_rows(total, part, skip * rows_y)
         sums[j] = total
 
 
@@ -326,12 +353,13 @@
         first = window_of(info, j, blocks, window)
         mask = window_mask(info, j, first, window, block_width)
         y_start = pl.multiple_of(first * block_width, block_width)
-        there = jnp.max(remote[j, :HEADER, :].astype(jnp.float32)).astype(jnp.int32)
+        slot = view_slot(info[0], j, views)
+        there = jnp.max(remote[slot, :HEADER, :].astype(jnp.float32)).astype(jnp.int32)
         there = jnp.clip(there, 0, blocks - window)
         y_there = pl.multiple_of(there * block_width, block_width)
         for r in range(rim):
             low = HEADER + r * rows_y
-            cells = remote[j, low : low + rows_y, :].astype(jnp.float32)
+            cells = remote[slot, low : low + rows_y, :].astype(jnp.float32)
             far[j, rim - 1 - r, pl.ds(PAD + y_there, rows_y), :] = cells
         for r in range(rim):
             pad[j, r] = far[j, r, pl.ds(y_start, rows_y + 2 * PAD), :]
@@ -426,7 +454,7 @@
         out_specs=out_specs if many else out_specs[0],
         scratch_shapes=list(scratch),
         compiler_params=pltpu.CompilerParams(vmem_limit_bytes=VMEM_LIMIT),
-        cost_estimate=pl.CostEstimate(flops=flops, bytes_accessed=1 << 20, transcendentals=0),
+        cost_estimate=pl.CostEstimate(flops=flops, bytes_accessed=1 << 16, transcendentals=0),
     )
 
 
@@ -484,7 +512,7 @@
             pltpu.VMEM((views, taps_x + 2, deep, depth), bf16),
             pltpu.VMEM((inner, width, deep), bf16),
             shape((MARKS + views,), jnp.int32),
-            pltpu.VMEM((half, share_w, depth), bf16),
+            pltpu.VMEM((slab_x, share_w, depth), bf16),
             pltpu.VMEM((rows, width, depth), f32),
         ),
         "svvhh",
@@ -497,6 +525,14 @@
         "vvsvv",
     )(ids, cov, spread, estimate, images)
 
+    early = call(
+        functools.partial(early_kernel, blocks=blocks),
+        "early",
+        pltpu.VMEM((views, half // 2 * rows_y, 2 * depth), f32),
+        "svv",
+        flops=0,
+    )(info, cols, table)
+
     quot, remote, near = call(
         functools.partial(blur_kernel, taps=taps, blocks=blocks),
         "blur",
@@ -505,15 +541,14 @@
             shape((views, HEADER + rim * rows_y, depth), bf16),
             shape((views, rim, rows_y, depth), bf16),
         ),
-        "svvvvv",
+        "svvvvvv",
         [
             pltpu.VMEM((rim, wide, depth), f32),
             pltpu.VMEM((rim, width, deep), bf16),
-            pltpu.VMEM((views, half, width, depth), bf16),
-            sems((2,)),
+            pltpu.VMEM((half, width, depth) if views == 1 else (8, depth), bf16),
         ],
         work,
-    )(info, halo, img_own, img_other, cols, table)
+    )(info, halo, img_own, img_other, cols, table, early)
     near = swap_cores(near)
     remote = swap_layers(remote)
 
@@ -521,13 +556,13 @@
         functools.partial(inner_kernel, taps=taps),
         "inner",
         pltpu.VMEM((views, half // 2 * rows_y, 2 * depth), f32),
-        "vvv",
+        "svvv",
         [
             pltpu.VMEM((views, inner, tall, depth), f32),
             pltpu.VMEM((views, inner, rows_y, deep), bf16),
         ],
         work,
-    )(quot, near, table)
+    )(info, quot, near, table)
 
     coded = shape((HEADER + rows * width, depth), jnp.int16)
     pieces = call(

time: 48.5 us -> 47.2 us (0.973)
  waiting for transfers between devices: 13.7 us -> 11 us
  Pallas kernels: 16.6 us -> 17.9 us
    ppermute x2, waiting for transfers between devices: 4.41 us -> 1.45 us  [swap_layers(): return lax.ppermute(cells, ('view', 'blk'), route)]
    pallas_call x0 -> x1, Pallas kernels: none -> 2.54 us  [local(): call(functools.partial(early_kernel, blocks=blocks), 'early', pltpu.VMEM(...]
    pallas_call x1, Pallas kernels: 4.5 us -> 2.74 us  [local(): call(functools.partial(blur_kernel, taps=taps, blocks=blocks), 'blur', (p...]
    ppermute x2, starting transfers between devices: 5.75 us -> 6.49 us  [swap_layers(): return lax.ppermute(cells, ('view', 'blk'), route)]
    ppermute x6, starting transfers between devices: 4.83 us -> 4.21 us  [swap_cores(): return lax.ppermute(cells, 'view', [(i, i ^ 1) for i in range(count)])]
    pallas_call x1, Pallas kernels: 3.6 us -> 4.14 us  [local(): call(functools.partial(inner_kernel, taps=taps), 'inner', pltpu.VMEM((vie...]
  transfers between devices with their start and end apart: 14 -> 14, of which waited for: 8 -> 7; matrix products, arithmetic and copies ran while one was open for 0% -> 0% of each run, Pallas kernels for 17% -> 24%
where the time goes in v5:
time: 47.2 us; the launch traced here: 47.1 us
  starting transfers between devices  18 us (38%)
  Pallas kernels  17.9 us (38%)
  waiting for transfers between devices  11 us (23%)
    ppermute x6, waiting for transfers between devices, swap_chips(): lax.ppermute(cells, 'view', [(i, i ^ 2 * step) for i in range(count)])  8.28 us
    ppermute x6, starting transfers between devices, swap_chips(): lax.ppermute(cells, 'view', [(i, i ^ 2 * step) for i in range(count)])  7.28 us
    ppermute x2, starting transfers between devices, swap_layers(): return lax.ppermute(cells, ('view', 'blk'), route)  6.49 us
    ppermute x6, starting transfers between devices, swap_cores(): return lax.ppermute(cells, 'view', [(i, i ^ 1) for i in range(count)])  4.21 us
    pallas_call x1, Pallas kernels, local(): call(functools.partial(inner_kernel, taps=taps), 'inner', pltpu.VMEM((vie...  4.14 us
    pallas_call x1, Pallas kernels, local(): call(functools.partial(tables_kernel, taps=taps), 'tables', (pltpu.VMEM((...  2.87 us
    pallas_call x1, Pallas kernels, local(): call(functools.partial(blur_kernel, taps=taps, blocks=blocks), 'blur', (p...  2.74 us
    pallas_call x1, Pallas kernels, local(): call(functools.partial(early_kernel, blocks=blocks), 'early', pltpu.VMEM(...  2.54 us
  transfers between devices with their start and end apart: 14, of which 7 were waited for; matrix products, arithmetic and copies ran while one was open for 0% of the time, Pallas kernels for 24%

profile of v5, /device:TPU:3, one launch (start us, length us, event | category | flops | bytes accessed | tf_op | source)
XLA Modules:
  0.0 47.1 jit_solution(3092629158338158514)
XLA Ops:
  0.0 0.7 %collective-permute-start.1 = (bf16[16,128,128]{2,1,0:T(8,128)(2,1)}, bf16[16,128,128]{2,1,0:T(8,128)(2,1)S(1)}, u32[]{:S(2)}, u32[]{:S(2)}) collective-permute-start(bf16[16,128,128]{2,1,0:T(8,128)(2,1)} %bitcast.11), channel_id=1, source_target_pairs={{0,4},{4,0},{8,12},{12,8},{16,20},{20,16},{24,28},{28,24},{1,5},{5... | collective-permute-start | bytes 1572872 | tf_op jit(solution)/shard_map/ppermute | solution.py:23
  0.8 1.6 %payload.1 = (bf16[4,128,128]{2,1,0:T(8,128)(2,1)S(1)}, s32[4,8]{1,0:T(4,128)S(1)}, f32[504,25]{1,0:T(8,128)S(1)}) custom-call(s32[2]{0:T(128)S(1)} %pad_add_fusion.ids, s32[4,8]{1,0:T(4,128)} %bitcast.10, f32[504,25]{1,0:T(8,128)} %bitcast.9, f32[16,128,128]{2,1,0:T(8,128)} %est.3), custom_call_target="tpu_custom_call" | custom-call | bytes 65536 | tf_op jit(solution)/shard_map/payload/pallas_call | solution.py:495
  2.4 3.0 %collective-permute-start = (bf16[4,128,128]{2,1,0:T(8,128)(2,1)S(1)}, bf16[4,128,128]{2,1,0:T(8,128)(2,1)S(1)}, u32[]{:S(2)}, u32[]{:S(2)}) collective-permute-start(bf16[4,128,128]{2,1,0:T(8,128)(2,1)S(1)} %get-tuple-element.23), channel_id=1, source_target_pairs={{4,1},{1,4},{5,2},{2,5},{6,3},{3,6},{12,9},{9,12},{13,10},{10,13},... | collective-permute-start | bytes 393224 | tf_op jit(solution)/shard_map/ppermute | solution.py:39
  5.4 2.9 %tables.1 = (bf16[2,11,896,128]{3,2,1,0:T(8,128)(2,1)S(1)}, bf16[12,128,896]{2,1,0:T(8,128)(2,1)S(1)}, s32[4]{0:T(128)S(1)}, bf16[16,128,128]{2,1,0:T(8,128)(2,1)S(1)}, f32[2,128,128]{2,1,0:T(8,128)S(1)}) custom-call(s32[2]{0:T(128)S(1)} %pad_add_fusion.ids, s32[4,8]{1,0:T(4,128)S(1)} %get-tuple-element.20.cov, f32[504,25]{1,0:T(8,128)S(1)} %get-tuple-element.21.spread, ...), custom_call_target="tpu_custom_call" | custom-call | flops 1585446912 | bytes 65536 | tf_op jit(solution)/shard_map/tables/pallas_call | solution.py:508
  8.2 2.5 %early.1 = f32[2,384,256]{2,1,0:T(8,128)S(1)} custom-call(s32[4]{0:T(128)S(1)} %get-tuple-element.22.info, bf16[12,128,896]{2,1,0:T(8,128)(2,1)S(1)} %get-tuple-element.25.cols, bf16[2,11,896,128]{3,2,1,0:T(8,128)(2,1)S(1)} %get-tuple-element.26.table), custom_call_target="tpu_custom_call" | custom-call | bytes 65536 | tf_op jit(solution)/shard_map/early/pallas_call | solution.py:528
  10.8 2.7 %blur.1 = (bf16[2,8,96,128]{3,2,1,0:T(8,128)(2,1)S(1)}, bf16[2,400,128]{2,1,0:T(8,128)(2,1)S(1)}, bf16[2,4,96,128]{3,2,1,0:T(8,128)(2,1)S(1)}) custom-call(s32[4]{0:T(128)S(1)} %get-tuple-element.22.info, bf16[4,128,128]{2,1,0:T(8,128)(2,1)S(1)} %collective-permute-done.halo, bf16[16,128,128]{2,1,0:T(8,128)(2,1)S(1)} %get-tuple-element.24.img_own, ...), custom_call_target="tpu_custom_call" | custom-call | flops 3170893824 | bytes 65536 | tf_op jit(solution)/shard_map/blur/pallas_call | solution.py:536
  13.6 3.5 %collective-permute-start.2 = (bf16[2,400,128]{2,1,0:T(8,128)(2,1)S(1)}, bf16[2,400,128]{2,1,0:T(8,128)(2,1)S(1)}, u32[]{:S(2)}, u32[]{:S(2)}) collective-permute-start(bf16[2,400,128]{2,1,0:T(8,128)(2,1)S(1)} %get-tuple-element.27), channel_id=1, source_target_pairs={{4,1},{1,4},{5,2},{2,5},{6,3},{3,6},{12,9},{9,12},{13,10},{10,13},... | collective-permute-start | bytes 614408 | tf_op jit(solution)/shard_map/ppermute | solution.py:39
  17.1 4.1 %inner.1.sums = f32[2,384,256]{2,1,0:T(8,128)S(1)} custom-call(s32[4]{0:T(128)S(1)} %get-tuple-element.22.info, bf16[2,8,96,128]{3,2,1,0:T(8,128)(2,1)S(1)} %get-tuple-element.28.quot, bf16[2,4,96,128]{3,2,1,0:T(8,128)(2,1)S(1)} %collective-permute-done.3.near, bf16[2,11,896,128]{3,2,1,0:T(8,128)(2,1)S(1)} %get-tuple-element.26.table), custom_call_target="tpu_custom_call" | custom-call | flops 3170893824 | bytes 65536 | tf_op jit(solution)/shard_map/inner/pallas_call | solution.py:555
  21.3 1.4 %collective-permute-done.2.remote = bf16[2,400,128]{2,1,0:T(8,128)(2,1)S(1)} collective-permute-done((bf16[2,400,128]{2,1,0:T(8,128)(2,1)S(1)}, bf16[2,400,128]{2,1,0:T(8,128)(2,1)S(1)}, u32[]{:S(2)}, u32[]{:S(2)}) %collective-permute-start.2) | collective-permute-done | bytes 204832 | tf_op jit(solution)/shard_map/ppermute | solution.py:39
  22.7 2.1 %correct.1 = (f32[2,128,128]{2,1,0:T(8,128)S(1)}, s16[272,128]{1,0:T(8,128)(2,1)S(1)}, s16[272,128]{1,0:T(8,128)(2,1)S(1)}, s16[272,128]{1,0:T(8,128)(2,1)S(1)}) custom-call(s32[4]{0:T(128)S(1)} %get-tuple-element.22.info, bf16[2,400,128]{2,1,0:T(8,128)(2,1)S(1)} %collective-permute-done.2.remote, f32[2,384,256]{2,1,0:T(8,128)S(1)} %inner.1.sums, ...), custom_call_target="tpu_custom_call" | custom-call | flops 792723456 | bytes 65536 | tf_op jit(solution)/shard_map/correct/pallas_call | solution.py:568
  24.8 1.4 %collective-permute-start.4 = (s16[272,128]{1,0:T(8,128)(2,1)S(1)}, s16[272,128]{1,0:T(8,128)(2,1)S(1)}, u32[]{:S(2)}, u32[]{:S(2)}) collective-permute-start(s16[272,128]{1,0:T(8,128)(2,1)S(1)} %get-tuple-element.32), channel_id=1, source_target_pairs={{0,8},{4,12},{8,0},{12,4},{16,24},{20,28},{24,16},{28,20},{1,9},{5... | collective-permute-start | bytes 208904 | tf_op jit(solution)/shard_map/ppermute | solution.py:28
  26.2 2.3 %collective-permute-start.5 = (s16[272,128]{1,0:T(8,128)(2,1)S(1)}, s16[272,128]{1,0:T(8,128)(2,1)S(1)}, u32[]{:S(2)}, u32[]{:S(2)}) collective-permute-start(s16[272,128]{1,0:T(8,128)(2,1)S(1)} %get-tuple-element.33), channel_id=1, source_target_pairs={{0,16},{4,20},{8,24},{12,28},{16,0},{20,4},{24,8},{28,12},{1,17},{... | collective-permute-start | bytes 208904 | tf_op jit(solution)/shard_map/ppermute | solution.py:28
  28.5 3.6 %collective-permute-done.5.rest_1_ = s16[272,128]{1,0:T(8,128)(2,1)S(1)} collective-permute-done((s16[272,128]{1,0:T(8,128)(2,1)S(1)}, s16[272,128]{1,0:T(8,128)(2,1)S(1)}, u32[]{:S(2)}, u32[]{:S(2)}) %collective-permute-start.5) | collective-permute-done | bytes 69664 | tf_op jit(solution)/shard_map/ppermute | solution.py:28
  32.1 1.7 %collective-permute-done.6.rest_2_ = s16[272,128]{1,0:T(8,128)(2,1)S(1)} collective-permute-done((s16[272,128]{1,0:T(8,128)(2,1)S(1)}, s16[272,128]{1,0:T(8,128)(2,1)S(1)}, u32[]{:S(2)}, u32[]{:S(2)}) %collective-permute-start.6) | collective-permute-done | bytes 69664 | tf_op jit(solution)/shard_map/ppermute | solution.py:28
  34.1 2.4 %collective-permute-start.9 = (s16[272,128]{1,0:T(8,128)(2,1)S(1)}, s16[272,128]{1,0:T(8,128)(2,1)S(1)}, u32[]{:S(2)}, u32[]{:S(2)}) collective-permute-start(s16[272,128]{1,0:T(8,128)(2,1)S(1)} %combine.1.rest_0_), channel_id=1, source_target_pairs={{0,24},{4,28},{8,16},{12,20},{16,8},{20,12},{24,0},{28,4},{1,25},{... | collective-permute-start | bytes 208904 | tf_op jit(solution)/shard_map/ppermute | solution.py:28
  36.5 1.2 %collective-permute-start.7 = (s16[272,128]{1,0:T(8,128)(2,1)S(1)}, s16[272,128]{1,0:T(8,128)(2,1)S(1)}, u32[]{:S(2)}, u32[]{:S(2)}) collective-permute-start(s16[272,128]{1,0:T(8,128)(2,1)S(1)} %combine.1.rest_0_), channel_id=1, source_target_pairs={{0,8},{4,12},{8,0},{12,4},{16,24},{20,28},{24,16},{28,20},{1,9},{5... | collective-permute-start | bytes 208904 | tf_op jit(solution)/shard_map/ppermute | solution.py:28
  37.7 1.1 %collective-permute-start.10 = (s16[272,128]{1,0:T(8,128)(2,1)S(1)}, s16[272,128]{1,0:T(8,128)(2,1)S(1)}, u32[]{:S(2)}, u32[]{:S(2)}) collective-permute-start(s16[272,128]{1,0:T(8,128)(2,1)S(1)} %combine.1.rest_0_), channel_id=1, source_target_pairs={{0,4},{4,0},{8,12},{12,8},{16,20},{20,16},{24,28},{28,24},{1,5},{5... | collective-permute-start | bytes 208904 | tf_op jit(solution)/shard_map/ppermute | solution.py:23
  38.8 0.7 %collective-permute-done.9.rest_3_ = s16[272,128]{1,0:T(8,128)(2,1)S(1)} collective-permute-done((s16[272,128]{1,0:T(8,128)(2,1)S(1)}, s16[272,128]{1,0:T(8,128)(2,1)S(1)}, u32[]{:S(2)}, u32[]{:S(2)}) %collective-permute-start.9) | collective-permute-done | bytes 69664 | tf_op jit(solution)/shard_map/ppermute | solution.py:28
  39.5 1.5 %collective-permute-start.13 = (s16[272,128]{1,0:T(8,128)(2,1)S(1)}, s16[272,128]{1,0:T(8,128)(2,1)S(1)}, u32[]{:S(2)}, u32[]{:S(2)}) collective-permute-start(s16[272,128]{1,0:T(8,128)(2,1)S(1)} %collective-permute-done.9.rest_3_), channel_id=1, source_target_pairs={{0,4},{4,0},{8,12},{12,8},{16,20},{20,16},{24,28},{28,24},{1,5},{5... | collective-permute-start | bytes 208904 | tf_op jit(solution)/shard_map/ppermute | solution.py:23
  41.0 2.3 %collective-permute-done.8.rest_2_ = s16[272,128]{1,0:T(8,128)(2,1)S(1)} collective-permute-done((s16[272,128]{1,0:T(8,128)(2,1)S(1)}, s16[272,128]{1,0:T(8,128)(2,1)S(1)}, u32[]{:S(2)}, u32[]{:S(2)}) %collective-permute-start.8) | collective-permute-done | bytes 69664 | tf_op jit(solution)/shard_map/ppermute | solution.py:28
  43.3 0.9 %collective-permute-start.12 = (s16[272,128]{1,0:T(8,128)(2,1)S(1)}, s16[272,128]{1,0:T(8,128)(2,1)S(1)}, u32[]{:S(2)}, u32[]{:S(2)}) collective-permute-start(s16[272,128]{1,0:T(8,128)(2,1)S(1)} %collective-permute-done.8.rest_2_), channel_id=1, source_target_pairs={{0,4},{4,0},{8,12},{12,8},{16,20},{20,16},{24,28},{28,24},{1,5},{5... | collective-permute-start | bytes 208904 | tf_op jit(solution)/shard_map/ppermute | solution.py:23
  44.2 0.9 %collective-permute-done.12.rest_6_ = s16[272,128]{1,0:T(8,128)(2,1)S(1)} collective-permute-done((s16[272,128]{1,0:T(8,128)(2,1)S(1)}, s16[272,128]{1,0:T(8,128)(2,1)S(1)}, u32[]{:S(2)}, u32[]{:S(2)}) %collective-permute-start.12) | collective-permute-done | bytes 69664 | tf_op jit(solution)/shard_map/ppermute | solution.py:23
  45.1 0.4 collective-permute-done.11.rest_5_
  45.4 1.7 %gather.1 = f32[16,128,128]{2,1,0:T(8,128)} custom-call(s32[2]{0:T(128)S(1)} %pad_add_fusion.ids, s16[272,128]{1,0:T(8,128)(2,1)S(1)} %combine.1.rest_0_, s16[272,128]{1,0:T(8,128)(2,1)S(1)} %collective-permute-done.7.rest_1_, s16[272,128]{1,0:T(8,128)(2,1)S(1)} %collective-permute-done.8.rest_2_, s16[272,128]{1,0:T(8,128)(2,1)S(1)} %collective-permute-done.9.rest_3_, ...), custom_call_target="tpu_custom_call" | custom-call | bytes 65536 | tf_op jit(solution)/shard_map/gather/pallas_call | solution.py:591
  (13 shorter events, 0.5 us)
Async XLA Ops:
  0.0 10.8 %collective-permute-start.1 = (bf16[16,128,128]{2,1,0:T(8,128)(2,1)}, bf16[16,128,128]{2,1,0:T(8,128)(2,1)S(1)}, u32[]{:S(2)}, u32[]{:S(2)}) collective-permute-start(bf16[16,128,128]{2,1,0:T(8,128)(2,1)} %bitcast.11), channel_id=1, source_target_pairs={{0,4},{4,0},{8,12},{12,8},{16,20},{20,16},{24,28},{28,24},{1,5},{5... | collective-permute-start | bytes 1572872 | tf_op jit(solution)/shard_map/ppermute | solution.py:23
  2.4 8.4 %collective-permute-start = (bf16[4,128,128]{2,1,0:T(8,128)(2,1)S(1)}, bf16[4,128,128]{2,1,0:T(8,128)(2,1)S(1)}, u32[]{:S(2)}, u32[]{:S(2)}) collective-permute-start(bf16[4,128,128]{2,1,0:T(8,128)(2,1)S(1)} %get-tuple-element.23), channel_id=1, source_target_pairs={{4,1},{1,4},{5,2},{2,5},{6,3},{3,6},{12,9},{9,12},{13,10},{10,13},... | collective-permute-start | bytes 393224 | tf_op jit(solution)/shard_map/ppermute | solution.py:39
  13.6 3.6 %collective-permute-start.3 = (bf16[2,4,96,128]{3,2,1,0:T(8,128)(2,1)S(1)}, bf16[2,4,96,128]{3,2,1,0:T(8,128)(2,1)S(1)}, u32[]{:S(2)}, u32[]{:S(2)}) collective-permute-start(bf16[2,4,96,128]{3,2,1,0:T(8,128)(2,1)S(1)} %get-tuple-element.29), channel_id=1, source_target_pairs={{0,4},{4,0},{8,12},{12,8},{16,20},{20,16},{24,28},{28,24},{1,5},{5... | collective-permute-start | bytes 589832 | tf_op jit(solution)/shard_map/ppermute | solution.py:23
  13.6 9.1 %collective-permute-start.2 = (bf16[2,400,128]{2,1,0:T(8,128)(2,1)S(1)}, bf16[2,400,128]{2,1,0:T(8,128)(2,1)S(1)}, u32[]{:S(2)}, u32[]{:S(2)}) collective-permute-start(bf16[2,400,128]{2,1,0:T(8,128)(2,1)S(1)} %get-tuple-element.27), channel_id=1, source_target_pairs={{4,1},{1,4},{5,2},{2,5},{6,3},{3,6},{12,9},{9,12},{13,10},{10,13},... | collective-permute-start | bytes 614408 | tf_op jit(solution)/shard_map/ppermute | solution.py:39
  24.8 3.7 %collective-permute-start.4 = (s16[272,128]{1,0:T(8,128)(2,1)S(1)}, s16[272,128]{1,0:T(8,128)(2,1)S(1)}, u32[]{:S(2)}, u32[]{:S(2)}) collective-permute-start(s16[272,128]{1,0:T(8,128)(2,1)S(1)} %get-tuple-element.32), channel_id=1, source_target_pairs={{0,8},{4,12},{8,0},{12,4},{16,24},{20,28},{24,16},{28,20},{1,9},{5... | collective-permute-start | bytes 208904 | tf_op jit(solution)/shard_map/ppermute | solution.py:28
  26.2 5.9 %collective-permute-start.5 = (s16[272,128]{1,0:T(8,128)(2,1)S(1)}, s16[272,128]{1,0:T(8,128)(2,1)S(1)}, u32[]{:S(2)}, u32[]{:S(2)}) collective-permute-start(s16[272,128]{1,0:T(8,128)(2,1)S(1)} %get-tuple-element.33), channel_id=1, source_target_pairs={{0,16},{4,20},{8,24},{12,28},{16,0},{20,4},{24,8},{28,12},{1,17},{... | collective-permute-start | bytes 208904 | tf_op jit(solution)/shard_map/ppermute | solution.py:28
  28.5 5.3 %collective-permute-start.6 = (s16[272,128]{1,0:T(8,128)(2,1)S(1)}, s16[272,128]{1,0:T(8,128)(2,1)S(1)}, u32[]{:S(2)}, u32[]{:S(2)}) collective-permute-start(s16[272,128]{1,0:T(8,128)(2,1)S(1)} %get-tuple-element.34), channel_id=1, source_target_pairs={{0,24},{4,28},{8,16},{12,20},{16,8},{20,12},{24,0},{28,4},{1,25},{... | collective-permute-start | bytes 208904 | tf_op jit(solution)/shard_map/ppermute | solution.py:28
  34.1 5.4 %collective-permute-start.9 = (s16[272,128]{1,0:T(8,128)(2,1)S(1)}, s16[272,128]{1,0:T(8,128)(2,1)S(1)}, u32[]{:S(2)}, u32[]{:S(2)}) collective-permute-start(s16[272,128]{1,0:T(8,128)(2,1)S(1)} %combine.1.rest_0_), channel_id=1, source_target_pairs={{0,24},{4,28},{8,16},{12,20},{16,8},{20,12},{24,0},{28,4},{1,25},{... | collective-permute-start | bytes 208904 | tf_op jit(solution)/shard_map/ppermute | solution.py:28
  36.5 6.7 %collective-permute-start.8 = (s16[272,128]{1,0:T(8,128)(2,1)S(1)}, s16[272,128]{1,0:T(8,128)(2,1)S(1)}, u32[]{:S(2)}, u32[]{:S(2)}) collective-permute-start(s16[272,128]{1,0:T(8,128)(2,1)S(1)} %combine.1.rest_0_), channel_id=1, source_target_pairs={{0,16},{4,20},{8,24},{12,28},{16,0},{20,4},{24,8},{28,12},{1,17},{... | collective-permute-start | bytes 208904 | tf_op jit(solution)/shard_map/ppermute | solution.py:28
  36.5 7.6 %collective-permute-start.7 = (s16[272,128]{1,0:T(8,128)(2,1)S(1)}, s16[272,128]{1,0:T(8,128)(2,1)S(1)}, u32[]{:S(2)}, u32[]{:S(2)}) collective-permute-start(s16[272,128]{1,0:T(8,128)(2,1)S(1)} %combine.1.rest_0_), channel_id=1, source_target_pairs={{0,8},{4,12},{8,0},{12,4},{16,24},{20,28},{24,16},{28,20},{1,9},{5... | collective-permute-start | bytes 208904 | tf_op jit(solution)/shard_map/ppermute | solution.py:28
  37.7 6.4 %collective-permute-start.10 = (s16[272,128]{1,0:T(8,128)(2,1)S(1)}, s16[272,128]{1,0:T(8,128)(2,1)S(1)}, u32[]{:S(2)}, u32[]{:S(2)}) collective-permute-start(s16[272,128]{1,0:T(8,128)(2,1)S(1)} %combine.1.rest_0_), channel_id=1, source_target_pairs={{0,4},{4,0},{8,12},{12,8},{16,20},{20,16},{24,28},{28,24},{1,5},{5... | collective-permute-start | bytes 208904 | tf_op jit(solution)/shard_map/ppermute | solution.py:23
  39.5 4.7 %collective-permute-start.13 = (s16[272,128]{1,0:T(8,128)(2,1)S(1)}, s16[272,128]{1,0:T(8,128)(2,1)S(1)}, u32[]{:S(2)}, u32[]{:S(2)}) collective-permute-start(s16[272,128]{1,0:T(8,128)(2,1)S(1)} %collective-permute-done.9.rest_3_), channel_id=1, source_target_pairs={{0,4},{4,0},{8,12},{12,8},{16,20},{20,16},{24,28},{28,24},{1,5},{5... | collective-permute-start | bytes 208904 | tf_op jit(solution)/shard_map/ppermute | solution.py:23
  43.3 1.8 %collective-permute-start.12 = (s16[272,128]{1,0:T(8,128)(2,1)S(1)}, s16[272,128]{1,0:T(8,128)(2,1)S(1)}, u32[]{:S(2)}, u32[]{:S(2)}) collective-permute-start(s16[272,128]{1,0:T(8,128)(2,1)S(1)} %collective-permute-done.8.rest_2_), channel_id=1, source_target_pairs={{0,4},{4,0},{8,12},{12,8},{16,20},{20,16},{24,28},{28,24},{1,5},{5... | collective-permute-start | bytes 208904 | tf_op jit(solution)/shard_map/ppermute | solution.py:23
  44.2 1.3 %collective-permute-start.11 = (s16[272,128]{1,0:T(8,128)(2,1)S(1)}, s16[272,128]{1,0:T(8,128)(2,1)S(1)}, u32[]{:S(2)}, u32[]{:S(2)}) collective-permute-start(s16[272,128]{1,0:T(8,128)(2,1)S(1)} %collective-permute-done.7.rest_1_), channel_id=1, source_target_pairs={{0,4},{4,0},{8,12},{12,8},{16,20},{20,16},{24,28},{28,24},{1,5},{5... | collective-permute-start | bytes 208904 | tf_op jit(solution)/shard_map/ppermute | solution.py:23

commit v6 on v5

--- a/solution.py
+++ b/solution.py
@@ -10,7 +10,7 @@
 CAP = 3
 LANES = 128
 PAD = 8
-MARKS = 2
+MARKS = 3
 HEADER = 16
 MARK = 256.0
 LEVEL = 32767.0
@@ -32,11 +32,21 @@
     views, layers = lax.axis_size("view"), lax.axis_size("blk")
     route = []
     for chip in range(views // 2):
-        for layer in range(layers - 1):
-            low = (2 * chip + 1) * layers + layer
-            high = 2 * chip * layers + layer + 1
-            route += [(low, high), (high, low)]
+        for layer in range(layers):
+            for core in range(2):
+                there = layer + (1 if core else -1)
+                if 0 <= there < layers:
+                    to = (2 * chip + 1 - core) * layers + there
+                else:
+                    to = (2 * (chip ^ 1) + core) * layers + layer
+                route.append(((2 * chip + core) * layers + layer, to))
     return lax.ppermute(cells, ("view", "blk"), route)
+
+
+def has_far(core):
+    layer = lax.axis_index("blk")
+    there = layer + 2 * core - 1
+    return (there >= 0) & (there < lax.axis_size("blk"))
 
 
 def code_header(low, high):
@@ -143,6 +153,7 @@
     total_views = spread.shape[0] // (taps_x * taps_y)
     info[0] = core
     info[1] = chip
+    info[2] = ids[2]
     block = lax.broadcasted_iota(jnp.int32, cov.shape, 0)
     lane = lax.broadcasted_iota(jnp.int32, cov.shape, 1)
     bits = jnp.where(cov[...] != 0, jnp.left_shift(1, block), 0)
@@ -277,7 +288,8 @@
     pad[:, :PAD, :] = margin
     pad[:, PAD + width :, :] = margin
     for x in range(rim):
-        pad[x, PAD : PAD + width, :] = halo[canonical(core, x, rim - 1)].astype(jnp.float32)
+        cells = halo[canonical(core, x, rim - 1)].astype(jnp.float32)
+        pad[x, PAD : PAD + width, :] = jnp.where(info[2] > 0, cells, 0.0)
     fill_columns(pad, edge, taps[1], width)
     for j in range(views):
         first = window_of(info, j, blocks, window)
@@ -360,6 +372,7 @@
         for r in range(rim):
             low = HEADER + r * rows_y
             cells = remote[slot, low : low + rows_y, :].astype(jnp.float32)
+            cells = jnp.where(info[2] > 0, cells, 0.0)
             far[j, rim - 1 - r, pl.ds(PAD + y_there, rows_y), :] = cells
         for r in range(rim):
             pad[j, r] = far[j, r, pl.ds(y_start, rows_y + 2 * PAD), :]
@@ -474,7 +487,7 @@
     group = lax.axis_index("view")
     chips = lax.axis_size("view") // 2
     core, chip = group % 2, group // 2
-    ids = jnp.stack([core, chip]).astype(jnp.int32)
+    ids = jnp.stack([core, chip, has_far(core)]).astype(jnp.int32)
     inner = half + rim
     rows = half // chips
     f32, bf16 = jnp.float32, jnp.bfloat16

time: 47.2 us -> 44.9 us (0.951)
  the two profiles are of different devices: /device:TPU:3 before, /device:TPU:0 now
where the time goes in v6:
time: 44.9 us; the launch traced here: 44.8 us
  Pallas kernels  17.9 us (40%)
  starting transfers between devices  14.2 us (32%)
  waiting for transfers between devices  12.5 us (28%)
    ppermute x6, waiting for transfers between devices, swap_chips(): lax.ppermute(cells, 'view', [(i, i ^ 2 * step) for i in range(count)])  11.5 us
    ppermute x6, starting transfers between devices, swap_chips(): lax.ppermute(cells, 'view', [(i, i ^ 2 * step) for i in range(count)])  8.9 us
    ppermute x2, starting transfers between devices, swap_layers(): return lax.ppermute(cells, ('view', 'blk'), route)  4.22 us
    pallas_call x1, Pallas kernels, local(): call(functools.partial(inner_kernel, taps=taps), 'inner', pltpu.VMEM((vie...  4.14 us
    pallas_call x1, Pallas kernels, local(): call(functools.partial(tables_kernel, taps=taps), 'tables', (pltpu.VMEM((...  2.87 us
    pallas_call x1, Pallas kernels, local(): call(functools.partial(blur_kernel, taps=taps, blocks=blocks), 'blur', (p...  2.77 us
    pallas_call x1, Pallas kernels, local(): call(functools.partial(early_kernel, blocks=blocks), 'early', pltpu.VMEM(...  2.53 us
    pallas_call x1, Pallas kernels, local(): call(functools.partial(correct_kernel, taps=taps, blocks=blocks), 'correc...  2.1 us
  transfers between devices with their start and end apart: 14, of which 7 were waited for; matrix products, arithmetic and copies ran while one was open for 0% of the time, Pallas kernels for 25%

profile of v6, /device:TPU:0, one launch (start us, length us, event | category | flops | bytes accessed | tf_op | source)
XLA Modules:
  0.0 44.8 jit_solution(10533294105354339724)
XLA Ops:
  0.0 0.5 %collective-permute-start.1 = (bf16[16,128,128]{2,1,0:T(8,128)(2,1)}, bf16[16,128,128]{2,1,0:T(8,128)(2,1)S(1)}, u32[]{:S(2)}, u32[]{:S(2)}) collective-permute-start(bf16[16,128,128]{2,1,0:T(8,128)(2,1)} %bitcast.12), channel_id=1, source_target_pairs={{0,4},{4,0},{8,12},{12,8},{16,20},{20,16},{24,28},{28,24},{1,5},{5... | collective-permute-start | bytes 1572872 | tf_op jit(solution)/shard_map/ppermute | solution.py:23
  0.5 1.6 %payload.1 = (bf16[4,128,128]{2,1,0:T(8,128)(2,1)S(1)}, s32[4,8]{1,0:T(4,128)S(1)}, f32[504,25]{1,0:T(8,128)S(1)}) custom-call(s32[3]{0:T(128)S(1)} %pad_add_fusion.ids, s32[4,8]{1,0:T(4,128)} %bitcast.11, f32[504,25]{1,0:T(8,128)} %bitcast.10, f32[16,128,128]{2,1,0:T(8,128)} %est.3), custom_call_target="tpu_custom_call" | custom-call | bytes 65536 | tf_op jit(solution)/shard_map/payload/pallas_call | solution.py:508
  2.1 2.6 %collective-permute-start = (bf16[4,128,128]{2,1,0:T(8,128)(2,1)S(1)}, bf16[4,128,128]{2,1,0:T(8,128)(2,1)S(1)}, u32[]{:S(2)}, u32[]{:S(2)}) collective-permute-start(bf16[4,128,128]{2,1,0:T(8,128)(2,1)S(1)} %get-tuple-element.23), channel_id=1, source_target_pairs={{0,8},{4,1},{1,4},{5,2},{2,5},{6,3},{3,6},{7,15},{8,0},{12,9},{9,1... | collective-permute-start | bytes 393224 | tf_op jit(solution)/shard_map/ppermute | solution.py:43
  4.8 2.9 %tables.1 = (bf16[2,11,896,128]{3,2,1,0:T(8,128)(2,1)S(1)}, bf16[12,128,896]{2,1,0:T(8,128)(2,1)S(1)}, s32[5]{0:T(128)S(1)}, bf16[16,128,128]{2,1,0:T(8,128)(2,1)S(1)}, f32[2,128,128]{2,1,0:T(8,128)S(1)}) custom-call(s32[3]{0:T(128)S(1)} %pad_add_fusion.ids, s32[4,8]{1,0:T(4,128)S(1)} %get-tuple-element.20.cov, f32[504,25]{1,0:T(8,128)S(1)} %get-tuple-element.21.spread, ...), custom_call_target="tpu_custom_call" | custom-call | flops 1585446912 | bytes 65536 | tf_op jit(solution)/shard_map/tables/pallas_call | solution.py:521
  7.7 2.5 %early.1 = f32[2,384,256]{2,1,0:T(8,128)S(1)} custom-call(s32[5]{0:T(128)S(1)} %get-tuple-element.22.info, bf16[12,128,896]{2,1,0:T(8,128)(2,1)S(1)} %get-tuple-element.25.cols, bf16[2,11,896,128]{3,2,1,0:T(8,128)(2,1)S(1)} %get-tuple-element.26.table), custom_call_target="tpu_custom_call" | custom-call | bytes 65536 | tf_op jit(solution)/shard_map/early/pallas_call | solution.py:541
  10.2 2.8 %blur.1 = (bf16[2,8,96,128]{3,2,1,0:T(8,128)(2,1)S(1)}, bf16[2,400,128]{2,1,0:T(8,128)(2,1)S(1)}, bf16[2,4,96,128]{3,2,1,0:T(8,128)(2,1)S(1)}) custom-call(s32[5]{0:T(128)S(1)} %get-tuple-element.22.info, bf16[4,128,128]{2,1,0:T(8,128)(2,1)S(1)} %collective-permute-done.halo, bf16[16,128,128]{2,1,0:T(8,128)(2,1)S(1)} %get-tuple-element.24.img_own, ...), custom_call_target="tpu_custom_call" | custom-call | flops 3170893824 | bytes 65536 | tf_op jit(solution)/shard_map/blur/pallas_call | solution.py:549
  13.1 1.6 %collective-permute-start.2 = (bf16[2,400,128]{2,1,0:T(8,128)(2,1)S(1)}, bf16[2,400,128]{2,1,0:T(8,128)(2,1)S(1)}, u32[]{:S(2)}, u32[]{:S(2)}) collective-permute-start(bf16[2,400,128]{2,1,0:T(8,128)(2,1)S(1)} %get-tuple-element.27), channel_id=1, source_target_pairs={{0,8},{4,1},{1,4},{5,2},{2,5},{6,3},{3,6},{7,15},{8,0},{12,9},{9,1... | collective-permute-start | bytes 614408 | tf_op jit(solution)/shard_map/ppermute | solution.py:43
  14.7 4.1 %inner.1.sums = f32[2,384,256]{2,1,0:T(8,128)S(1)} custom-call(s32[5]{0:T(128)S(1)} %get-tuple-element.22.info, bf16[2,8,96,128]{3,2,1,0:T(8,128)(2,1)S(1)} %get-tuple-element.28.quot, bf16[2,4,96,128]{3,2,1,0:T(8,128)(2,1)S(1)} %collective-permute-done.3.near, bf16[2,11,896,128]{3,2,1,0:T(8,128)(2,1)S(1)} %get-tuple-element.26.table), custom_call_target="tpu_custom_call" | custom-call | flops 3170893824 | bytes 65536 | tf_op jit(solution)/shard_map/inner/pallas_call | solution.py:568
  18.9 2.1 %correct.1 = (f32[2,128,128]{2,1,0:T(8,128)S(1)}, s16[272,128]{1,0:T(8,128)(2,1)S(1)}, s16[272,128]{1,0:T(8,128)(2,1)S(1)}, s16[272,128]{1,0:T(8,128)(2,1)S(1)}) custom-call(s32[5]{0:T(128)S(1)} %get-tuple-element.22.info, bf16[2,400,128]{2,1,0:T(8,128)(2,1)S(1)} %collective-permute-done.2.remote, f32[2,384,256]{2,1,0:T(8,128)S(1)} %inner.1.sums, ...), custom_call_target="tpu_custom_call" | custom-call | flops 792723456 | bytes 65536 | tf_op jit(solution)/shard_map/correct/pallas_call | solution.py:581
  21.0 1.6 %collective-permute-start.4 = (s16[272,128]{1,0:T(8,128)(2,1)S(1)}, s16[272,128]{1,0:T(8,128)(2,1)S(1)}, u32[]{:S(2)}, u32[]{:S(2)}) collective-permute-start(s16[272,128]{1,0:T(8,128)(2,1)S(1)} %get-tuple-element.32), channel_id=1, source_target_pairs={{0,8},{4,12},{8,0},{12,4},{16,24},{20,28},{24,16},{28,20},{1,9},{5... | collective-permute-start | bytes 208904 | tf_op jit(solution)/shard_map/ppermute | solution.py:28
  22.6 2.6 %collective-permute-start.5 = (s16[272,128]{1,0:T(8,128)(2,1)S(1)}, s16[272,128]{1,0:T(8,128)(2,1)S(1)}, u32[]{:S(2)}, u32[]{:S(2)}) collective-permute-start(s16[272,128]{1,0:T(8,128)(2,1)S(1)} %get-tuple-element.33), channel_id=1, source_target_pairs={{0,16},{4,20},{8,24},{12,28},{16,0},{20,4},{24,8},{28,12},{1,17},{... | collective-permute-start | bytes 208904 | tf_op jit(solution)/shard_map/ppermute | solution.py:28
  25.2 0.3 collective-permute-start.6
  25.4 4.5 %collective-permute-done.5.rest_1_ = s16[272,128]{1,0:T(8,128)(2,1)S(1)} collective-permute-done((s16[272,128]{1,0:T(8,128)(2,1)S(1)}, s16[272,128]{1,0:T(8,128)(2,1)S(1)}, u32[]{:S(2)}, u32[]{:S(2)}) %collective-permute-start.5) | collective-permute-done | bytes 69664 | tf_op jit(solution)/shard_map/ppermute | solution.py:28
  29.9 1.6 %collective-permute-done.6.rest_2_ = s16[272,128]{1,0:T(8,128)(2,1)S(1)} collective-permute-done((s16[272,128]{1,0:T(8,128)(2,1)S(1)}, s16[272,128]{1,0:T(8,128)(2,1)S(1)}, u32[]{:S(2)}, u32[]{:S(2)}) %collective-permute-start.6) | collective-permute-done | bytes 69664 | tf_op jit(solution)/shard_map/ppermute | solution.py:28
  31.6 0.3 combine.1.rest_0_
  31.9 2.2 %collective-permute-start.9 = (s16[272,128]{1,0:T(8,128)(2,1)S(1)}, s16[272,128]{1,0:T(8,128)(2,1)S(1)}, u32[]{:S(2)}, u32[]{:S(2)}) collective-permute-start(s16[272,128]{1,0:T(8,128)(2,1)S(1)} %combine.1.rest_0_), channel_id=1, source_target_pairs={{0,24},{4,28},{8,16},{12,20},{16,8},{20,12},{24,0},{28,4},{1,25},{... | collective-permute-start | bytes 208904 | tf_op jit(solution)/shard_map/ppermute | solution.py:28
  34.0 1.2 %collective-permute-start.8 = (s16[272,128]{1,0:T(8,128)(2,1)S(1)}, s16[272,128]{1,0:T(8,128)(2,1)S(1)}, u32[]{:S(2)}, u32[]{:S(2)}) collective-permute-start(s16[272,128]{1,0:T(8,128)(2,1)S(1)} %combine.1.rest_0_), channel_id=1, source_target_pairs={{0,16},{4,20},{8,24},{12,28},{16,0},{20,4},{24,8},{28,12},{1,17},{... | collective-permute-start | bytes 208904 | tf_op jit(solution)/shard_map/ppermute | solution.py:28
  35.2 1.1 %collective-permute-start.7 = (s16[272,128]{1,0:T(8,128)(2,1)S(1)}, s16[272,128]{1,0:T(8,128)(2,1)S(1)}, u32[]{:S(2)}, u32[]{:S(2)}) collective-permute-start(s16[272,128]{1,0:T(8,128)(2,1)S(1)} %combine.1.rest_0_), channel_id=1, source_target_pairs={{0,8},{4,12},{8,0},{12,4},{16,24},{20,28},{24,16},{28,20},{1,9},{5... | collective-permute-start | bytes 208904 | tf_op jit(solution)/shard_map/ppermute | solution.py:28
  36.3 1.9 %collective-permute-done.9.rest_3_ = s16[272,128]{1,0:T(8,128)(2,1)S(1)} collective-permute-done((s16[272,128]{1,0:T(8,128)(2,1)S(1)}, s16[272,128]{1,0:T(8,128)(2,1)S(1)}, u32[]{:S(2)}, u32[]{:S(2)}) %collective-permute-start.9) | collective-permute-done | bytes 69664 | tf_op jit(solution)/shard_map/ppermute | solution.py:28
  38.2 3.5 %collective-permute-done.8.rest_2_ = s16[272,128]{1,0:T(8,128)(2,1)S(1)} collective-permute-done((s16[272,128]{1,0:T(8,128)(2,1)S(1)}, s16[272,128]{1,0:T(8,128)(2,1)S(1)}, u32[]{:S(2)}, u32[]{:S(2)}) %collective-permute-start.8) | collective-permute-done | bytes 69664 | tf_op jit(solution)/shard_map/ppermute | solution.py:28
  41.7 0.5 %collective-permute-start.11 = (s16[272,128]{1,0:T(8,128)(2,1)S(1)}, s16[272,128]{1,0:T(8,128)(2,1)S(1)}, u32[]{:S(2)}, u32[]{:S(2)}) collective-permute-start(s16[272,128]{1,0:T(8,128)(2,1)S(1)} %collective-permute-done.7.rest_1_), channel_id=1, source_target_pairs={{0,4},{4,0},{8,12},{12,8},{16,20},{20,16},{24,28},{28,24},{1,5},{5... | collective-permute-start | bytes 208904 | tf_op jit(solution)/shard_map/ppermute | solution.py:23
  42.2 0.7 %collective-permute-done.12.rest_6_ = s16[272,128]{1,0:T(8,128)(2,1)S(1)} collective-permute-done((s16[272,128]{1,0:T(8,128)(2,1)S(1)}, s16[272,128]{1,0:T(8,128)(2,1)S(1)}, u32[]{:S(2)}, u32[]{:S(2)}) %collective-permute-start.12) | collective-permute-done | bytes 69664 | tf_op jit(solution)/shard_map/ppermute | solution.py:23
  43.0 0.2 collective-permute-done.11.rest_5_
  43.1 1.6 %gather.1 = f32[16,128,128]{2,1,0:T(8,128)} custom-call(s32[3]{0:T(128)S(1)} %pad_add_fusion.ids, s16[272,128]{1,0:T(8,128)(2,1)S(1)} %combine.1.rest_0_, s16[272,128]{1,0:T(8,128)(2,1)S(1)} %collective-permute-done.7.rest_1_, s16[272,128]{1,0:T(8,128)(2,1)S(1)} %collective-permute-done.8.rest_2_, s16[272,128]{1,0:T(8,128)(2,1)S(1)} %collective-permute-done.9.rest_3_, ...), custom_call_target="tpu_custom_call" | custom-call | bytes 65536 | tf_op jit(solution)/shard_map/gather/pallas_call | solution.py:604
  (13 shorter events, 0.3 us)
Async XLA Ops:
  0.0 10.2 %collective-permute-start.1 = (bf16[16,128,128]{2,1,0:T(8,128)(2,1)}, bf16[16,128,128]{2,1,0:T(8,128)(2,1)S(1)}, u32[]{:S(2)}, u32[]{:S(2)}) collective-permute-start(bf16[16,128,128]{2,1,0:T(8,128)(2,1)} %bitcast.12), channel_id=1, source_target_pairs={{0,4},{4,0},{8,12},{12,8},{16,20},{20,16},{24,28},{28,24},{1,5},{5... | collective-permute-start | bytes 1572872 | tf_op jit(solution)/shard_map/ppermute | solution.py:23
  2.1 8.1 %collective-permute-start = (bf16[4,128,128]{2,1,0:T(8,128)(2,1)S(1)}, bf16[4,128,128]{2,1,0:T(8,128)(2,1)S(1)}, u32[]{:S(2)}, u32[]{:S(2)}) collective-permute-start(bf16[4,128,128]{2,1,0:T(8,128)(2,1)S(1)} %get-tuple-element.23), channel_id=1, source_target_pairs={{0,8},{4,1},{1,4},{5,2},{2,5},{6,3},{3,6},{7,15},{8,0},{12,9},{9,1... | collective-permute-start | bytes 393224 | tf_op jit(solution)/shard_map/ppermute | solution.py:43
  13.0 1.7 %collective-permute-start.3 = (bf16[2,4,96,128]{3,2,1,0:T(8,128)(2,1)S(1)}, bf16[2,4,96,128]{3,2,1,0:T(8,128)(2,1)S(1)}, u32[]{:S(2)}, u32[]{:S(2)}) collective-permute-start(bf16[2,4,96,128]{3,2,1,0:T(8,128)(2,1)S(1)} %get-tuple-element.29), channel_id=1, source_target_pairs={{0,4},{4,0},{8,12},{12,8},{16,20},{20,16},{24,28},{28,24},{1,5},{5... | collective-permute-start | bytes 589832 | tf_op jit(solution)/shard_map/ppermute | solution.py:23
  13.1 5.8 %collective-permute-start.2 = (bf16[2,400,128]{2,1,0:T(8,128)(2,1)S(1)}, bf16[2,400,128]{2,1,0:T(8,128)(2,1)S(1)}, u32[]{:S(2)}, u32[]{:S(2)}) collective-permute-start(bf16[2,400,128]{2,1,0:T(8,128)(2,1)S(1)} %get-tuple-element.27), channel_id=1, source_target_pairs={{0,8},{4,1},{1,4},{5,2},{2,5},{6,3},{3,6},{7,15},{8,0},{12,9},{9,1... | collective-permute-start | bytes 614408 | tf_op jit(solution)/shard_map/ppermute | solution.py:43
  21.0 4.5 %collective-permute-start.4 = (s16[272,128]{1,0:T(8,128)(2,1)S(1)}, s16[272,128]{1,0:T(8,128)(2,1)S(1)}, u32[]{:S(2)}, u32[]{:S(2)}) collective-permute-start(s16[272,128]{1,0:T(8,128)(2,1)S(1)} %get-tuple-element.32), channel_id=1, source_target_pairs={{0,8},{4,12},{8,0},{12,4},{16,24},{20,28},{24,16},{28,20},{1,9},{5... | collective-permute-start | bytes 208904 | tf_op jit(solution)/shard_map/ppermute | solution.py:28
  22.6 7.3 %collective-permute-start.5 = (s16[272,128]{1,0:T(8,128)(2,1)S(1)}, s16[272,128]{1,0:T(8,128)(2,1)S(1)}, u32[]{:S(2)}, u32[]{:S(2)}) collective-permute-start(s16[272,128]{1,0:T(8,128)(2,1)S(1)} %get-tuple-element.33), channel_id=1, source_target_pairs={{0,16},{4,20},{8,24},{12,28},{16,0},{20,4},{24,8},{28,12},{1,17},{... | collective-permute-start | bytes 208904 | tf_op jit(solution)/shard_map/ppermute | solution.py:28
  25.2 6.4 %collective-permute-start.6 = (s16[272,128]{1,0:T(8,128)(2,1)S(1)}, s16[272,128]{1,0:T(8,128)(2,1)S(1)}, u32[]{:S(2)}, u32[]{:S(2)}) collective-permute-start(s16[272,128]{1,0:T(8,128)(2,1)S(1)} %get-tuple-element.34), channel_id=1, source_target_pairs={{0,24},{4,28},{8,16},{12,20},{16,8},{20,12},{24,0},{28,4},{1,25},{... | collective-permute-start | bytes 208904 | tf_op jit(solution)/shard_map/ppermute | solution.py:28
  31.9 6.3 %collective-permute-start.9 = (s16[272,128]{1,0:T(8,128)(2,1)S(1)}, s16[272,128]{1,0:T(8,128)(2,1)S(1)}, u32[]{:S(2)}, u32[]{:S(2)}) collective-permute-start(s16[272,128]{1,0:T(8,128)(2,1)S(1)} %combine.1.rest_0_), channel_id=1, source_target_pairs={{0,24},{4,28},{8,16},{12,20},{16,8},{20,12},{24,0},{28,4},{1,25},{... | collective-permute-start | bytes 208904 | tf_op jit(solution)/shard_map/ppermute | solution.py:28
  34.0 7.7 %collective-permute-start.8 = (s16[272,128]{1,0:T(8,128)(2,1)S(1)}, s16[272,128]{1,0:T(8,128)(2,1)S(1)}, u32[]{:S(2)}, u32[]{:S(2)}) collective-permute-start(s16[272,128]{1,0:T(8,128)(2,1)S(1)} %combine.1.rest_0_), channel_id=1, source_target_pairs={{0,16},{4,20},{8,24},{12,28},{16,0},{20,4},{24,8},{28,12},{1,17},{... | collective-permute-start | bytes 208904 | tf_op jit(solution)/shard_map/ppermute | solution.py:28
  35.2 6.5 %collective-permute-start.7 = (s16[272,128]{1,0:T(8,128)(2,1)S(1)}, s16[272,128]{1,0:T(8,128)(2,1)S(1)}, u32[]{:S(2)}, u32[]{:S(2)}) collective-permute-start(s16[272,128]{1,0:T(8,128)(2,1)S(1)} %combine.1.rest_0_), channel_id=1, source_target_pairs={{0,8},{4,12},{8,0},{12,4},{16,24},{20,28},{24,16},{28,20},{1,9},{5... | collective-permute-start | bytes 208904 | tf_op jit(solution)/shard_map/ppermute | solution.py:28
  36.3 5.9 %collective-permute-start.10 = (s16[272,128]{1,0:T(8,128)(2,1)S(1)}, s16[272,128]{1,0:T(8,128)(2,1)S(1)}, u32[]{:S(2)}, u32[]{:S(2)}) collective-permute-start(s16[272,128]{1,0:T(8,128)(2,1)S(1)} %combine.1.rest_0_), channel_id=1, source_target_pairs={{0,4},{4,0},{8,12},{12,8},{16,20},{20,16},{24,28},{28,24},{1,5},{5... | collective-permute-start | bytes 208904 | tf_op jit(solution)/shard_map/ppermute | solution.py:23
  38.2 4.0 %collective-permute-start.13 = (s16[272,128]{1,0:T(8,128)(2,1)S(1)}, s16[272,128]{1,0:T(8,128)(2,1)S(1)}, u32[]{:S(2)}, u32[]{:S(2)}) collective-permute-start(s16[272,128]{1,0:T(8,128)(2,1)S(1)} %collective-permute-done.9.rest_3_), channel_id=1, source_target_pairs={{0,4},{4,0},{8,12},{12,8},{16,20},{20,16},{24,28},{28,24},{1,5},{5... | collective-permute-start | bytes 208904 | tf_op jit(solution)/shard_map/ppermute | solution.py:23
  41.7 1.3 %collective-permute-start.12 = (s16[272,128]{1,0:T(8,128)(2,1)S(1)}, s16[272,128]{1,0:T(8,128)(2,1)S(1)}, u32[]{:S(2)}, u32[]{:S(2)}) collective-permute-start(s16[272,128]{1,0:T(8,128)(2,1)S(1)} %collective-permute-done.8.rest_2_), channel_id=1, source_target_pairs={{0,4},{4,0},{8,12},{12,8},{16,20},{20,16},{24,28},{28,24},{1,5},{5... | collective-permute-start | bytes 208904 | tf_op jit(solution)/shard_map/ppermute | solution.py:23
  41.7 1.4 %collective-permute-start.11 = (s16[272,128]{1,0:T(8,128)(2,1)S(1)}, s16[272,128]{1,0:T(8,128)(2,1)S(1)}, u32[]{:S(2)}, u32[]{:S(2)}) collective-permute-start(s16[272,128]{1,0:T(8,128)(2,1)S(1)} %collective-permute-done.7.rest_1_), channel_id=1, source_target_pairs={{0,4},{4,0},{8,12},{12,8},{16,20},{20,16},{24,28},{28,24},{1,5},{5... | collective-permute-start | bytes 208904 | tf_op jit(solution)/shard_map/ppermute | solution.py:23

commit v7 on v6

--- a/solution.py
+++ b/solution.py
@@ -122,7 +122,23 @@
 
 
 def tables_kernel(
-    ids, cov, spread, est, images, table, cols, info, img_own, est_own, rows, pad, sems, *, taps
+    ids,
+    cov,
+    spread,
+    est,
+    images,
+    table,
+    cols,
+    info,
+    img_own,
+    est_own,
+    sums,
+    rows,
+    pad,
+    sems,
+    *,
+    taps,
+    blocks,
 ):
     taps_x, taps_y, taps_z = taps
     core, chip = ids[0], ids[1]
@@ -148,7 +164,6 @@
     at = row - rim_z
     place = ((col == at) | (col == at + depth)) & (row < taps_z)
     place = jnp.where(place, 1.0, 0.0).astype(jnp.bfloat16)
-    zero = jnp.zeros((taps_y * depth, depth), jnp.bfloat16)
     rows[...] = jnp.zeros(rows.shape, jnp.float32)
     total_views = spread.shape[0] // (taps_x * taps_y)
     info[0] = core
@@ -161,8 +176,6 @@
         view = chip * views + view_slot(core, j, views)
         code = jnp.sum(jnp.where(lane == view, bits, 0).astype(jnp.float32))
         info[MARKS + j] = code.astype(jnp.int32)
-        table[j, 0] = zero
-        table[j, taps_x + 1] = zero
         taps_all = spread[pl.ds(view, taps_x * taps_y, stride=total_views), :]
         rows[j, : taps_x * taps_y, :taps_z] = taps_all
         weights = rows[j]
@@ -177,7 +190,7 @@
                 line = jnp.broadcast_to(line, (depth, depth))
                 line = pltpu.roll(line, 0, 1, stride=1, stride_axis=0)
                 line = jnp.where(band, line, 0.0).astype(jnp.bfloat16)
-                table[j, a + 1, b * depth : (b + 1) * depth, :] = line
+                table[j, a, b * depth : (b + 1) * depth, :] = line
         return carry
 
     lax.fori_loop(0, taps_x, fill, 0, unroll=3)
@@ -186,6 +199,18 @@
     fill_columns(pad, cols, taps_y, width)
     for r in range(est_own.shape[0]):
         est_own[r] = pad[chip * est_own.shape[0] + r, PAD : PAD + width, :]
+    rim = count // 3
+    rows_y = sums.shape[1] // rim
+    for j in range(views):
+        first = window_of(info, j, blocks, rows_y // (width // blocks))
+        y_start = pl.multiple_of(first * (width // blocks), width // blocks)
+        total = None
+        for s in early_steps(j, rim, (taps_x + 1) // 2):
+            part = dot_turned(
+                lambda x: cols[x - rim, pl.ds(y_start, rows_y), :], range(rim), table, j, s
+            )
+            total = part if total is None else total + part
+        sums[j] = total
 
 
 def fill_columns(pad, cols, taps_y, rows_y):
@@ -205,26 +230,30 @@
 
 
 def right_side(table, j, s):
+    taps_x = table.shape[1]
+
+    def block(at):
+        return table[j, at] if 0 <= at < taps_x else jnp.zeros(table.shape[2:], table.dtype)
+
     return jnp.concatenate(
-        [
-            jnp.concatenate([table[j, 2 * s + u + 1], table[j, 2 * s + u]], axis=1)
-            for u in range(2)
-        ],
+        [jnp.concatenate([block(2 * s + u), block(2 * s + u - 1)], axis=1) for u in range(2)],
         axis=0,
     )
 
 
 def right_side_turned(table, j, s):
-    taps_x = table.shape[1] - 2
+    taps_x = table.shape[1]
     taps_y = table.shape[2] // LANES
     lines = []
     for w in range(2):
         line = []
         for u in range(2):
-            at = taps_x - 1 - (2 * s + u - w) + 1
-            for b in range(taps_y):
-                low = (taps_y - 1 - b) * LANES
-                line.append(table[j, at, low : low + LANES, :])
+            at = taps_x - 1 - (2 * s + u - w)
+            for b in range(taps_y - 1, -1, -1):
+                if 0 <= at < taps_x:
+                    line.append(table[j, at, b * LANES : (b + 1) * LANES, :])
+                else:
+                    line.append(jnp.zeros((LANES, LANES), table.dtype))
         lines.append(jnp.concatenate(line, axis=1))
     return jnp.concatenate(lines, axis=0)
 
@@ -248,25 +277,6 @@
 
 def early_steps(j, rim, steps):
     return range(rim // 2 + j, steps)
-
-
-def early_kernel(info, cols, table, sums, *, blocks):
-    views, steps = table.shape[0], (table.shape[1] - 1) // 2
-    pairs = cols.shape[0] // 3
-    rim = cols.shape[0] // 3
-    width = cols.shape[1]
-    rows_y = sums.shape[1] // pairs
-    block_width = width // blocks
-    for j in range(views):
-        first = window_of(info, j, blocks, rows_y // block_width)
-        y_start = pl.multiple_of(first * block_width, block_width)
-        total = None
-        for s in early_steps(j, rim, steps):
-            part = dot_turned(
-                lambda x: cols[x - rim, pl.ds(y_start, rows_y), :], range(pairs), table, j, s
-            )
-            total = part if total is None else total + part
-        sums[j] = total
 
 
 def blur_kernel(
@@ -327,7 +337,7 @@
     views, half, rows_y, depth = quot.shape
     rim = near.shape[1]
     pairs = half // 2
-    steps = (table.shape[1] - 1) // 2
+    steps = (table.shape[1] + 1) // 2
     margin = jnp.zeros((half + rim, PAD, depth), jnp.float32)
     for j in range(views):
         pad[j, :, :PAD, :] = margin
@@ -518,15 +528,16 @@
     )(ids, cov, spread, estimate)
     halo = swap_layers(edge)
 
-    table, cols, info, img_own, est_own = call(
-        functools.partial(tables_kernel, taps=taps),
+    table, cols, info, img_own, est_own, early = call(
+        functools.partial(tables_kernel, taps=taps, blocks=blocks),
         "tables",
         (
-            pltpu.VMEM((views, taps_x + 2, deep, depth), bf16),
+            pltpu.VMEM((views, taps_x, deep, depth), bf16),
             pltpu.VMEM((inner, width, deep), bf16),
             shape((MARKS + views,), jnp.int32),
             pltpu.VMEM((slab_x, share_w, depth), bf16),
             pltpu.VMEM((rows, width, depth), f32),
+            pltpu.VMEM((views, half // 2 * rows_y, 2 * depth), f32),
         ),
         "svvhh",
         [
@@ -535,16 +546,8 @@
             sems((inner + 1,)),
         ],
         work // 2,
-        "vvsvv",
+        "vvsvvv",
     )(ids, cov, spread, estimate, images)
-
-    early = call(
-        functools.partial(early_kernel, blocks=blocks),
-        "early",
-        pltpu.VMEM((views, half // 2 * rows_y, 2 * depth), f32),
-        "svv",
-        flops=0,
-    )(info, cols, table)
 
     quot, remote, near = call(
         functools.partial(blur_kernel, taps=taps, blocks=blocks),

time: 44.9 us -> 44.2 us (0.984)
  Pallas kernels: 17.9 us -> 17.2 us
    pallas_call x2 -> x1, Pallas kernels: 5.39 us -> 4.73 us  [local(): call(functools.partial(tables_kernel, taps=taps, blocks=blocks), 'tables'...]
  transfers between devices with their start and end apart: 14 -> 14, of which waited for: 7 -> 7; matrix products, arithmetic and copies ran while one was open for 0% -> 0% of each run, Pallas kernels for 25% -> 24%
where the time goes in v7:
time: 44.2 us; the launch traced here: 44.1 us
  Pallas kernels  17.2 us (39%)
  starting transfers between devices  14.2 us (32%)
  waiting for transfers between devices  12.5 us (28%)
    ppermute x6, waiting for transfers between devices, swap_chips(): lax.ppermute(cells, 'view', [(i, i ^ 2 * step) for i in range(count)])  11.5 us
    ppermute x6, starting transfers between devices, swap_chips(): lax.ppermute(cells, 'view', [(i, i ^ 2 * step) for i in range(count)])  8.9 us
    pallas_call x1, Pallas kernels, local(): call(functools.partial(tables_kernel, taps=taps, blocks=blocks), 'tables'...  4.73 us
    ppermute x2, starting transfers between devices, swap_layers(): return lax.ppermute(cells, ('view', 'blk'), route)  4.24 us
    pallas_call x1, Pallas kernels, local(): call(functools.partial(inner_kernel, taps=taps), 'inner', pltpu.VMEM((vie...  4.05 us
    pallas_call x1, Pallas kernels, local(): call(functools.partial(blur_kernel, taps=taps, blocks=blocks), 'blur', (p...  2.73 us
    pallas_call x1, Pallas kernels, local(): call(functools.partial(correct_kernel, taps=taps, blocks=blocks), 'correc...  2.15 us
    pallas_call x1, Pallas kernels, local(): call(gather_kernel, 'gather', shape(estimate.shape, f32), 's' + 'v' * (2...  1.65 us
  transfers between devices with their start and end apart: 14, of which 7 were waited for; matrix products, arithmetic and copies ran while one was open for 0% of the time, Pallas kernels for 24%

profile of v7, /device:TPU:0, one launch (start us, length us, event | category | flops | bytes accessed | tf_op | source)
XLA Modules:
  0.0 44.1 jit_solution(4529945619099141834)
XLA Ops:
  0.0 0.5 %collective-permute-start.1 = (bf16[16,128,128]{2,1,0:T(8,128)(2,1)}, bf16[16,128,128]{2,1,0:T(8,128)(2,1)S(1)}, u32[]{:S(2)}, u32[]{:S(2)}) collective-permute-start(bf16[16,128,128]{2,1,0:T(8,128)(2,1)} %bitcast.12), channel_id=1, source_target_pairs={{0,4},{4,0},{8,12},{12,8},{16,20},{20,16},{24,28},{28,24},{1,5},{5... | collective-permute-start | bytes 1572872 | tf_op jit(solution)/shard_map/ppermute | solution.py:23
  0.5 1.6 %payload.1 = (bf16[4,128,128]{2,1,0:T(8,128)(2,1)S(1)}, s32[4,8]{1,0:T(4,128)S(1)}, f32[504,25]{1,0:T(8,128)S(1)}) custom-call(s32[3]{0:T(128)S(1)} %pad_add_fusion.ids, s32[4,8]{1,0:T(4,128)} %bitcast.11, f32[504,25]{1,0:T(8,128)} %bitcast.10, f32[16,128,128]{2,1,0:T(8,128)} %est.3), custom_call_target="tpu_custom_call" | custom-call | bytes 65536 | tf_op jit(solution)/shard_map/payload/pallas_call | solution.py:518
  2.1 2.6 %collective-permute-start = (bf16[4,128,128]{2,1,0:T(8,128)(2,1)S(1)}, bf16[4,128,128]{2,1,0:T(8,128)(2,1)S(1)}, u32[]{:S(2)}, u32[]{:S(2)}) collective-permute-start(bf16[4,128,128]{2,1,0:T(8,128)(2,1)S(1)} %get-tuple-element.24), channel_id=1, source_target_pairs={{0,8},{4,1},{1,4},{5,2},{2,5},{6,3},{3,6},{7,15},{8,0},{12,9},{9,1... | collective-permute-start | bytes 393224 | tf_op jit(solution)/shard_map/ppermute | solution.py:43
  4.8 4.7 %tables.1 = (bf16[2,9,896,128]{3,2,1,0:T(8,128)(2,1)S(1)}, bf16[12,128,896]{2,1,0:T(8,128)(2,1)S(1)}, s32[5]{0:T(128)S(1)}, bf16[16,128,128]{2,1,0:T(8,128)(2,1)...) custom-call(s32[3]{0:T(128)S(1)} %pad_add_fusion.ids, s32[4,8]{1,0:T(4,128)S(1)} %get-tuple-element.21.cov, ...), custom_call_target="tpu_custom_call" | custom-call | flops 1585446912 | bytes 65536 | tf_op jit(solution)/shard_map/tables/pallas_call | solution.py:531
  9.5 2.7 %blur.1 = (bf16[2,8,96,128]{3,2,1,0:T(8,128)(2,1)S(1)}, bf16[2,400,128]{2,1,0:T(8,128)(2,1)S(1)}, bf16[2,4,96,128]{3,2,1,0:T(8,128)(2,1)S(1)}) custom-call(s32[5]{0:T(128)S(1)} %get-tuple-element.23.info, bf16[4,128,128]{2,1,0:T(8,128)(2,1)S(1)} %collective-permute-done.halo, bf16[16,128,128]{2,1,0:T(8,128)(2,1)S(1)} %get-tuple-element.25.img_own, ...), custom_call_target="tpu_custom_call" | custom-call | flops 3170893824 | bytes 65536 | tf_op jit(solution)/shard_map/blur/pallas_call | solution.py:552
  12.4 1.6 %collective-permute-start.2 = (bf16[2,400,128]{2,1,0:T(8,128)(2,1)S(1)}, bf16[2,400,128]{2,1,0:T(8,128)(2,1)S(1)}, u32[]{:S(2)}, u32[]{:S(2)}) collective-permute-start(bf16[2,400,128]{2,1,0:T(8,128)(2,1)S(1)} %get-tuple-element.29), channel_id=1, source_target_pairs={{0,8},{4,1},{1,4},{5,2},{2,5},{6,3},{3,6},{7,15},{8,0},{12,9},{9,1... | collective-permute-start | bytes 614408 | tf_op jit(solution)/shard_map/ppermute | solution.py:43
  14.0 4.1 %inner.1.sums = f32[2,384,256]{2,1,0:T(8,128)S(1)} custom-call(s32[5]{0:T(128)S(1)} %get-tuple-element.23.info, bf16[2,8,96,128]{3,2,1,0:T(8,128)(2,1)S(1)} %get-tuple-element.30.quot, bf16[2,4,96,128]{3,2,1,0:T(8,128)(2,1)S(1)} %collective-permute-done.3.near, bf16[2,9,896,128]{3,2,1,0:T(8,128)(2,1)S(1)} %get-tuple-element.27.table), custom_call_target="tpu_custom_call" | custom-call | flops 3170893824 | bytes 65536 | tf_op jit(solution)/shard_map/inner/pallas_call | solution.py:571
  18.0 0.1 collective-permute-done.2.remote
  18.2 2.1 %correct.1 = (f32[2,128,128]{2,1,0:T(8,128)S(1)}, s16[272,128]{1,0:T(8,128)(2,1)S(1)}, s16[272,128]{1,0:T(8,128)(2,1)S(1)}, s16[272,128]{1,0:T(8,128)(2,1)S(1)}) custom-call(s32[5]{0:T(128)S(1)} %get-tuple-element.23.info, bf16[2,400,128]{2,1,0:T(8,128)(2,1)S(1)} %collective-permute-done.2.remote, f32[2,384,256]{2,1,0:T(8,128)S(1)} %inner.1.sums, ...), custom_call_target="tpu_custom_call" | custom-call | flops 792723456 | bytes 65536 | tf_op jit(solution)/shard_map/correct/pallas_call | solution.py:584
  20.3 1.6 %collective-permute-start.4 = (s16[272,128]{1,0:T(8,128)(2,1)S(1)}, s16[272,128]{1,0:T(8,128)(2,1)S(1)}, u32[]{:S(2)}, u32[]{:S(2)}) collective-permute-start(s16[272,128]{1,0:T(8,128)(2,1)S(1)} %get-tuple-element.34), channel_id=1, source_target_pairs={{0,8},{4,12},{8,0},{12,4},{16,24},{20,28},{24,16},{28,20},{1,9},{5... | collective-permute-start | bytes 208904 | tf_op jit(solution)/shard_map/ppermute | solution.py:28
  21.9 2.6 %collective-permute-start.5 = (s16[272,128]{1,0:T(8,128)(2,1)S(1)}, s16[272,128]{1,0:T(8,128)(2,1)S(1)}, u32[]{:S(2)}, u32[]{:S(2)}) collective-permute-start(s16[272,128]{1,0:T(8,128)(2,1)S(1)} %get-tuple-element.35), channel_id=1, source_target_pairs={{0,16},{4,20},{8,24},{12,28},{16,0},{20,4},{24,8},{28,12},{1,17},{... | collective-permute-start | bytes 208904 | tf_op jit(solution)/shard_map/ppermute | solution.py:28
  24.5 0.2 collective-permute-start.6
  24.8 3.5 %collective-permute-done.5.rest_1_ = s16[272,128]{1,0:T(8,128)(2,1)S(1)} collective-permute-done((s16[272,128]{1,0:T(8,128)(2,1)S(1)}, s16[272,128]{1,0:T(8,128)(2,1)S(1)}, u32[]{:S(2)}, u32[]{:S(2)}) %collective-permute-start.5) | collective-permute-done | bytes 69664 | tf_op jit(solution)/shard_map/ppermute | solution.py:28
  28.2 2.6 %collective-permute-done.6.rest_2_ = s16[272,128]{1,0:T(8,128)(2,1)S(1)} collective-permute-done((s16[272,128]{1,0:T(8,128)(2,1)S(1)}, s16[272,128]{1,0:T(8,128)(2,1)S(1)}, u32[]{:S(2)}, u32[]{:S(2)}) %collective-permute-start.6) | collective-permute-done | bytes 69664 | tf_op jit(solution)/shard_map/ppermute | solution.py:28
  30.8 0.3 combine.1.rest_0_
  31.1 2.3 %collective-permute-start.9 = (s16[272,128]{1,0:T(8,128)(2,1)S(1)}, s16[272,128]{1,0:T(8,128)(2,1)S(1)}, u32[]{:S(2)}, u32[]{:S(2)}) collective-permute-start(s16[272,128]{1,0:T(8,128)(2,1)S(1)} %combine.1.rest_0_), channel_id=1, source_target_pairs={{0,24},{4,28},{8,16},{12,20},{16,8},{20,12},{24,0},{28,4},{1,25},{... | collective-permute-start | bytes 208904 | tf_op jit(solution)/shard_map/ppermute | solution.py:28
  33.4 1.0 %collective-permute-start.8 = (s16[272,128]{1,0:T(8,128)(2,1)S(1)}, s16[272,128]{1,0:T(8,128)(2,1)S(1)}, u32[]{:S(2)}, u32[]{:S(2)}) collective-permute-start(s16[272,128]{1,0:T(8,128)(2,1)S(1)} %combine.1.rest_0_), channel_id=1, source_target_pairs={{0,16},{4,20},{8,24},{12,28},{16,0},{20,4},{24,8},{28,12},{1,17},{... | collective-permute-start | bytes 208904 | tf_op jit(solution)/shard_map/ppermute | solution.py:28
  34.4 1.2 %collective-permute-start.7 = (s16[272,128]{1,0:T(8,128)(2,1)S(1)}, s16[272,128]{1,0:T(8,128)(2,1)S(1)}, u32[]{:S(2)}, u32[]{:S(2)}) collective-permute-start(s16[272,128]{1,0:T(8,128)(2,1)S(1)} %combine.1.rest_0_), channel_id=1, source_target_pairs={{0,8},{4,12},{8,0},{12,4},{16,24},{20,28},{24,16},{28,20},{1,9},{5... | collective-permute-start | bytes 208904 | tf_op jit(solution)/shard_map/ppermute | solution.py:28
  35.6 1.9 %collective-permute-done.9.rest_3_ = s16[272,128]{1,0:T(8,128)(2,1)S(1)} collective-permute-done((s16[272,128]{1,0:T(8,128)(2,1)S(1)}, s16[272,128]{1,0:T(8,128)(2,1)S(1)}, u32[]{:S(2)}, u32[]{:S(2)}) %collective-permute-start.9) | collective-permute-done | bytes 69664 | tf_op jit(solution)/shard_map/ppermute | solution.py:28
  37.5 3.5 %collective-permute-done.8.rest_2_ = s16[272,128]{1,0:T(8,128)(2,1)S(1)} collective-permute-done((s16[272,128]{1,0:T(8,128)(2,1)S(1)}, s16[272,128]{1,0:T(8,128)(2,1)S(1)}, u32[]{:S(2)}, u32[]{:S(2)}) %collective-permute-start.8) | collective-permute-done | bytes 69664 | tf_op jit(solution)/shard_map/ppermute | solution.py:28
  41.0 0.5 %collective-permute-start.11 = (s16[272,128]{1,0:T(8,128)(2,1)S(1)}, s16[272,128]{1,0:T(8,128)(2,1)S(1)}, u32[]{:S(2)}, u32[]{:S(2)}) collective-permute-start(s16[272,128]{1,0:T(8,128)(2,1)S(1)} %collective-permute-done.7.rest_1_), channel_id=1, source_target_pairs={{0,4},{4,0},{8,12},{12,8},{16,20},{20,16},{24,28},{28,24},{1,5},{5... | collective-permute-start | bytes 208904 | tf_op jit(solution)/shard_map/ppermute | solution.py:23
  41.5 0.7 %collective-permute-done.12.rest_6_ = s16[272,128]{1,0:T(8,128)(2,1)S(1)} collective-permute-done((s16[272,128]{1,0:T(8,128)(2,1)S(1)}, s16[272,128]{1,0:T(8,128)(2,1)S(1)}, u32[]{:S(2)}, u32[]{:S(2)}) %collective-permute-start.12) | collective-permute-done | bytes 69664 | tf_op jit(solution)/shard_map/ppermute | solution.py:23
  42.3 0.2 collective-permute-done.11.rest_5_
  42.4 1.6 %gather.1 = f32[16,128,128]{2,1,0:T(8,128)} custom-call(s32[3]{0:T(128)S(1)} %pad_add_fusion.ids, s16[272,128]{1,0:T(8,128)(2,1)S(1)} %combine.1.rest_0_, s16[272,128]{1,0:T(8,128)(2,1)S(1)} %collective-permute-done.7.rest_1_, s16[272,128]{1,0:T(8,128)(2,1)S(1)} %collective-permute-done.8.rest_2_, s16[272,128]{1,0:T(8,128)(2,1)S(1)} %collective-permute-done.9.rest_3_, ...), custom_call_target="tpu_custom_call" | custom-call | bytes 65536 | tf_op jit(solution)/shard_map/gather/pallas_call | solution.py:607
  (12 shorter events, 0.2 us)
Async XLA Ops:
  0.0 9.5 %collective-permute-start.1 = (bf16[16,128,128]{2,1,0:T(8,128)(2,1)}, bf16[16,128,128]{2,1,0:T(8,128)(2,1)S(1)}, u32[]{:S(2)}, u32[]{:S(2)}) collective-permute-start(bf16[16,128,128]{2,1,0:T(8,128)(2,1)} %bitcast.12), channel_id=1, source_target_pairs={{0,4},{4,0},{8,12},{12,8},{16,20},{20,16},{24,28},{28,24},{1,5},{5... | collective-permute-start | bytes 1572872 | tf_op jit(solution)/shard_map/ppermute | solution.py:23
  2.1 7.4 %collective-permute-start = (bf16[4,128,128]{2,1,0:T(8,128)(2,1)S(1)}, bf16[4,128,128]{2,1,0:T(8,128)(2,1)S(1)}, u32[]{:S(2)}, u32[]{:S(2)}) collective-permute-start(bf16[4,128,128]{2,1,0:T(8,128)(2,1)S(1)} %get-tuple-element.24), channel_id=1, source_target_pairs={{0,8},{4,1},{1,4},{5,2},{2,5},{6,3},{3,6},{7,15},{8,0},{12,9},{9,1... | collective-permute-start | bytes 393224 | tf_op jit(solution)/shard_map/ppermute | solution.py:43
  12.3 1.7 %collective-permute-start.3 = (bf16[2,4,96,128]{3,2,1,0:T(8,128)(2,1)S(1)}, bf16[2,4,96,128]{3,2,1,0:T(8,128)(2,1)S(1)}, u32[]{:S(2)}, u32[]{:S(2)}) collective-permute-start(bf16[2,4,96,128]{3,2,1,0:T(8,128)(2,1)S(1)} %get-tuple-element.31), channel_id=1, source_target_pairs={{0,4},{4,0},{8,12},{12,8},{16,20},{20,16},{24,28},{28,24},{1,5},{5... | collective-permute-start | bytes 589832 | tf_op jit(solution)/shard_map/ppermute | solution.py:23
  12.4 5.8 %collective-permute-start.2 = (bf16[2,400,128]{2,1,0:T(8,128)(2,1)S(1)}, bf16[2,400,128]{2,1,0:T(8,128)(2,1)S(1)}, u32[]{:S(2)}, u32[]{:S(2)}) collective-permute-start(bf16[2,400,128]{2,1,0:T(8,128)(2,1)S(1)} %get-tuple-element.29), channel_id=1, source_target_pairs={{0,8},{4,1},{1,4},{5,2},{2,5},{6,3},{3,6},{7,15},{8,0},{12,9},{9,1... | collective-permute-start | bytes 614408 | tf_op jit(solution)/shard_map/ppermute | solution.py:43
  20.3 4.5 %collective-permute-start.4 = (s16[272,128]{1,0:T(8,128)(2,1)S(1)}, s16[272,128]{1,0:T(8,128)(2,1)S(1)}, u32[]{:S(2)}, u32[]{:S(2)}) collective-permute-start(s16[272,128]{1,0:T(8,128)(2,1)S(1)} %get-tuple-element.34), channel_id=1, source_target_pairs={{0,8},{4,12},{8,0},{12,4},{16,24},{20,28},{24,16},{28,20},{1,9},{5... | collective-permute-start | bytes 208904 | tf_op jit(solution)/shard_map/ppermute | solution.py:28
  21.9 6.3 %collective-permute-start.5 = (s16[272,128]{1,0:T(8,128)(2,1)S(1)}, s16[272,128]{1,0:T(8,128)(2,1)S(1)}, u32[]{:S(2)}, u32[]{:S(2)}) collective-permute-start(s16[272,128]{1,0:T(8,128)(2,1)S(1)} %get-tuple-element.35), channel_id=1, source_target_pairs={{0,16},{4,20},{8,24},{12,28},{16,0},{20,4},{24,8},{28,12},{1,17},{... | collective-permute-start | bytes 208904 | tf_op jit(solution)/shard_map/ppermute | solution.py:28
  24.5 6.3 %collective-permute-start.6 = (s16[272,128]{1,0:T(8,128)(2,1)S(1)}, s16[272,128]{1,0:T(8,128)(2,1)S(1)}, u32[]{:S(2)}, u32[]{:S(2)}) collective-permute-start(s16[272,128]{1,0:T(8,128)(2,1)S(1)} %get-tuple-element.36), channel_id=1, source_target_pairs={{0,24},{4,28},{8,16},{12,20},{16,8},{20,12},{24,0},{28,4},{1,25},{... | collective-permute-start | bytes 208904 | tf_op jit(solution)/shard_map/ppermute | solution.py:28
  31.1 6.4 %collective-permute-start.9 = (s16[272,128]{1,0:T(8,128)(2,1)S(1)}, s16[272,128]{1,0:T(8,128)(2,1)S(1)}, u32[]{:S(2)}, u32[]{:S(2)}) collective-permute-start(s16[272,128]{1,0:T(8,128)(2,1)S(1)} %combine.1.rest_0_), channel_id=1, source_target_pairs={{0,24},{4,28},{8,16},{12,20},{16,8},{20,12},{24,0},{28,4},{1,25},{... | collective-permute-start | bytes 208904 | tf_op jit(solution)/shard_map/ppermute | solution.py:28
  33.4 7.6 %collective-permute-start.8 = (s16[272,128]{1,0:T(8,128)(2,1)S(1)}, s16[272,128]{1,0:T(8,128)(2,1)S(1)}, u32[]{:S(2)}, u32[]{:S(2)}) collective-permute-start(s16[272,128]{1,0:T(8,128)(2,1)S(1)} %combine.1.rest_0_), channel_id=1, source_target_pairs={{0,16},{4,20},{8,24},{12,28},{16,0},{20,4},{24,8},{28,12},{1,17},{... | collective-permute-start | bytes 208904 | tf_op jit(solution)/shard_map/ppermute | solution.py:28
  34.4 6.7 %collective-permute-start.7 = (s16[272,128]{1,0:T(8,128)(2,1)S(1)}, s16[272,128]{1,0:T(8,128)(2,1)S(1)}, u32[]{:S(2)}, u32[]{:S(2)}) collective-permute-start(s16[272,128]{1,0:T(8,128)(2,1)S(1)} %combine.1.rest_0_), channel_id=1, source_target_pairs={{0,8},{4,12},{8,0},{12,4},{16,24},{20,28},{24,16},{28,20},{1,9},{5... | collective-permute-start | bytes 208904 | tf_op jit(solution)/shard_map/ppermute | solution.py:28
  35.6 6.0 %collective-permute-start.10 = (s16[272,128]{1,0:T(8,128)(2,1)S(1)}, s16[272,128]{1,0:T(8,128)(2,1)S(1)}, u32[]{:S(2)}, u32[]{:S(2)}) collective-permute-start(s16[272,128]{1,0:T(8,128)(2,1)S(1)} %combine.1.rest_0_), channel_id=1, source_target_pairs={{0,4},{4,0},{8,12},{12,8},{16,20},{20,16},{24,28},{28,24},{1,5},{5... | collective-permute-start | bytes 208904 | tf_op jit(solution)/shard_map/ppermute | solution.py:23
  37.5 4.0 %collective-permute-start.13 = (s16[272,128]{1,0:T(8,128)(2,1)S(1)}, s16[272,128]{1,0:T(8,128)(2,1)S(1)}, u32[]{:S(2)}, u32[]{:S(2)}) collective-permute-start(s16[272,128]{1,0:T(8,128)(2,1)S(1)} %collective-permute-done.9.rest_3_), channel_id=1, source_target_pairs={{0,4},{4,0},{8,12},{12,8},{16,20},{20,16},{24,28},{28,24},{1,5},{5... | collective-permute-start | bytes 208904 | tf_op jit(solution)/shard_map/ppermute | solution.py:23
  41.0 1.3 %collective-permute-start.12 = (s16[272,128]{1,0:T(8,128)(2,1)S(1)}, s16[272,128]{1,0:T(8,128)(2,1)S(1)}, u32[]{:S(2)}, u32[]{:S(2)}) collective-permute-start(s16[272,128]{1,0:T(8,128)(2,1)S(1)} %collective-permute-done.8.rest_2_), channel_id=1, source_target_pairs={{0,4},{4,0},{8,12},{12,8},{16,20},{20,16},{24,28},{28,24},{1,5},{5... | collective-permute-start | bytes 208904 | tf_op jit(solution)/shard_map/ppermute | solution.py:23
  41.0 1.4 %collective-permute-start.11 = (s16[272,128]{1,0:T(8,128)(2,1)S(1)}, s16[272,128]{1,0:T(8,128)(2,1)S(1)}, u32[]{:S(2)}, u32[]{:S(2)}) collective-permute-start(s16[272,128]{1,0:T(8,128)(2,1)S(1)} %collective-permute-done.7.rest_1_), channel_id=1, source_target_pairs={{0,4},{4,0},{8,12},{12,8},{16,20},{20,16},{24,28},{28,24},{1,5},{5... | collective-permute-start | bytes 208904 | tf_op jit(solution)/shard_map/ppermute | solution.py:23

commit v8 on v7

--- a/solution.py
+++ b/solution.py
@@ -205,7 +205,7 @@
         first = window_of(info, j, blocks, rows_y // (width // blocks))
         y_start = pl.multiple_of(first * (width // blocks), width // blocks)
         total = None
-        for s in early_steps(j, rim, (taps_x + 1) // 2):
+        for s in early_steps(rim, (taps_x + 1) // 2):
             part = dot_turned(
                 lambda x: cols[x - rim, pl.ds(y_start, rows_y), :], range(rim), table, j, s
             )
@@ -275,8 +275,8 @@
     return jnp.concatenate([total[:cut], total[cut:] + part], axis=0)
 
 
-def early_steps(j, rim, steps):
-    return range(rim // 2 + j, steps)
+def early_steps(rim, steps):
+    return range(rim // 2, steps)
 
 
 def blur_kernel(
@@ -311,7 +311,7 @@
             return part[pl.ds(y_start, rows_y), :]
 
         total = early[j]
-        for s in range(early_steps(j, rim, 0).start):
+        for s in range(early_steps(rim, 0).start):
             total = total + dot_turned(slab, range(half // 2), table, j, s)
         blurred = [total[i * rows_y : (i + 1) * rows_y] for i in range(half // 2)]
         slot = view_slot(core, j, views)
@@ -595,7 +595,8 @@
         ],
         work // 4,
     )(info, remote, sums, table, est_own)
-    arrived = [pieces[0]] + [swap_chips(pieces[step], step) for step in range(1, chips)]
+    steps = range(chips - 1, 0, -1)
+    arrived = [pieces[0]] + [swap_chips(pieces[step], step) for step in steps]
     mine = call(
         combine_kernel,
         "combine",

time: 44.2 us -> 43.7 us (0.989)
  waiting for transfers between devices: 12.5 us -> 12 us
    ppermute x6, waiting for transfers between devices: 11.5 us -> 11 us  [swap_chips(): lax.ppermute(cells, 'view', [(i, i ^ 2 * step) for i in range(count)])]
    pallas_call x1, Pallas kernels: 2.73 us -> 2.27 us  [local(): call(functools.partial(blur_kernel, taps=taps, blocks=blocks), 'blur', (p...]
  transfers between devices with their start and end apart: 14 -> 14, of which waited for: 7 -> 7; matrix products, arithmetic and copies ran while one was open for 0% -> 0% of each run, Pallas kernels for 24% -> 25%
where the time goes in v8:
time: 43.7 us; the launch traced here: 43.5 us
  Pallas kernels  17.1 us (39%)
  starting transfers between devices  14.2 us (32%)
  waiting for transfers between devices  12 us (27%)
    ppermute x6, waiting for transfers between devices, swap_chips(): lax.ppermute(cells, 'view', [(i, i ^ 2 * step) for i in range(count)])  11 us
    ppermute x6, starting transfers between devices, swap_chips(): lax.ppermute(cells, 'view', [(i, i ^ 2 * step) for i in range(count)])  8.91 us
    pallas_call x1, Pallas kernels, local(): call(functools.partial(tables_kernel, taps=taps, blocks=blocks), 'tables'...  5.1 us
    ppermute x2, starting transfers between devices, swap_layers(): return lax.ppermute(cells, ('view', 'blk'), route)  4.21 us
    pallas_call x1, Pallas kernels, local(): call(functools.partial(inner_kernel, taps=taps), 'inner', pltpu.VMEM((vie...  4.05 us
    pallas_call x1, Pallas kernels, local(): call(functools.partial(blur_kernel, taps=taps, blocks=blocks), 'blur', (p...  2.27 us
    pallas_call x1, Pallas kernels, local(): call(functools.partial(correct_kernel, taps=taps, blocks=blocks), 'correc...  2.15 us
    pallas_call x1, Pallas kernels, local(): call(gather_kernel, 'gather', shape(estimate.shape, f32), 's' + 'v' * (2...  1.65 us
  transfers between devices with their start and end apart: 14, of which 7 were waited for; matrix products, arithmetic and copies ran while one was open for 0% of the time, Pallas kernels for 25%

profile of v8, /device:TPU:0, one launch (start us, length us, event | category | flops | bytes accessed | tf_op | source)
XLA Modules:
  0.0 43.5 jit_solution(3634030264218436910)
XLA Ops:
  0.0 0.5 %collective-permute-start.1 = (bf16[16,128,128]{2,1,0:T(8,128)(2,1)}, bf16[16,128,128]{2,1,0:T(8,128)(2,1)S(1)}, u32[]{:S(2)}, u32[]{:S(2)}) collective-permute-start(bf16[16,128,128]{2,1,0:T(8,128)(2,1)} %bitcast.12), channel_id=1, source_target_pairs={{0,4},{4,0},{8,12},{12,8},{16,20},{20,16},{24,28},{28,24},{1,5},{5... | collective-permute-start | bytes 1572872 | tf_op jit(solution)/shard_map/ppermute | solution.py:23
  0.5 1.6 %payload.1 = (bf16[4,128,128]{2,1,0:T(8,128)(2,1)S(1)}, s32[4,8]{1,0:T(4,128)S(1)}, f32[504,25]{1,0:T(8,128)S(1)}) custom-call(s32[3]{0:T(128)S(1)} %pad_add_fusion.ids, s32[4,8]{1,0:T(4,128)} %bitcast.11, f32[504,25]{1,0:T(8,128)} %bitcast.10, f32[16,128,128]{2,1,0:T(8,128)} %est.3), custom_call_target="tpu_custom_call" | custom-call | bytes 65536 | tf_op jit(solution)/shard_map/payload/pallas_call | solution.py:518
  2.1 2.6 %collective-permute-start = (bf16[4,128,128]{2,1,0:T(8,128)(2,1)S(1)}, bf16[4,128,128]{2,1,0:T(8,128)(2,1)S(1)}, u32[]{:S(2)}, u32[]{:S(2)}) collective-permute-start(bf16[4,128,128]{2,1,0:T(8,128)(2,1)S(1)} %get-tuple-element.24), channel_id=1, source_target_pairs={{0,8},{4,1},{1,4},{5,2},{2,5},{6,3},{3,6},{7,15},{8,0},{12,9},{9,1... | collective-permute-start | bytes 393224 | tf_op jit(solution)/shard_map/ppermute | solution.py:43
  4.8 5.1 %tables.1 = (bf16[2,9,896,128]{3,2,1,0:T(8,128)(2,1)S(1)}, bf16[12,128,896]{2,1,0:T(8,128)(2,1)S(1)}, s32[5]{0:T(128)S(1)}, bf16[16,128,128]{2,1,0:T(8,128)(2,1)...) custom-call(s32[3]{0:T(128)S(1)} %pad_add_fusion.ids, s32[4,8]{1,0:T(4,128)S(1)} %get-tuple-element.21.cov, ...), custom_call_target="tpu_custom_call" | custom-call | flops 1585446912 | bytes 65536 | tf_op jit(solution)/shard_map/tables/pallas_call | solution.py:531
  9.9 2.3 %blur.1 = (bf16[2,8,96,128]{3,2,1,0:T(8,128)(2,1)S(1)}, bf16[2,400,128]{2,1,0:T(8,128)(2,1)S(1)}, bf16[2,4,96,128]{3,2,1,0:T(8,128)(2,1)S(1)}) custom-call(s32[5]{0:T(128)S(1)} %get-tuple-element.23.info, bf16[4,128,128]{2,1,0:T(8,128)(2,1)S(1)} %collective-permute-done.halo, bf16[16,128,128]{2,1,0:T(8,128)(2,1)S(1)} %get-tuple-element.25.img_own, ...), custom_call_target="tpu_custom_call" | custom-call | flops 3170893824 | bytes 65536 | tf_op jit(solution)/shard_map/blur/pallas_call | solution.py:552
  12.2 0.1 collective-permute-start.3
  12.3 1.6 %collective-permute-start.2 = (bf16[2,400,128]{2,1,0:T(8,128)(2,1)S(1)}, bf16[2,400,128]{2,1,0:T(8,128)(2,1)S(1)}, u32[]{:S(2)}, u32[]{:S(2)}) collective-permute-start(bf16[2,400,128]{2,1,0:T(8,128)(2,1)S(1)} %get-tuple-element.29), channel_id=1, source_target_pairs={{0,8},{4,1},{1,4},{5,2},{2,5},{6,3},{3,6},{7,15},{8,0},{12,9},{9,1... | collective-permute-start | bytes 614408 | tf_op jit(solution)/shard_map/ppermute | solution.py:43
  13.9 4.1 %inner.1.sums = f32[2,384,256]{2,1,0:T(8,128)S(1)} custom-call(s32[5]{0:T(128)S(1)} %get-tuple-element.23.info, bf16[2,8,96,128]{3,2,1,0:T(8,128)(2,1)S(1)} %get-tuple-element.30.quot, bf16[2,4,96,128]{3,2,1,0:T(8,128)(2,1)S(1)} %collective-permute-done.3.near, bf16[2,9,896,128]{3,2,1,0:T(8,128)(2,1)S(1)} %get-tuple-element.27.table), custom_call_target="tpu_custom_call" | custom-call | flops 3170893824 | bytes 65536 | tf_op jit(solution)/shard_map/inner/pallas_call | solution.py:571
  17.9 0.2 collective-permute-done.2.remote
  18.1 2.2 %correct.1 = (f32[2,128,128]{2,1,0:T(8,128)S(1)}, s16[272,128]{1,0:T(8,128)(2,1)S(1)}, s16[272,128]{1,0:T(8,128)(2,1)S(1)}, s16[272,128]{1,0:T(8,128)(2,1)S(1)}) custom-call(s32[5]{0:T(128)S(1)} %get-tuple-element.23.info, bf16[2,400,128]{2,1,0:T(8,128)(2,1)S(1)} %collective-permute-done.2.remote, f32[2,384,256]{2,1,0:T(8,128)S(1)} %inner.1.sums, ...), custom_call_target="tpu_custom_call" | custom-call | flops 792723456 | bytes 65536 | tf_op jit(solution)/shard_map/correct/pallas_call | solution.py:584
  20.2 3.6 %collective-permute-start.4 = (s16[272,128]{1,0:T(8,128)(2,1)S(1)}, s16[272,128]{1,0:T(8,128)(2,1)S(1)}, u32[]{:S(2)}, u32[]{:S(2)}) collective-permute-start(s16[272,128]{1,0:T(8,128)(2,1)S(1)} %get-tuple-element.34), channel_id=1, source_target_pairs={{0,24},{4,28},{8,16},{12,20},{16,8},{20,12},{24,0},{28,4},{1,25},{... | collective-permute-start | bytes 208904 | tf_op jit(solution)/shard_map/ppermute | solution.py:28
  23.8 0.9 %collective-permute-start.6 = (s16[272,128]{1,0:T(8,128)(2,1)S(1)}, s16[272,128]{1,0:T(8,128)(2,1)S(1)}, u32[]{:S(2)}, u32[]{:S(2)}) collective-permute-start(s16[272,128]{1,0:T(8,128)(2,1)S(1)} %get-tuple-element.36), channel_id=1, source_target_pairs={{0,8},{4,12},{8,0},{12,4},{16,24},{20,28},{24,16},{28,20},{1,9},{5... | collective-permute-start | bytes 208904 | tf_op jit(solution)/shard_map/ppermute | solution.py:28
  24.7 1.8 %collective-permute-done.4.rest_0_ = s16[272,128]{1,0:T(8,128)(2,1)S(1)} collective-permute-done((s16[272,128]{1,0:T(8,128)(2,1)S(1)}, s16[272,128]{1,0:T(8,128)(2,1)S(1)}, u32[]{:S(2)}, u32[]{:S(2)}) %collective-permute-start.4) | collective-permute-done | bytes 69664 | tf_op jit(solution)/shard_map/ppermute | solution.py:28
  26.5 3.9 %collective-permute-done.5.rest_1_ = s16[272,128]{1,0:T(8,128)(2,1)S(1)} collective-permute-done((s16[272,128]{1,0:T(8,128)(2,1)S(1)}, s16[272,128]{1,0:T(8,128)(2,1)S(1)}, u32[]{:S(2)}, u32[]{:S(2)}) %collective-permute-start.5) | collective-permute-done | bytes 69664 | tf_op jit(solution)/shard_map/ppermute | solution.py:28
  30.4 0.3 combine.1.rest_0_
  30.7 2.7 %collective-permute-start.9 = (s16[272,128]{1,0:T(8,128)(2,1)S(1)}, s16[272,128]{1,0:T(8,128)(2,1)S(1)}, u32[]{:S(2)}, u32[]{:S(2)}) collective-permute-start(s16[272,128]{1,0:T(8,128)(2,1)S(1)} %combine.1.rest_0_), channel_id=1, source_target_pairs={{0,24},{4,28},{8,16},{12,20},{16,8},{20,12},{24,0},{28,4},{1,25},{... | collective-permute-start | bytes 208904 | tf_op jit(solution)/shard_map/ppermute | solution.py:28
  33.4 0.3 collective-permute-start.8
  33.7 1.5 %collective-permute-start.7 = (s16[272,128]{1,0:T(8,128)(2,1)S(1)}, s16[272,128]{1,0:T(8,128)(2,1)S(1)}, u32[]{:S(2)}, u32[]{:S(2)}) collective-permute-start(s16[272,128]{1,0:T(8,128)(2,1)S(1)} %combine.1.rest_0_), channel_id=1, source_target_pairs={{0,8},{4,12},{8,0},{12,4},{16,24},{20,28},{24,16},{28,20},{1,9},{5... | collective-permute-start | bytes 208904 | tf_op jit(solution)/shard_map/ppermute | solution.py:28
  35.2 2.5 %collective-permute-done.9.rest_3_ = s16[272,128]{1,0:T(8,128)(2,1)S(1)} collective-permute-done((s16[272,128]{1,0:T(8,128)(2,1)S(1)}, s16[272,128]{1,0:T(8,128)(2,1)S(1)}, u32[]{:S(2)}, u32[]{:S(2)}) %collective-permute-start.9) | collective-permute-done | bytes 69664 | tf_op jit(solution)/shard_map/ppermute | solution.py:28
  37.7 2.7 %collective-permute-done.8.rest_2_ = s16[272,128]{1,0:T(8,128)(2,1)S(1)} collective-permute-done((s16[272,128]{1,0:T(8,128)(2,1)S(1)}, s16[272,128]{1,0:T(8,128)(2,1)S(1)}, u32[]{:S(2)}, u32[]{:S(2)}) %collective-permute-start.8) | collective-permute-done | bytes 69664 | tf_op jit(solution)/shard_map/ppermute | solution.py:28
  40.4 0.5 %collective-permute-start.11 = (s16[272,128]{1,0:T(8,128)(2,1)S(1)}, s16[272,128]{1,0:T(8,128)(2,1)S(1)}, u32[]{:S(2)}, u32[]{:S(2)}) collective-permute-start(s16[272,128]{1,0:T(8,128)(2,1)S(1)} %collective-permute-done.7.rest_1_), channel_id=1, source_target_pairs={{0,4},{4,0},{8,12},{12,8},{16,20},{20,16},{24,28},{28,24},{1,5},{5... | collective-permute-start | bytes 208904 | tf_op jit(solution)/shard_map/ppermute | solution.py:23
  41.0 0.7 %collective-permute-done.12.rest_6_ = s16[272,128]{1,0:T(8,128)(2,1)S(1)} collective-permute-done((s16[272,128]{1,0:T(8,128)(2,1)S(1)}, s16[272,128]{1,0:T(8,128)(2,1)S(1)}, u32[]{:S(2)}, u32[]{:S(2)}) %collective-permute-start.12) | collective-permute-done | bytes 69664 | tf_op jit(solution)/shard_map/ppermute | solution.py:23
  41.7 0.2 collective-permute-done.11.rest_5_
  41.9 1.6 %gather.1 = f32[16,128,128]{2,1,0:T(8,128)} custom-call(s32[3]{0:T(128)S(1)} %pad_add_fusion.ids, s16[272,128]{1,0:T(8,128)(2,1)S(1)} %combine.1.rest_0_, s16[272,128]{1,0:T(8,128)(2,1)S(1)} %collective-permute-done.7.rest_1_, s16[272,128]{1,0:T(8,128)(2,1)S(1)} %collective-permute-done.8.rest_2_, s16[272,128]{1,0:T(8,128)(2,1)S(1)} %collective-permute-done.9.rest_3_, ...), custom_call_target="tpu_custom_call" | custom-call | bytes 65536 | tf_op jit(solution)/shard_map/gather/pallas_call | solution.py:608
  (12 shorter events, 0.1 us)
Async XLA Ops:
  0.0 9.9 %collective-permute-start.1 = (bf16[16,128,128]{2,1,0:T(8,128)(2,1)}, bf16[16,128,128]{2,1,0:T(8,128)(2,1)S(1)}, u32[]{:S(2)}, u32[]{:S(2)}) collective-permute-start(bf16[16,128,128]{2,1,0:T(8,128)(2,1)} %bitcast.12), channel_id=1, source_target_pairs={{0,4},{4,0},{8,12},{12,8},{16,20},{20,16},{24,28},{28,24},{1,5},{5... | collective-permute-start | bytes 1572872 | tf_op jit(solution)/shard_map/ppermute | solution.py:23
  2.1 7.8 %collective-permute-start = (bf16[4,128,128]{2,1,0:T(8,128)(2,1)S(1)}, bf16[4,128,128]{2,1,0:T(8,128)(2,1)S(1)}, u32[]{:S(2)}, u32[]{:S(2)}) collective-permute-start(bf16[4,128,128]{2,1,0:T(8,128)(2,1)S(1)} %get-tuple-element.24), channel_id=1, source_target_pairs={{0,8},{4,1},{1,4},{5,2},{2,5},{6,3},{3,6},{7,15},{8,0},{12,9},{9,1... | collective-permute-start | bytes 393224 | tf_op jit(solution)/shard_map/ppermute | solution.py:43
  12.2 1.7 %collective-permute-start.3 = (bf16[2,4,96,128]{3,2,1,0:T(8,128)(2,1)S(1)}, bf16[2,4,96,128]{3,2,1,0:T(8,128)(2,1)S(1)}, u32[]{:S(2)}, u32[]{:S(2)}) collective-permute-start(bf16[2,4,96,128]{3,2,1,0:T(8,128)(2,1)S(1)} %get-tuple-element.31), channel_id=1, source_target_pairs={{0,4},{4,0},{8,12},{12,8},{16,20},{20,16},{24,28},{28,24},{1,5},{5... | collective-permute-start | bytes 589832 | tf_op jit(solution)/shard_map/ppermute | solution.py:23
  12.3 5.8 %collective-permute-start.2 = (bf16[2,400,128]{2,1,0:T(8,128)(2,1)S(1)}, bf16[2,400,128]{2,1,0:T(8,128)(2,1)S(1)}, u32[]{:S(2)}, u32[]{:S(2)}) collective-permute-start(bf16[2,400,128]{2,1,0:T(8,128)(2,1)S(1)} %get-tuple-element.29), channel_id=1, source_target_pairs={{0,8},{4,1},{1,4},{5,2},{2,5},{6,3},{3,6},{7,15},{8,0},{12,9},{9,1... | collective-permute-start | bytes 614408 | tf_op jit(solution)/shard_map/ppermute | solution.py:43
  20.2 6.3 %collective-permute-start.4 = (s16[272,128]{1,0:T(8,128)(2,1)S(1)}, s16[272,128]{1,0:T(8,128)(2,1)S(1)}, u32[]{:S(2)}, u32[]{:S(2)}) collective-permute-start(s16[272,128]{1,0:T(8,128)(2,1)S(1)} %get-tuple-element.34), channel_id=1, source_target_pairs={{0,24},{4,28},{8,16},{12,20},{16,8},{20,12},{24,0},{28,4},{1,25},{... | collective-permute-start | bytes 208904 | tf_op jit(solution)/shard_map/ppermute | solution.py:28
  23.8 6.6 %collective-permute-start.5 = (s16[272,128]{1,0:T(8,128)(2,1)S(1)}, s16[272,128]{1,0:T(8,128)(2,1)S(1)}, u32[]{:S(2)}, u32[]{:S(2)}) collective-permute-start(s16[272,128]{1,0:T(8,128)(2,1)S(1)} %get-tuple-element.35), channel_id=1, source_target_pairs={{0,16},{4,20},{8,24},{12,28},{16,0},{20,4},{24,8},{28,12},{1,17},{... | collective-permute-start | bytes 208904 | tf_op jit(solution)/shard_map/ppermute | solution.py:28
  23.8 6.6 %collective-permute-start.6 = (s16[272,128]{1,0:T(8,128)(2,1)S(1)}, s16[272,128]{1,0:T(8,128)(2,1)S(1)}, u32[]{:S(2)}, u32[]{:S(2)}) collective-permute-start(s16[272,128]{1,0:T(8,128)(2,1)S(1)} %get-tuple-element.36), channel_id=1, source_target_pairs={{0,8},{4,12},{8,0},{12,4},{16,24},{20,28},{24,16},{28,20},{1,9},{5... | collective-permute-start | bytes 208904 | tf_op jit(solution)/shard_map/ppermute | solution.py:28
  30.7 7.0 %collective-permute-start.9 = (s16[272,128]{1,0:T(8,128)(2,1)S(1)}, s16[272,128]{1,0:T(8,128)(2,1)S(1)}, u32[]{:S(2)}, u32[]{:S(2)}) collective-permute-start(s16[272,128]{1,0:T(8,128)(2,1)S(1)} %combine.1.rest_0_), channel_id=1, source_target_pairs={{0,24},{4,28},{8,16},{12,20},{16,8},{20,12},{24,0},{28,4},{1,25},{... | collective-permute-start | bytes 208904 | tf_op jit(solution)/shard_map/ppermute | solution.py:28
  33.4 7.1 %collective-permute-start.8 = (s16[272,128]{1,0:T(8,128)(2,1)S(1)}, s16[272,128]{1,0:T(8,128)(2,1)S(1)}, u32[]{:S(2)}, u32[]{:S(2)}) collective-permute-start(s16[272,128]{1,0:T(8,128)(2,1)S(1)} %combine.1.rest_0_), channel_id=1, source_target_pairs={{0,16},{4,20},{8,24},{12,28},{16,0},{20,4},{24,8},{28,12},{1,17},{... | collective-permute-start | bytes 208904 | tf_op jit(solution)/shard_map/ppermute | solution.py:28
  33.7 6.8 %collective-permute-start.7 = (s16[272,128]{1,0:T(8,128)(2,1)S(1)}, s16[272,128]{1,0:T(8,128)(2,1)S(1)}, u32[]{:S(2)}, u32[]{:S(2)}) collective-permute-start(s16[272,128]{1,0:T(8,128)(2,1)S(1)} %combine.1.rest_0_), channel_id=1, source_target_pairs={{0,8},{4,12},{8,0},{12,4},{16,24},{20,28},{24,16},{28,20},{1,9},{5... | collective-permute-start | bytes 208904 | tf_op jit(solution)/shard_map/ppermute | solution.py:28
  35.2 5.8 %collective-permute-start.10 = (s16[272,128]{1,0:T(8,128)(2,1)S(1)}, s16[272,128]{1,0:T(8,128)(2,1)S(1)}, u32[]{:S(2)}, u32[]{:S(2)}) collective-permute-start(s16[272,128]{1,0:T(8,128)(2,1)S(1)} %combine.1.rest_0_), channel_id=1, source_target_pairs={{0,4},{4,0},{8,12},{12,8},{16,20},{20,16},{24,28},{28,24},{1,5},{5... | collective-permute-start | bytes 208904 | tf_op jit(solution)/shard_map/ppermute | solution.py:23
  37.7 3.3 %collective-permute-start.13 = (s16[272,128]{1,0:T(8,128)(2,1)S(1)}, s16[272,128]{1,0:T(8,128)(2,1)S(1)}, u32[]{:S(2)}, u32[]{:S(2)}) collective-permute-start(s16[272,128]{1,0:T(8,128)(2,1)S(1)} %collective-permute-done.9.rest_3_), channel_id=1, source_target_pairs={{0,4},{4,0},{8,12},{12,8},{16,20},{20,16},{24,28},{28,24},{1,5},{5... | collective-permute-start | bytes 208904 | tf_op jit(solution)/shard_map/ppermute | solution.py:23
  40.4 1.3 %collective-permute-start.12 = (s16[272,128]{1,0:T(8,128)(2,1)S(1)}, s16[272,128]{1,0:T(8,128)(2,1)S(1)}, u32[]{:S(2)}, u32[]{:S(2)}) collective-permute-start(s16[272,128]{1,0:T(8,128)(2,1)S(1)} %collective-permute-done.8.rest_2_), channel_id=1, source_target_pairs={{0,4},{4,0},{8,12},{12,8},{16,20},{20,16},{24,28},{28,24},{1,5},{5... | collective-permute-start | bytes 208904 | tf_op jit(solution)/shard_map/ppermute | solution.py:23
  40.4 1.4 %collective-permute-start.11 = (s16[272,128]{1,0:T(8,128)(2,1)S(1)}, s16[272,128]{1,0:T(8,128)(2,1)S(1)}, u32[]{:S(2)}, u32[]{:S(2)}) collective-permute-start(s16[272,128]{1,0:T(8,128)(2,1)S(1)} %collective-permute-done.7.rest_1_), channel_id=1, source_target_pairs={{0,4},{4,0},{8,12},{12,8},{16,20},{20,16},{24,28},{28,24},{1,5},{5... | collective-permute-start | bytes 208904 | tf_op jit(solution)/shard_map/ppermute | solution.py:23

commit v9 on v8

--- a/solution.py
+++ b/solution.py
@@ -333,12 +333,15 @@
                 near[slot, r - rim] = ratio
 
 
-def inner_kernel(info, quot, near, table, sums, pad, cols, *, taps):
+def inner_kernel(
+    info, quot, near, table, sums, product, logs, ends, pad, cols, *, taps, blocks
+):
     views, half, rows_y, depth = quot.shape
     rim = near.shape[1]
     pairs = half // 2
     steps = (table.shape[1] + 1) // 2
     margin = jnp.zeros((half + rim, PAD, depth), jnp.float32)
+    product[...] = jnp.ones(product.shape, jnp.float32)
     for j in range(views):
         pad[j, :, :PAD, :] = margin
         pad[j, :, PAD + rows_y :, :] = margin
@@ -358,10 +361,29 @@
                 preferred_element_type=jnp.float32,
             )
             total = add_rows(total, part, skip * rows_y)
-        sums[j] = total
-
-
-def correct_kernel(info, remote, sums, table, est_own, *rest, taps, blocks):
+        whole = rim // 2 * rows_y
+        sums[j] = total[:whole]
+        block_width = product.shape[1] // blocks
+        first = window_of(info, j, blocks, rows_y // block_width)
+        mask = window_mask(info, j, first, rows_y // block_width, block_width)
+        y_start = pl.multiple_of(first * block_width, block_width)
+        for r in range(half - rim):
+            low, w = whole + r // 2 * rows_y, r % 2
+            factor = jnp.where(mask, total[low : low + rows_y, w * depth : (w + 1) * depth], 1.0)
+            at = (r, pl.ds(y_start, rows_y), slice(None))
+            product[at] = product[at] * factor
+    least = jnp.full(ends.shape[1:], jnp.inf, jnp.float32)
+    most = -least
+    for r in range(half - rim):
+        cells = jnp.log(product[r])
+        logs[r] = cells
+        least = jnp.minimum(least, cells)
+        most = jnp.maximum(most, cells)
+    ends[0] = least
+    ends[1] = most
+
+
+def correct_kernel(info, remote, sums, table, est_own, near_product, near_logs, ends, *rest, taps, blocks):
     *pieces, pad, cols, far, product, logs = rest
     chip = info[1]
     views, rim, rows_y, _ = cols.shape
@@ -369,7 +391,9 @@
     block_width = width // blocks
     window = rows_y // block_width
     rows = half // len(pieces)
-    product[...] = jnp.ones(product.shape, jnp.float32)
+    product[:rim] = jnp.ones((rim, width, depth), jnp.float32)
+    product[rim:] = near_product[...]
+    logs[rim:] = near_logs[...]
     far[...] = jnp.zeros(far.shape, jnp.float32)
     for j in range(views):
         first = window_of(info, j, blocks, window)
@@ -387,7 +411,7 @@
         for r in range(rim):
             pad[j, r] = far[j, r, pl.ds(y_start, rows_y + 2 * PAD), :]
         fill_columns(pad.at[j], cols.at[j], taps[1], rows_y)
-        edges = [None] * (half // 2)
+        edges = [None] * (rim // 2)
         for s in range(rim // 2):
             pairs = range(rim // 2 - s)
             part = jnp.dot(
@@ -398,17 +422,15 @@
             for i in pairs:
                 cells = part[i * rows_y : (i + 1) * rows_y]
                 edges[i] = cells if edges[i] is None else edges[i] + cells
-        for r in range(half):
+        for r in range(rim):
             i, w = r // 2, r % 2
             cells = sums[j, i * rows_y : (i + 1) * rows_y, w * depth : (w + 1) * depth]
-            if edges[i] is not None:
-                cells = cells + edges[i][:, w * depth : (w + 1) * depth]
+            cells = cells + edges[i][:, w * depth : (w + 1) * depth]
             factor = jnp.where(mask, cells, 1.0)
             at = (r, pl.ds(y_start, rows_y), slice(None))
             product[at] = product[at] * factor
-    least = jnp.full((width, depth), jnp.inf, jnp.float32)
-    most = -least
-    for r in range(half):
+    least, most = ends[0], ends[1]
+    for r in range(rim):
         cells = jnp.log(product[r])
         logs[r] = cells
         least = jnp.minimum(least, cells)
@@ -568,10 +590,16 @@
     near = swap_cores(near)
     remote = swap_layers(remote)
 
-    sums = call(
-        functools.partial(inner_kernel, taps=taps),
+    part = pltpu.VMEM((half - rim, width, depth), f32)
+    sums, near_product, near_logs, ends = call(
+        functools.partial(inner_kernel, taps=taps, blocks=blocks),
         "inner",
-        pltpu.VMEM((views, half // 2 * rows_y, 2 * depth), f32),
+        (
+            pltpu.VMEM((views, rim // 2 * rows_y, 2 * depth), f32),
+            part,
+            part,
+            pltpu.VMEM((2, width, depth), f32),
+        ),
         "svvv",
         [
             pltpu.VMEM((views, inner, tall, depth), f32),
@@ -585,7 +613,7 @@
         functools.partial(correct_kernel, taps=taps, blocks=blocks),
         "correct",
         (pltpu.VMEM((rows, width, depth), f32),) + (coded,) * (chips - 1),
-        "svvvv",
+        "svvvvvvv",
         [
             pltpu.VMEM((views, rim, tall, depth), f32),
             pltpu.VMEM((views, rim, rows_y, deep), bf16),
@@ -594,7 +622,7 @@
             pltpu.VMEM((half, width, depth), f32),
         ],
         work // 4,
-    )(info, remote, sums, table, est_own)
+    )(info, remote, sums, table, est_own, near_product, near_logs, ends)
     steps = range(chips - 1, 0, -1)
     arrived = [pieces[0]] + [swap_chips(pieces[step], step) for step in steps]
     mine = call(

time: 43.7 us -> 43.6 us (level)
  no operation moved by 1% of the time
where the time goes in v9:
time: 43.6 us; the launch traced here: 43.5 us
  Pallas kernels  17.1 us (39%)
  starting transfers between devices  14.1 us (32%)
  waiting for transfers between devices  12.1 us (28%)
    ppermute x6, waiting for transfers between devices, swap_chips(): lax.ppermute(cells, 'view', [(i, i ^ 2 * step) for i in range(count)])  11 us
    ppermute x6, starting transfers between devices, swap_chips(): lax.ppermute(cells, 'view', [(i, i ^ 2 * step) for i in range(count)])  8.91 us
    pallas_call x1, Pallas kernels, local(): call(functools.partial(tables_kernel, taps=taps, blocks=blocks), 'tables'...  5.13 us
    ppermute x2, starting transfers between devices, swap_layers(): return lax.ppermute(cells, ('view', 'blk'), route)  4.16 us
    pallas_call x1, Pallas kernels, local(): call(functools.partial(inner_kernel, taps=taps, blocks=blocks), 'inner',...  4.14 us
    pallas_call x1, Pallas kernels, local(): call(functools.partial(blur_kernel, taps=taps, blocks=blocks), 'blur', (p...  2.26 us
    pallas_call x1, Pallas kernels, local(): call(functools.partial(correct_kernel, taps=taps, blocks=blocks), 'correc...  2.06 us
    pallas_call x1, Pallas kernels, local(): call(gather_kernel, 'gather', shape(estimate.shape, f32), 's' + 'v' * (2...  1.65 us
  transfers between devices with their start and end apart: 14, of which 7 were waited for; matrix products, arithmetic and copies ran while one was open for 0% of the time, Pallas kernels for 25%

profile of v9, /device:TPU:0, one launch (start us, length us, event | category | flops | bytes accessed | tf_op | source)
XLA Modules:
  0.0 43.5 jit_solution(9469494718456111294)
XLA Ops:
  0.0 0.5 %collective-permute-start.1 = (bf16[16,128,128]{2,1,0:T(8,128)(2,1)}, bf16[16,128,128]{2,1,0:T(8,128)(2,1)S(1)}, u32[]{:S(2)}, u32[]{:S(2)}) collective-permute-start(bf16[16,128,128]{2,1,0:T(8,128)(2,1)} %bitcast.12), channel_id=1, source_target_pairs={{0,4},{4,0},{8,12},{12,8},{16,20},{20,16},{24,28},{28,24},{1,5},{5... | collective-permute-start | bytes 1572872 | tf_op jit(solution)/shard_map/ppermute | solution.py:23
  0.5 0.1 pad_add_fusion.ids
  0.5 1.6 %payload.1 = (bf16[4,128,128]{2,1,0:T(8,128)(2,1)S(1)}, s32[4,8]{1,0:T(4,128)S(1)}, f32[504,25]{1,0:T(8,128)S(1)}) custom-call(s32[3]{0:T(128)S(1)} %pad_add_fusion.ids, s32[4,8]{1,0:T(4,128)} %bitcast.11, f32[504,25]{1,0:T(8,128)} %bitcast.10, f32[16,128,128]{2,1,0:T(8,128)} %est.3), custom_call_target="tpu_custom_call" | custom-call | bytes 65536 | tf_op jit(solution)/shard_map/payload/pallas_call | solution.py:540
  2.1 2.6 %collective-permute-start = (bf16[4,128,128]{2,1,0:T(8,128)(2,1)S(1)}, bf16[4,128,128]{2,1,0:T(8,128)(2,1)S(1)}, u32[]{:S(2)}, u32[]{:S(2)}) collective-permute-start(bf16[4,128,128]{2,1,0:T(8,128)(2,1)S(1)} %get-tuple-element.28), channel_id=1, source_target_pairs={{0,8},{4,1},{1,4},{5,2},{2,5},{6,3},{3,6},{7,15},{8,0},{12,9},{9,1... | collective-permute-start | bytes 393224 | tf_op jit(solution)/shard_map/ppermute | solution.py:43
  4.8 5.1 %tables.1 = (bf16[2,9,896,128]{3,2,1,0:T(8,128)(2,1)S(1)}, bf16[12,128,896]{2,1,0:T(8,128)(2,1)S(1)}, s32[5]{0:T(128)S(1)}, bf16[16,128,128]{2,1,0:T(8,128)(2,1)...) custom-call(s32[3]{0:T(128)S(1)} %pad_add_fusion.ids, s32[4,8]{1,0:T(4,128)S(1)} %get-tuple-element.25.cov, ...), custom_call_target="tpu_custom_call" | custom-call | flops 1585446912 | bytes 65536 | tf_op jit(solution)/shard_map/tables/pallas_call | solution.py:553
  9.9 2.3 %blur.1 = (bf16[2,8,96,128]{3,2,1,0:T(8,128)(2,1)S(1)}, bf16[2,400,128]{2,1,0:T(8,128)(2,1)S(1)}, bf16[2,4,96,128]{3,2,1,0:T(8,128)(2,1)S(1)}) custom-call(s32[5]{0:T(128)S(1)} %get-tuple-element.27.info, bf16[4,128,128]{2,1,0:T(8,128)(2,1)S(1)} %collective-permute-done.halo, bf16[16,128,128]{2,1,0:T(8,128)(2,1)S(1)} %get-tuple-element.29.img_own, ...), custom_call_target="tpu_custom_call" | custom-call | flops 3170893824 | bytes 65536 | tf_op jit(solution)/shard_map/blur/pallas_call | solution.py:574
  12.3 1.5 %collective-permute-start.2 = (bf16[2,400,128]{2,1,0:T(8,128)(2,1)S(1)}, bf16[2,400,128]{2,1,0:T(8,128)(2,1)S(1)}, u32[]{:S(2)}, u32[]{:S(2)}) collective-permute-start(bf16[2,400,128]{2,1,0:T(8,128)(2,1)S(1)} %get-tuple-element.33), channel_id=1, source_target_pairs={{0,8},{4,1},{1,4},{5,2},{2,5},{6,3},{3,6},{7,15},{8,0},{12,9},{9,1... | collective-permute-start | bytes 614408 | tf_op jit(solution)/shard_map/ppermute | solution.py:43
  13.8 4.1 %inner.1 = (f32[2,192,256]{2,1,0:T(8,128)S(1)}, f32[4,128,128]{2,1,0:T(8,128)S(1)}, f32[4,128,128]{2,1,0:T(8,128)S(1)}, f32[2,128,128]{2,1,0:T(8,128)S(1)}) custom-call(s32[5]{0:T(128)S(1)} %get-tuple-element.27.info, bf16[2,8,96,128]{3,2,1,0:T(8,128)(2,1)S(1)} %get-tuple-element.34.quot, bf16[2,4,96,128]{3,2,1,0:T(8,128)(2,1)S(1)} %collective-permute-done.3.near, ...), custom_call_target="tpu_custom_call" | custom-call | flops 3170893824 | bytes 65536 | tf_op jit(solution)/shard_map/inner/pallas_call | solution.py:594
  18.0 0.2 collective-permute-done.2.remote
  18.1 2.1 %correct.1 = (f32[2,128,128]{2,1,0:T(8,128)S(1)}, s16[272,128]{1,0:T(8,128)(2,1)S(1)}, s16[272,128]{1,0:T(8,128)(2,1)S(1)}, s16[272,128]{1,0:T(8,128)(2,1)S(1)}) custom-call(s32[5]{0:T(128)S(1)} %get-tuple-element.27.info, bf16[2,400,128]{2,1,0:T(8,128)(2,1)S(1)} %collective-permute-done.2.remote, f32[2,192,256]{2,1,0:T(8,128)S(1)} %get-tuple-element.36.sums, ...), custom_call_target="tpu_custom_call" | custom-call | flops 792723456 | bytes 65536 | tf_op jit(solution)/shard_map/correct/pallas_call | solution.py:612
  20.2 3.6 %collective-permute-start.4 = (s16[272,128]{1,0:T(8,128)(2,1)S(1)}, s16[272,128]{1,0:T(8,128)(2,1)S(1)}, u32[]{:S(2)}, u32[]{:S(2)}) collective-permute-start(s16[272,128]{1,0:T(8,128)(2,1)S(1)} %get-tuple-element.42), channel_id=1, source_target_pairs={{0,24},{4,28},{8,16},{12,20},{16,8},{20,12},{24,0},{28,4},{1,25},{... | collective-permute-start | bytes 208904 | tf_op jit(solution)/shard_map/ppermute | solution.py:28
  23.8 0.8 %collective-permute-start.6 = (s16[272,128]{1,0:T(8,128)(2,1)S(1)}, s16[272,128]{1,0:T(8,128)(2,1)S(1)}, u32[]{:S(2)}, u32[]{:S(2)}) collective-permute-start(s16[272,128]{1,0:T(8,128)(2,1)S(1)} %get-tuple-element.44), channel_id=1, source_target_pairs={{0,8},{4,12},{8,0},{12,4},{16,24},{20,28},{24,16},{28,20},{1,9},{5... | collective-permute-start | bytes 208904 | tf_op jit(solution)/shard_map/ppermute | solution.py:28
  24.6 1.8 %collective-permute-done.4.rest_0_ = s16[272,128]{1,0:T(8,128)(2,1)S(1)} collective-permute-done((s16[272,128]{1,0:T(8,128)(2,1)S(1)}, s16[272,128]{1,0:T(8,128)(2,1)S(1)}, u32[]{:S(2)}, u32[]{:S(2)}) %collective-permute-start.4) | collective-permute-done | bytes 69664 | tf_op jit(solution)/shard_map/ppermute | solution.py:28
  26.5 3.9 %collective-permute-done.5.rest_1_ = s16[272,128]{1,0:T(8,128)(2,1)S(1)} collective-permute-done((s16[272,128]{1,0:T(8,128)(2,1)S(1)}, s16[272,128]{1,0:T(8,128)(2,1)S(1)}, u32[]{:S(2)}, u32[]{:S(2)}) %collective-permute-start.5) | collective-permute-done | bytes 69664 | tf_op jit(solution)/shard_map/ppermute | solution.py:28
  30.4 0.3 combine.1.rest_0_
  30.7 2.6 %collective-permute-start.9 = (s16[272,128]{1,0:T(8,128)(2,1)S(1)}, s16[272,128]{1,0:T(8,128)(2,1)S(1)}, u32[]{:S(2)}, u32[]{:S(2)}) collective-permute-start(s16[272,128]{1,0:T(8,128)(2,1)S(1)} %combine.1.rest_0_), channel_id=1, source_target_pairs={{0,24},{4,28},{8,16},{12,20},{16,8},{20,12},{24,0},{28,4},{1,25},{... | collective-permute-start | bytes 208904 | tf_op jit(solution)/shard_map/ppermute | solution.py:28
  33.3 0.4 collective-permute-start.8
  33.6 1.5 %collective-permute-start.7 = (s16[272,128]{1,0:T(8,128)(2,1)S(1)}, s16[272,128]{1,0:T(8,128)(2,1)S(1)}, u32[]{:S(2)}, u32[]{:S(2)}) collective-permute-start(s16[272,128]{1,0:T(8,128)(2,1)S(1)} %combine.1.rest_0_), channel_id=1, source_target_pairs={{0,8},{4,12},{8,0},{12,4},{16,24},{20,28},{24,16},{28,20},{1,9},{5... | collective-permute-start | bytes 208904 | tf_op jit(solution)/shard_map/ppermute | solution.py:28
  35.2 2.5 %collective-permute-done.9.rest_3_ = s16[272,128]{1,0:T(8,128)(2,1)S(1)} collective-permute-done((s16[272,128]{1,0:T(8,128)(2,1)S(1)}, s16[272,128]{1,0:T(8,128)(2,1)S(1)}, u32[]{:S(2)}, u32[]{:S(2)}) %collective-permute-start.9) | collective-permute-done | bytes 69664 | tf_op jit(solution)/shard_map/ppermute | solution.py:28
  37.6 2.8 %collective-permute-done.8.rest_2_ = s16[272,128]{1,0:T(8,128)(2,1)S(1)} collective-permute-done((s16[272,128]{1,0:T(8,128)(2,1)S(1)}, s16[272,128]{1,0:T(8,128)(2,1)S(1)}, u32[]{:S(2)}, u32[]{:S(2)}) %collective-permute-start.8) | collective-permute-done | bytes 69664 | tf_op jit(solution)/shard_map/ppermute | solution.py:28
  40.4 0.5 %collective-permute-start.11 = (s16[272,128]{1,0:T(8,128)(2,1)S(1)}, s16[272,128]{1,0:T(8,128)(2,1)S(1)}, u32[]{:S(2)}, u32[]{:S(2)}) collective-permute-start(s16[272,128]{1,0:T(8,128)(2,1)S(1)} %collective-permute-done.7.rest_1_), channel_id=1, source_target_pairs={{0,4},{4,0},{8,12},{12,8},{16,20},{20,16},{24,28},{28,24},{1,5},{5... | collective-permute-start | bytes 208904 | tf_op jit(solution)/shard_map/ppermute | solution.py:23
  40.9 0.7 %collective-permute-done.12.rest_6_ = s16[272,128]{1,0:T(8,128)(2,1)S(1)} collective-permute-done((s16[272,128]{1,0:T(8,128)(2,1)S(1)}, s16[272,128]{1,0:T(8,128)(2,1)S(1)}, u32[]{:S(2)}, u32[]{:S(2)}) %collective-permute-start.12) | collective-permute-done | bytes 69664 | tf_op jit(solution)/shard_map/ppermute | solution.py:23
  41.7 0.2 collective-permute-done.11.rest_5_
  41.8 1.6 %gather.1 = f32[16,128,128]{2,1,0:T(8,128)} custom-call(s32[3]{0:T(128)S(1)} %pad_add_fusion.ids, s16[272,128]{1,0:T(8,128)(2,1)S(1)} %combine.1.rest_0_, s16[272,128]{1,0:T(8,128)(2,1)S(1)} %collective-permute-done.7.rest_1_, s16[272,128]{1,0:T(8,128)(2,1)S(1)} %collective-permute-done.8.rest_2_, s16[272,128]{1,0:T(8,128)(2,1)S(1)} %collective-permute-done.9.rest_3_, ...), custom_call_target="tpu_custom_call" | custom-call | bytes 65536 | tf_op jit(solution)/shard_map/gather/pallas_call | solution.py:636
  (12 shorter events, 0.1 us)
Async XLA Ops:
  0.0 9.9 %collective-permute-start.1 = (bf16[16,128,128]{2,1,0:T(8,128)(2,1)}, bf16[16,128,128]{2,1,0:T(8,128)(2,1)S(1)}, u32[]{:S(2)}, u32[]{:S(2)}) collective-permute-start(bf16[16,128,128]{2,1,0:T(8,128)(2,1)} %bitcast.12), channel_id=1, source_target_pairs={{0,4},{4,0},{8,12},{12,8},{16,20},{20,16},{24,28},{28,24},{1,5},{5... | collective-permute-start | bytes 1572872 | tf_op jit(solution)/shard_map/ppermute | solution.py:23
  2.1 7.8 %collective-permute-start = (bf16[4,128,128]{2,1,0:T(8,128)(2,1)S(1)}, bf16[4,128,128]{2,1,0:T(8,128)(2,1)S(1)}, u32[]{:S(2)}, u32[]{:S(2)}) collective-permute-start(bf16[4,128,128]{2,1,0:T(8,128)(2,1)S(1)} %get-tuple-element.28), channel_id=1, source_target_pairs={{0,8},{4,1},{1,4},{5,2},{2,5},{6,3},{3,6},{7,15},{8,0},{12,9},{9,1... | collective-permute-start | bytes 393224 | tf_op jit(solution)/shard_map/ppermute | solution.py:43
  12.2 1.6 %collective-permute-start.3 = (bf16[2,4,96,128]{3,2,1,0:T(8,128)(2,1)S(1)}, bf16[2,4,96,128]{3,2,1,0:T(8,128)(2,1)S(1)}, u32[]{:S(2)}, u32[]{:S(2)}) collective-permute-start(bf16[2,4,96,128]{3,2,1,0:T(8,128)(2,1)S(1)} %get-tuple-element.35), channel_id=1, source_target_pairs={{0,4},{4,0},{8,12},{12,8},{16,20},{20,16},{24,28},{28,24},{1,5},{5... | collective-permute-start | bytes 589832 | tf_op jit(solution)/shard_map/ppermute | solution.py:23
  12.3 5.8 %collective-permute-start.2 = (bf16[2,400,128]{2,1,0:T(8,128)(2,1)S(1)}, bf16[2,400,128]{2,1,0:T(8,128)(2,1)S(1)}, u32[]{:S(2)}, u32[]{:S(2)}) collective-permute-start(bf16[2,400,128]{2,1,0:T(8,128)(2,1)S(1)} %get-tuple-element.33), channel_id=1, source_target_pairs={{0,8},{4,1},{1,4},{5,2},{2,5},{6,3},{3,6},{7,15},{8,0},{12,9},{9,1... | collective-permute-start | bytes 614408 | tf_op jit(solution)/shard_map/ppermute | solution.py:43
  20.2 6.3 %collective-permute-start.4 = (s16[272,128]{1,0:T(8,128)(2,1)S(1)}, s16[272,128]{1,0:T(8,128)(2,1)S(1)}, u32[]{:S(2)}, u32[]{:S(2)}) collective-permute-start(s16[272,128]{1,0:T(8,128)(2,1)S(1)} %get-tuple-element.42), channel_id=1, source_target_pairs={{0,24},{4,28},{8,16},{12,20},{16,8},{20,12},{24,0},{28,4},{1,25},{... | collective-permute-start | bytes 208904 | tf_op jit(solution)/shard_map/ppermute | solution.py:28
  23.8 6.6 %collective-permute-start.5 = (s16[272,128]{1,0:T(8,128)(2,1)S(1)}, s16[272,128]{1,0:T(8,128)(2,1)S(1)}, u32[]{:S(2)}, u32[]{:S(2)}) collective-permute-start(s16[272,128]{1,0:T(8,128)(2,1)S(1)} %get-tuple-element.43), channel_id=1, source_target_pairs={{0,16},{4,20},{8,24},{12,28},{16,0},{20,4},{24,8},{28,12},{1,17},{... | collective-permute-start | bytes 208904 | tf_op jit(solution)/shard_map/ppermute | solution.py:28
  23.8 6.6 %collective-permute-start.6 = (s16[272,128]{1,0:T(8,128)(2,1)S(1)}, s16[272,128]{1,0:T(8,128)(2,1)S(1)}, u32[]{:S(2)}, u32[]{:S(2)}) collective-permute-start(s16[272,128]{1,0:T(8,128)(2,1)S(1)} %get-tuple-element.44), channel_id=1, source_target_pairs={{0,8},{4,12},{8,0},{12,4},{16,24},{20,28},{24,16},{28,20},{1,9},{5... | collective-permute-start | bytes 208904 | tf_op jit(solution)/shard_map/ppermute | solution.py:28
  30.7 6.9 %collective-permute-start.9 = (s16[272,128]{1,0:T(8,128)(2,1)S(1)}, s16[272,128]{1,0:T(8,128)(2,1)S(1)}, u32[]{:S(2)}, u32[]{:S(2)}) collective-permute-start(s16[272,128]{1,0:T(8,128)(2,1)S(1)} %combine.1.rest_0_), channel_id=1, source_target_pairs={{0,24},{4,28},{8,16},{12,20},{16,8},{20,12},{24,0},{28,4},{1,25},{... | collective-permute-start | bytes 208904 | tf_op jit(solution)/shard_map/ppermute | solution.py:28
  33.3 7.1 %collective-permute-start.8 = (s16[272,128]{1,0:T(8,128)(2,1)S(1)}, s16[272,128]{1,0:T(8,128)(2,1)S(1)}, u32[]{:S(2)}, u32[]{:S(2)}) collective-permute-start(s16[272,128]{1,0:T(8,128)(2,1)S(1)} %combine.1.rest_0_), channel_id=1, source_target_pairs={{0,16},{4,20},{8,24},{12,28},{16,0},{20,4},{24,8},{28,12},{1,17},{... | collective-permute-start | bytes 208904 | tf_op jit(solution)/shard_map/ppermute | solution.py:28
  33.6 6.8 %collective-permute-start.7 = (s16[272,128]{1,0:T(8,128)(2,1)S(1)}, s16[272,128]{1,0:T(8,128)(2,1)S(1)}, u32[]{:S(2)}, u32[]{:S(2)}) collective-permute-start(s16[272,128]{1,0:T(8,128)(2,1)S(1)} %combine.1.rest_0_), channel_id=1, source_target_pairs={{0,8},{4,12},{8,0},{12,4},{16,24},{20,28},{24,16},{28,20},{1,9},{5... | collective-permute-start | bytes 208904 | tf_op jit(solution)/shard_map/ppermute | solution.py:28
  35.1 5.8 %collective-permute-start.10 = (s16[272,128]{1,0:T(8,128)(2,1)S(1)}, s16[272,128]{1,0:T(8,128)(2,1)S(1)}, u32[]{:S(2)}, u32[]{:S(2)}) collective-permute-start(s16[272,128]{1,0:T(8,128)(2,1)S(1)} %combine.1.rest_0_), channel_id=1, source_target_pairs={{0,4},{4,0},{8,12},{12,8},{16,20},{20,16},{24,28},{28,24},{1,5},{5... | collective-permute-start | bytes 208904 | tf_op jit(solution)/shard_map/ppermute | solution.py:23
  37.6 3.3 %collective-permute-start.13 = (s16[272,128]{1,0:T(8,128)(2,1)S(1)}, s16[272,128]{1,0:T(8,128)(2,1)S(1)}, u32[]{:S(2)}, u32[]{:S(2)}) collective-permute-start(s16[272,128]{1,0:T(8,128)(2,1)S(1)} %collective-permute-done.9.rest_3_), channel_id=1, source_target_pairs={{0,4},{4,0},{8,12},{12,8},{16,20},{20,16},{24,28},{28,24},{1,5},{5... | collective-permute-start | bytes 208904 | tf_op jit(solution)/shard_map/ppermute | solution.py:23
  40.4 1.3 %collective-permute-start.12 = (s16[272,128]{1,0:T(8,128)(2,1)S(1)}, s16[272,128]{1,0:T(8,128)(2,1)S(1)}, u32[]{:S(2)}, u32[]{:S(2)}) collective-permute-start(s16[272,128]{1,0:T(8,128)(2,1)S(1)} %collective-permute-done.8.rest_2_), channel_id=1, source_target_pairs={{0,4},{4,0},{8,12},{12,8},{16,20},{20,16},{24,28},{28,24},{1,5},{5... | collective-permute-start | bytes 208904 | tf_op jit(solution)/shard_map/ppermute | solution.py:23
  40.4 1.4 %collective-permute-start.11 = (s16[272,128]{1,0:T(8,128)(2,1)S(1)}, s16[272,128]{1,0:T(8,128)(2,1)S(1)}, u32[]{:S(2)}, u32[]{:S(2)}) collective-permute-start(s16[272,128]{1,0:T(8,128)(2,1)S(1)} %collective-permute-done.7.rest_1_), channel_id=1, source_target_pairs={{0,4},{4,0},{8,12},{12,8},{16,20},{20,16},{24,28},{28,24},{1,5},{5... | collective-permute-start | bytes 208904 | tf_op jit(solution)/shard_map/ppermute | solution.py:23

commit v10 on v9

--- a/solution.py
+++ b/solution.py
@@ -475,13 +475,15 @@
     for place, piece in enumerate(pieces):
         side = core if place < count else 1 - core
         marks = code_marks(piece)
+        first = canonical(side, (chip ^ (place % count)) * rows, slab_x - rows)
         for r in range(rows):
-            at = canonical(side, (chip ^ (place % count)) * rows + r, slab_x - 1)
-            slot = place * rows + r
+            slot = place * rows + canonical(side, r, rows - 1)
             cells[slot] = jnp.exp(decode(piece, marks, HEADER + r * width, width))
-            store = pltpu.make_async_copy(cells.at[slot], out.at[at], sems.at[slot])
-            store.start()
-            stores.append(store)
+        store = pltpu.make_async_copy(
+            cells.at[pl.ds(place * rows, rows)], out.at[pl.ds(first, rows)], sems.at[place]
+        )
+        store.start()
+        stores.append(store)
     for store in stores:
         store.wait()
 

time: 43.6 us -> 43.6 us (level)
  transfers between devices with their start and end apart: 14 -> 14, of which waited for: 7 -> 6; matrix products, arithmetic and copies ran while one was open for 0% -> 0% of each run, Pallas kernels for 25% -> 25%
where the time goes in v10:
time: 43.6 us; the launch traced here: 43.5 us
  Pallas kernels  17.1 us (39%)
  starting transfers between devices  14.2 us (33%)
  waiting for transfers between devices  12 us (28%)
    ppermute x6, waiting for transfers between devices, swap_chips(): lax.ppermute(cells, 'view', [(i, i ^ 2 * step) for i in range(count)])  11.1 us
    ppermute x6, starting transfers between devices, swap_chips(): lax.ppermute(cells, 'view', [(i, i ^ 2 * step) for i in range(count)])  8.91 us
    pallas_call x1, Pallas kernels, local(): call(functools.partial(tables_kernel, taps=taps, blocks=blocks), 'tables'...  5.08 us
    ppermute x2, starting transfers between devices, swap_layers(): return lax.ppermute(cells, ('view', 'blk'), route)  4.28 us
    pallas_call x1, Pallas kernels, local(): call(functools.partial(inner_kernel, taps=taps, blocks=blocks), 'inner',...  4.14 us
    pallas_call x1, Pallas kernels, local(): call(functools.partial(blur_kernel, taps=taps, blocks=blocks), 'blur', (p...  2.25 us
    pallas_call x1, Pallas kernels, local(): call(functools.partial(correct_kernel, taps=taps, blocks=blocks), 'correc...  2.06 us
    pallas_call x1, Pallas kernels, local(): call(gather_kernel, 'gather', shape(estimate.shape, f32), 's' + 'v' * (2...  1.67 us
  transfers between devices with their start and end apart: 14, of which 6 were waited for; matrix products, arithmetic and copies ran while one was open for 0% of the time, Pallas kernels for 25%

profile of v10, /device:TPU:0, one launch (start us, length us, event | category | flops | bytes accessed | tf_op | source)
XLA Modules:
  0.0 43.5 jit_solution(9689145390398310097)
XLA Ops:
  0.0 0.5 %collective-permute-start.1 = (bf16[16,128,128]{2,1,0:T(8,128)(2,1)}, bf16[16,128,128]{2,1,0:T(8,128)(2,1)S(1)}, u32[]{:S(2)}, u32[]{:S(2)}) collective-permute-start(bf16[16,128,128]{2,1,0:T(8,128)(2,1)} %bitcast.12), channel_id=1, source_target_pairs={{0,4},{4,0},{8,12},{12,8},{16,20},{20,16},{24,28},{28,24},{1,5},{5... | collective-permute-start | bytes 1572872 | tf_op jit(solution)/shard_map/ppermute | solution.py:23
  0.5 0.1 pad_add_fusion.ids
  0.5 1.6 %payload.1 = (bf16[4,128,128]{2,1,0:T(8,128)(2,1)S(1)}, s32[4,8]{1,0:T(4,128)S(1)}, f32[504,25]{1,0:T(8,128)S(1)}) custom-call(s32[3]{0:T(128)S(1)} %pad_add_fusion.ids, s32[4,8]{1,0:T(4,128)} %bitcast.11, f32[504,25]{1,0:T(8,128)} %bitcast.10, f32[16,128,128]{2,1,0:T(8,128)} %est.3), custom_call_target="tpu_custom_call" | custom-call | bytes 65536 | tf_op jit(solution)/shard_map/payload/pallas_call | solution.py:542
  2.1 2.6 %collective-permute-start = (bf16[4,128,128]{2,1,0:T(8,128)(2,1)S(1)}, bf16[4,128,128]{2,1,0:T(8,128)(2,1)S(1)}, u32[]{:S(2)}, u32[]{:S(2)}) collective-permute-start(bf16[4,128,128]{2,1,0:T(8,128)(2,1)S(1)} %get-tuple-element.28), channel_id=1, source_target_pairs={{0,8},{4,1},{1,4},{5,2},{2,5},{6,3},{3,6},{7,15},{8,0},{12,9},{9,1... | collective-permute-start | bytes 393224 | tf_op jit(solution)/shard_map/ppermute | solution.py:43
  4.8 5.1 %tables.1 = (bf16[2,9,896,128]{3,2,1,0:T(8,128)(2,1)S(1)}, bf16[12,128,896]{2,1,0:T(8,128)(2,1)S(1)}, s32[5]{0:T(128)S(1)}, bf16[16,128,128]{2,1,0:T(8,128)(2,1)...) custom-call(s32[3]{0:T(128)S(1)} %pad_add_fusion.ids, s32[4,8]{1,0:T(4,128)S(1)} %get-tuple-element.25.cov, ...), custom_call_target="tpu_custom_call" | custom-call | flops 1585446912 | bytes 65536 | tf_op jit(solution)/shard_map/tables/pallas_call | solution.py:555
  9.9 2.3 %blur.1 = (bf16[2,8,96,128]{3,2,1,0:T(8,128)(2,1)S(1)}, bf16[2,400,128]{2,1,0:T(8,128)(2,1)S(1)}, bf16[2,4,96,128]{3,2,1,0:T(8,128)(2,1)S(1)}) custom-call(s32[5]{0:T(128)S(1)} %get-tuple-element.27.info, bf16[4,128,128]{2,1,0:T(8,128)(2,1)S(1)} %collective-permute-done.halo, bf16[16,128,128]{2,1,0:T(8,128)(2,1)S(1)} %get-tuple-element.29.img_own, ...), custom_call_target="tpu_custom_call" | custom-call | flops 3170893824 | bytes 65536 | tf_op jit(solution)/shard_map/blur/pallas_call | solution.py:576
  12.1 0.1 collective-permute-start.3
  12.2 1.6 %collective-permute-start.2 = (bf16[2,400,128]{2,1,0:T(8,128)(2,1)S(1)}, bf16[2,400,128]{2,1,0:T(8,128)(2,1)S(1)}, u32[]{:S(2)}, u32[]{:S(2)}) collective-permute-start(bf16[2,400,128]{2,1,0:T(8,128)(2,1)S(1)} %get-tuple-element.33), channel_id=1, source_target_pairs={{0,8},{4,1},{1,4},{5,2},{2,5},{6,3},{3,6},{7,15},{8,0},{12,9},{9,1... | collective-permute-start | bytes 614408 | tf_op jit(solution)/shard_map/ppermute | solution.py:43
  13.9 4.1 %inner.1 = (f32[2,192,256]{2,1,0:T(8,128)S(1)}, f32[4,128,128]{2,1,0:T(8,128)S(1)}, f32[4,128,128]{2,1,0:T(8,128)S(1)}, f32[2,128,128]{2,1,0:T(8,128)S(1)}) custom-call(s32[5]{0:T(128)S(1)} %get-tuple-element.27.info, bf16[2,8,96,128]{3,2,1,0:T(8,128)(2,1)S(1)} %get-tuple-element.34.quot, bf16[2,4,96,128]{3,2,1,0:T(8,128)(2,1)S(1)} %collective-permute-done.3.near, ...), custom_call_target="tpu_custom_call" | custom-call | flops 3170893824 | bytes 65536 | tf_op jit(solution)/shard_map/inner/pallas_call | solution.py:596
  18.0 2.1 %correct.1 = (f32[2,128,128]{2,1,0:T(8,128)S(1)}, s16[272,128]{1,0:T(8,128)(2,1)S(1)}, s16[272,128]{1,0:T(8,128)(2,1)S(1)}, s16[272,128]{1,0:T(8,128)(2,1)S(1)}) custom-call(s32[5]{0:T(128)S(1)} %get-tuple-element.27.info, bf16[2,400,128]{2,1,0:T(8,128)(2,1)S(1)} %collective-permute-done.2.remote, f32[2,192,256]{2,1,0:T(8,128)S(1)} %get-tuple-element.36.sums, ...), custom_call_target="tpu_custom_call" | custom-call | flops 792723456 | bytes 65536 | tf_op jit(solution)/shard_map/correct/pallas_call | solution.py:614
  20.1 3.7 %collective-permute-start.4 = (s16[272,128]{1,0:T(8,128)(2,1)S(1)}, s16[272,128]{1,0:T(8,128)(2,1)S(1)}, u32[]{:S(2)}, u32[]{:S(2)}) collective-permute-start(s16[272,128]{1,0:T(8,128)(2,1)S(1)} %get-tuple-element.42), channel_id=1, source_target_pairs={{0,24},{4,28},{8,16},{12,20},{16,8},{20,12},{24,0},{28,4},{1,25},{... | collective-permute-start | bytes 208904 | tf_op jit(solution)/shard_map/ppermute | solution.py:28
  23.8 0.8 %collective-permute-start.6 = (s16[272,128]{1,0:T(8,128)(2,1)S(1)}, s16[272,128]{1,0:T(8,128)(2,1)S(1)}, u32[]{:S(2)}, u32[]{:S(2)}) collective-permute-start(s16[272,128]{1,0:T(8,128)(2,1)S(1)} %get-tuple-element.44), channel_id=1, source_target_pairs={{0,8},{4,12},{8,0},{12,4},{16,24},{20,28},{24,16},{28,20},{1,9},{5... | collective-permute-start | bytes 208904 | tf_op jit(solution)/shard_map/ppermute | solution.py:28
  24.6 1.8 %collective-permute-done.4.rest_0_ = s16[272,128]{1,0:T(8,128)(2,1)S(1)} collective-permute-done((s16[272,128]{1,0:T(8,128)(2,1)S(1)}, s16[272,128]{1,0:T(8,128)(2,1)S(1)}, u32[]{:S(2)}, u32[]{:S(2)}) %collective-permute-start.4) | collective-permute-done | bytes 69664 | tf_op jit(solution)/shard_map/ppermute | solution.py:28
  26.4 3.9 %collective-permute-done.5.rest_1_ = s16[272,128]{1,0:T(8,128)(2,1)S(1)} collective-permute-done((s16[272,128]{1,0:T(8,128)(2,1)S(1)}, s16[272,128]{1,0:T(8,128)(2,1)S(1)}, u32[]{:S(2)}, u32[]{:S(2)}) %collective-permute-start.5) | collective-permute-done | bytes 69664 | tf_op jit(solution)/shard_map/ppermute | solution.py:28
  30.3 0.3 combine.1.rest_0_
  30.6 2.7 %collective-permute-start.9 = (s16[272,128]{1,0:T(8,128)(2,1)S(1)}, s16[272,128]{1,0:T(8,128)(2,1)S(1)}, u32[]{:S(2)}, u32[]{:S(2)}) collective-permute-start(s16[272,128]{1,0:T(8,128)(2,1)S(1)} %combine.1.rest_0_), channel_id=1, source_target_pairs={{0,24},{4,28},{8,16},{12,20},{16,8},{20,12},{24,0},{28,4},{1,25},{... | collective-permute-start | bytes 208904 | tf_op jit(solution)/shard_map/ppermute | solution.py:28
  33.2 0.4 collective-permute-start.8
  33.6 1.4 %collective-permute-start.7 = (s16[272,128]{1,0:T(8,128)(2,1)S(1)}, s16[272,128]{1,0:T(8,128)(2,1)S(1)}, u32[]{:S(2)}, u32[]{:S(2)}) collective-permute-start(s16[272,128]{1,0:T(8,128)(2,1)S(1)} %combine.1.rest_0_), channel_id=1, source_target_pairs={{0,8},{4,12},{8,0},{12,4},{16,24},{20,28},{24,16},{28,20},{1,9},{5... | collective-permute-start | bytes 208904 | tf_op jit(solution)/shard_map/ppermute | solution.py:28
  35.0 2.5 %collective-permute-done.9.rest_3_ = s16[272,128]{1,0:T(8,128)(2,1)S(1)} collective-permute-done((s16[272,128]{1,0:T(8,128)(2,1)S(1)}, s16[272,128]{1,0:T(8,128)(2,1)S(1)}, u32[]{:S(2)}, u32[]{:S(2)}) %collective-permute-start.9) | collective-permute-done | bytes 69664 | tf_op jit(solution)/shard_map/ppermute | solution.py:28
  37.5 2.9 %collective-permute-done.8.rest_2_ = s16[272,128]{1,0:T(8,128)(2,1)S(1)} collective-permute-done((s16[272,128]{1,0:T(8,128)(2,1)S(1)}, s16[272,128]{1,0:T(8,128)(2,1)S(1)}, u32[]{:S(2)}, u32[]{:S(2)}) %collective-permute-start.8) | collective-permute-done | bytes 69664 | tf_op jit(solution)/shard_map/ppermute | solution.py:28
  40.4 0.5 %collective-permute-start.11 = (s16[272,128]{1,0:T(8,128)(2,1)S(1)}, s16[272,128]{1,0:T(8,128)(2,1)S(1)}, u32[]{:S(2)}, u32[]{:S(2)}) collective-permute-start(s16[272,128]{1,0:T(8,128)(2,1)S(1)} %collective-permute-done.7.rest_1_), channel_id=1, source_target_pairs={{0,4},{4,0},{8,12},{12,8},{16,20},{20,16},{24,28},{28,24},{1,5},{5... | collective-permute-start | bytes 208904 | tf_op jit(solution)/shard_map/ppermute | solution.py:23
  40.9 0.7 %collective-permute-done.12.rest_6_ = s16[272,128]{1,0:T(8,128)(2,1)S(1)} collective-permute-done((s16[272,128]{1,0:T(8,128)(2,1)S(1)}, s16[272,128]{1,0:T(8,128)(2,1)S(1)}, u32[]{:S(2)}, u32[]{:S(2)}) %collective-permute-start.12) | collective-permute-done | bytes 69664 | tf_op jit(solution)/shard_map/ppermute | solution.py:23
  41.7 0.2 collective-permute-done.11.rest_5_
  41.8 1.7 %gather.1 = f32[16,128,128]{2,1,0:T(8,128)} custom-call(s32[3]{0:T(128)S(1)} %pad_add_fusion.ids, s16[272,128]{1,0:T(8,128)(2,1)S(1)} %combine.1.rest_0_, s16[272,128]{1,0:T(8,128)(2,1)S(1)} %collective-permute-done.7.rest_1_, s16[272,128]{1,0:T(8,128)(2,1)S(1)} %collective-permute-done.8.rest_2_, s16[272,128]{1,0:T(8,128)(2,1)S(1)} %collective-permute-done.9.rest_3_, ...), custom_call_target="tpu_custom_call" | custom-call | bytes 65536 | tf_op jit(solution)/shard_map/gather/pallas_call | solution.py:638
  (12 shorter events, 0.1 us)
Async XLA Ops:
  0.0 9.9 %collective-permute-start.1 = (bf16[16,128,128]{2,1,0:T(8,128)(2,1)}, bf16[16,128,128]{2,1,0:T(8,128)(2,1)S(1)}, u32[]{:S(2)}, u32[]{:S(2)}) collective-permute-start(bf16[16,128,128]{2,1,0:T(8,128)(2,1)} %bitcast.12), channel_id=1, source_target_pairs={{0,4},{4,0},{8,12},{12,8},{16,20},{20,16},{24,28},{28,24},{1,5},{5... | collective-permute-start | bytes 1572872 | tf_op jit(solution)/shard_map/ppermute | solution.py:23
  2.1 7.7 %collective-permute-start = (bf16[4,128,128]{2,1,0:T(8,128)(2,1)S(1)}, bf16[4,128,128]{2,1,0:T(8,128)(2,1)S(1)}, u32[]{:S(2)}, u32[]{:S(2)}) collective-permute-start(bf16[4,128,128]{2,1,0:T(8,128)(2,1)S(1)} %get-tuple-element.28), channel_id=1, source_target_pairs={{0,8},{4,1},{1,4},{5,2},{2,5},{6,3},{3,6},{7,15},{8,0},{12,9},{9,1... | collective-permute-start | bytes 393224 | tf_op jit(solution)/shard_map/ppermute | solution.py:43
  12.1 1.7 %collective-permute-start.3 = (bf16[2,4,96,128]{3,2,1,0:T(8,128)(2,1)S(1)}, bf16[2,4,96,128]{3,2,1,0:T(8,128)(2,1)S(1)}, u32[]{:S(2)}, u32[]{:S(2)}) collective-permute-start(bf16[2,4,96,128]{3,2,1,0:T(8,128)(2,1)S(1)} %get-tuple-element.35), channel_id=1, source_target_pairs={{0,4},{4,0},{8,12},{12,8},{16,20},{20,16},{24,28},{28,24},{1,5},{5... | collective-permute-start | bytes 589832 | tf_op jit(solution)/shard_map/ppermute | solution.py:23
  12.2 5.8 %collective-permute-start.2 = (bf16[2,400,128]{2,1,0:T(8,128)(2,1)S(1)}, bf16[2,400,128]{2,1,0:T(8,128)(2,1)S(1)}, u32[]{:S(2)}, u32[]{:S(2)}) collective-permute-start(bf16[2,400,128]{2,1,0:T(8,128)(2,1)S(1)} %get-tuple-element.33), channel_id=1, source_target_pairs={{0,8},{4,1},{1,4},{5,2},{2,5},{6,3},{3,6},{7,15},{8,0},{12,9},{9,1... | collective-permute-start | bytes 614408 | tf_op jit(solution)/shard_map/ppermute | solution.py:43
  20.1 6.3 %collective-permute-start.4 = (s16[272,128]{1,0:T(8,128)(2,1)S(1)}, s16[272,128]{1,0:T(8,128)(2,1)S(1)}, u32[]{:S(2)}, u32[]{:S(2)}) collective-permute-start(s16[272,128]{1,0:T(8,128)(2,1)S(1)} %get-tuple-element.42), channel_id=1, source_target_pairs={{0,24},{4,28},{8,16},{12,20},{16,8},{20,12},{24,0},{28,4},{1,25},{... | collective-permute-start | bytes 208904 | tf_op jit(solution)/shard_map/ppermute | solution.py:28
  23.8 6.5 %collective-permute-start.5 = (s16[272,128]{1,0:T(8,128)(2,1)S(1)}, s16[272,128]{1,0:T(8,128)(2,1)S(1)}, u32[]{:S(2)}, u32[]{:S(2)}) collective-permute-start(s16[272,128]{1,0:T(8,128)(2,1)S(1)} %get-tuple-element.43), channel_id=1, source_target_pairs={{0,16},{4,20},{8,24},{12,28},{16,0},{20,4},{24,8},{28,12},{1,17},{... | collective-permute-start | bytes 208904 | tf_op jit(solution)/shard_map/ppermute | solution.py:28
  23.8 6.5 %collective-permute-start.6 = (s16[272,128]{1,0:T(8,128)(2,1)S(1)}, s16[272,128]{1,0:T(8,128)(2,1)S(1)}, u32[]{:S(2)}, u32[]{:S(2)}) collective-permute-start(s16[272,128]{1,0:T(8,128)(2,1)S(1)} %get-tuple-element.44), channel_id=1, source_target_pairs={{0,8},{4,12},{8,0},{12,4},{16,24},{20,28},{24,16},{28,20},{1,9},{5... | collective-permute-start | bytes 208904 | tf_op jit(solution)/shard_map/ppermute | solution.py:28
  30.6 7.0 %collective-permute-start.9 = (s16[272,128]{1,0:T(8,128)(2,1)S(1)}, s16[272,128]{1,0:T(8,128)(2,1)S(1)}, u32[]{:S(2)}, u32[]{:S(2)}) collective-permute-start(s16[272,128]{1,0:T(8,128)(2,1)S(1)} %combine.1.rest_0_), channel_id=1, source_target_pairs={{0,24},{4,28},{8,16},{12,20},{16,8},{20,12},{24,0},{28,4},{1,25},{... | collective-permute-start | bytes 208904 | tf_op jit(solution)/shard_map/ppermute | solution.py:28
  33.2 7.2 %collective-permute-start.8 = (s16[272,128]{1,0:T(8,128)(2,1)S(1)}, s16[272,128]{1,0:T(8,128)(2,1)S(1)}, u32[]{:S(2)}, u32[]{:S(2)}) collective-permute-start(s16[272,128]{1,0:T(8,128)(2,1)S(1)} %combine.1.rest_0_), channel_id=1, source_target_pairs={{0,16},{4,20},{8,24},{12,28},{16,0},{20,4},{24,8},{28,12},{1,17},{... | collective-permute-start | bytes 208904 | tf_op jit(solution)/shard_map/ppermute | solution.py:28
  33.6 6.8 %collective-permute-start.7 = (s16[272,128]{1,0:T(8,128)(2,1)S(1)}, s16[272,128]{1,0:T(8,128)(2,1)S(1)}, u32[]{:S(2)}, u32[]{:S(2)}) collective-permute-start(s16[272,128]{1,0:T(8,128)(2,1)S(1)} %combine.1.rest_0_), channel_id=1, source_target_pairs={{0,8},{4,12},{8,0},{12,4},{16,24},{20,28},{24,16},{28,20},{1,9},{5... | collective-permute-start | bytes 208904 | tf_op jit(solution)/shard_map/ppermute | solution.py:28
  35.0 5.9 %collective-permute-start.10 = (s16[272,128]{1,0:T(8,128)(2,1)S(1)}, s16[272,128]{1,0:T(8,128)(2,1)S(1)}, u32[]{:S(2)}, u32[]{:S(2)}) collective-permute-start(s16[272,128]{1,0:T(8,128)(2,1)S(1)} %combine.1.rest_0_), channel_id=1, source_target_pairs={{0,4},{4,0},{8,12},{12,8},{16,20},{20,16},{24,28},{28,24},{1,5},{5... | collective-permute-start | bytes 208904 | tf_op jit(solution)/shard_map/ppermute | solution.py:23
  37.5 3.4 %collective-permute-start.13 = (s16[272,128]{1,0:T(8,128)(2,1)S(1)}, s16[272,128]{1,0:T(8,128)(2,1)S(1)}, u32[]{:S(2)}, u32[]{:S(2)}) collective-permute-start(s16[272,128]{1,0:T(8,128)(2,1)S(1)} %collective-permute-done.9.rest_3_), channel_id=1, source_target_pairs={{0,4},{4,0},{8,12},{12,8},{16,20},{20,16},{24,28},{28,24},{1,5},{5... | collective-permute-start | bytes 208904 | tf_op jit(solution)/shard_map/ppermute | solution.py:23
  40.4 1.3 %collective-permute-start.12 = (s16[272,128]{1,0:T(8,128)(2,1)S(1)}, s16[272,128]{1,0:T(8,128)(2,1)S(1)}, u32[]{:S(2)}, u32[]{:S(2)}) collective-permute-start(s16[272,128]{1,0:T(8,128)(2,1)S(1)} %collective-permute-done.8.rest_2_), channel_id=1, source_target_pairs={{0,4},{4,0},{8,12},{12,8},{16,20},{20,16},{24,28},{28,24},{1,5},{5... | collective-permute-start | bytes 208904 | tf_op jit(solution)/shard_map/ppermute | solution.py:23
  40.4 1.4 %collective-permute-start.11 = (s16[272,128]{1,0:T(8,128)(2,1)S(1)}, s16[272,128]{1,0:T(8,128)(2,1)S(1)}, u32[]{:S(2)}, u32[]{:S(2)}) collective-permute-start(s16[272,128]{1,0:T(8,128)(2,1)S(1)} %collective-permute-done.7.rest_1_), channel_id=1, source_target_pairs={{0,4},{4,0},{8,12},{12,8},{16,20},{20,16},{24,28},{28,24},{1,5},{5... | collective-permute-start | bytes 208904 | tf_op jit(solution)/shard_map/ppermute | solution.py:23
